TPU v7x, 256 devices: a whole 4x4x8 slice. The times are simulated.
256 devices in a mesh: batch: 16 (over x, y), layer: 16 (over z, core).
Axes of the slice: x: 4, y: 4, z: 8, core: 2. Of those that a mesh axis runs over, the one named last changes fastest.
Arguments:
- inputs: float32 [256, 4096], P(None, 'batch'), parts along dimension 1, may hold values from -6 to 6
- guess: float32 [16, 256, 4096], P('layer', None, 'batch'), parts along dimension 2, may hold values from -6 to 6
- weights: bfloat16 [64, 256, 2304], P('layer'), may hold values from -0.125 to 0.125
Outputs:
- states: float32 [64, 256, 4096], P('layer', None, 'batch'), parts along dimension 2
There are 16 independent parts, one for each index of `batch`. A program takes and returns all parts, laid end to end along the dimension named above; an argument that names none is the same for every part. Nothing has to cross between parts.
All inputs are finite; a program needn't handle non-finite values.
Results may differ from a plain program's by a relative error of at most 0.01.
Values may be sent and summed in bfloat16 or wider, within the bound.
No kernel may reach another device: no remote copies, remote signals or barrier semaphores. Data moves between devices by JAX's collectives and lax.ppermute only.
A program may use at most 64 MiB of HBM per device.

v0:
```python
import functools

import jax
import jax.numpy as jnp
from jax import lax
from jax.experimental import pallas as pl
from jax.experimental.pallas import tpu as pltpu
from jax.sharding import PartitionSpec as P

SIDE = 16
CELLS = 256
CHANS = 256
TAPS = 9 * CHANS
COARSEN = 4
DEVICES = 16
F32 = jnp.float32
BF16 = jnp.bfloat16
STATE = (CELLS, CHANS)
VMEM_LIMIT = 12 << 20


def conv_tanh(state, weight):
    column = lax.broadcasted_iota(jnp.int32, STATE, 0) % SIDE
    before = jnp.where(column == 0, 0.0, pltpu.roll(state, 1, 0)).astype(BF16)
    after = jnp.where(column == SIDE - 1, 0.0, pltpu.roll(state, CELLS - 1, 0)).astype(BF16)
    trio = [before, state.astype(BF16), after]
    edge = jnp.zeros((SIDE, CHANS), BF16)
    above = [jnp.concatenate([edge, x[:-SIDE]], 0) for x in trio]
    below = [jnp.concatenate([x[SIDE:], edge], 0) for x in trio]
    total = None
    for tap, piece in enumerate(above + trio + below):
        part = lax.dot_general(
            piece,
            weight[:, tap * CHANS : (tap + 1) * CHANS],
            (((1,), (1,)), ((), ())),
            preferred_element_type=F32,
        )
        total = part if total is None else total + part
    return jnp.tanh(total)


def vmem(shape, dtype):
    return pltpu.VMEM(shape, dtype)


def kernel_call(body, outs, args, name, steps, hbm=(), scratch=(), aliases=None):
    def space(i):
        return pltpu.HBM if i in hbm else pltpu.VMEM

    args = [pltpu.with_memory_space_constraint(a, space(i)) for i, a in enumerate(args)]
    return pl.pallas_call(
        body,
        out_shape=outs,
        in_specs=[pl.BlockSpec(memory_space=space(i)) for i in range(len(args))],
        out_specs=[
            pl.BlockSpec(memory_space=pltpu.VMEM if hasattr(o, "memory_space") else pl.ANY)
            for o in outs
        ],
        scratch_shapes=list(scratch),
        input_output_aliases=aliases or {},
        compiler_params=pltpu.CompilerParams(vmem_limit_bytes=VMEM_LIMIT),
        cost_estimate=pl.CostEstimate(
            flops=steps * 2 * TAPS * CELLS * CHANS, bytes_accessed=1 << 20, transcendentals=0
        ),
        name=name,
    )(*args)


def place():
    return lax.axis_index("layer")


def first_sweep(parity, *refs):
    inputs, guess, weights = refs[:3]
    cpoint, own_w, later_w, start, raw, sems = refs[-6:]
    me = place()

    @pl.when(me % 2 == parity)
    def _():
        source = [pltpu.make_async_copy(weights.at[0], own_w, sems.at[1])]
        for i in range(COARSEN - 1):
            source.append(pltpu.make_async_copy(weights.at[i + 1], later_w.at[i], sems.at[i + 2]))
        begin = pltpu.make_async_copy(inputs, raw, sems.at[0])
        other = pltpu.make_async_copy(guess.at[0], raw, sems.at[0])

        @pl.when(me == 0)
        def _():
            begin.start()

        @pl.when(me > 0)
        def _():
            other.start()

        for copy in source:
            copy.start()
        other.wait()
        state = raw[...].T

        @pl.when(me == 0)
        def _():
            start[...] = state

        for i in range(COARSEN):
            source[i].wait()
            state = state + 0.25 * conv_tanh(state, own_w if i == 0 else later_w[i - 1])
        cpoint[...] = state.astype(BF16)

        @pl.when(me == 1)
        def _():
            begin.start()
            begin.wait()
            start[...] = raw[...].T


def sweep(state, own_w, later_w, rhs):
    terms = []
    for i in range(COARSEN):
        terms.append(conv_tanh(state, own_w if i == 0 else later_w[i - 1]))
        state = state + 0.25 * terms[-1]
    rhs[...] = 0.25 * (terms[0] + terms[1] + terms[2] + terms[3]) - terms[0]
    return state


def second_sweep_lead(left_odd, own_w, later_w, _, rhs, solved, out):
    @pl.when(place() == 1)
    def _():
        out[...] = sweep(left_odd[...].astype(F32), own_w, later_w, rhs).astype(BF16)


def second_sweep(left_odd, left_even, own_w, later_w, start, _, rhs, first):
    me = place()

    @pl.when(me != 1)
    def _():
        left = jnp.where(me % 2 == 0, left_even[...], left_odd[...]).astype(F32)
        first[...] = sweep(jnp.where(me == 0, start[...], left), own_w, later_w, rhs)


def in_order(*refs):
    pass


def either(me, owners):
    chosen = me == owners[0]
    for owner in owners[1:]:
        chosen |= me == owner
    return chosen


def two_steps(owners, keep, even_rhs, rhs, even_w, own_w, got, _, out, solved):
    @pl.when(either(place(), owners))
    def _():
        value = got[...].astype(F32)
        value = value + conv_tanh(value, even_w) + even_rhs[...]
        value = value + conv_tanh(value, own_w) + rhs[...]
        if keep:
            solved[...] = value
        out[...] = value.astype(BF16)


def one_step(owners, first, rhs, own_w, _, out, solved):
    @pl.when(either(place(), owners))
    def _():
        value = first[...]
        out[...] = (value + conv_tanh(value, own_w) + rhs[...]).astype(BF16)


def coarse_step(got, own_w):
    value = got[...].astype(F32)
    return value + 4.0 * conv_tanh(value, own_w)


def coarse_base(owners, upper, own_w, _, out, solved):
    @pl.when(either(place(), owners))
    def _():
        out[...] = coarse_step(upper, own_w)


def lead_step(got, base, own_w, early3, early4, mine, _, out, solved):
    me = place()

    @pl.when(me == 11)
    def _():
        value = coarse_step(got, own_w) + (solved[...] - base[...])
        solved[...] = value
        out[...] = value.astype(BF16)

    for owner, source in ((3, early3), (5, early4), (7, mine)):

        @pl.when(me == owner)
        def _():
            out[...] = source[...]


def lead_two_steps(got, mine, early5, even_rhs, rhs, even_w, own_w, _, out, solved):
    two_steps((9, 13), False, even_rhs, rhs, even_w, own_w, got, _, out, solved)
    for owner, source in ((11, mine), (7, early5)):

        @pl.when(place() == owner)
        def _():
            out[...] = source[...]


def end_step(got, base, own_w, _, solved):
    @pl.when(place() == 15)
    def _():
        solved[...] = coarse_step(got, own_w) + (solved[...] - base[...])


def last_sweep(
    start, got8b, got8, got3, got4, got5, got7, got7b,
    even_rhs, rhs, even_w, own_w, later_w, solved, states, left, ready, sems,
):
    me = place()
    sources = (
        (start, (0, 1)),
        (got7b, (2, 4, 8)),
        (got8b, (6, 10, 12, 14)),
        (got3, (3,)),
        (got4, (5,)),
        (got5, (7,)),
        (got7, (9, 13)),
        (got8, (11, 15)),
    )
    for source, owners in sources:

        @pl.when(either(me, owners))
        def _():
            left[...] = source[...].astype(F32)

    @pl.when(me % 2 == 1)
    def _():
        value = left[...]
        left[...] = value + conv_tanh(value, even_w) + even_rhs[...]

    def store(i, value):
        ready[i] = value.T
        copy = pltpu.make_async_copy(ready.at[i], states.at[i], sems.at[i])
        copy.start()
        return copy

    state = left[...]
    term = conv_tanh(state, own_w)
    end = jnp.where(me % 4 == 3, solved[...], state + term + rhs[...])
    copies = [store(COARSEN - 1, end)]
    state = state + 0.25 * term
    copies.append(store(0, state))
    for i in range(1, COARSEN - 1):
        state = state + 0.25 * conv_tanh(state, later_w[i - 1])
        copies.append(store(i, state))
    for copy in copies:
        copy.wait()


def per_device(inputs, guess, weights):
    def send(value, pairs):
        return lax.ppermute(value, "layer", pairs)

    narrow = vmem(STATE, BF16)
    wide = vmem(STATE, F32)
    held = [vmem((CHANS, TAPS), BF16), vmem((COARSEN - 1, CHANS, TAPS), BF16), wide]
    up_inside = [(i, i + 1) for i in range(0, DEVICES, 2)]
    up_between = [(i, i + 1) for i in range(1, DEVICES - 1, 2)]
    scratch = [pltpu.VMEM((CHANS, CELLS), F32), pltpu.SemaphoreType.DMA((COARSEN + 1,))]

    from_odd, *kept = kernel_call(
        functools.partial(first_sweep, 1),
        [narrow, *held],
        [inputs, guess, weights],
        "first_sweep_odd",
        4,
        hbm=(0, 1, 2),
        scratch=scratch,
    )
    left_even = send(from_odd, up_between)
    from_even, own_w, later_w, start = kernel_call(
        functools.partial(first_sweep, 0),
        [narrow, *held],
        [inputs, guess, weights, *kept],
        "first_sweep_even",
        4,
        hbm=(0, 1, 2),
        scratch=scratch,
        aliases={3: 1, 4: 2, 5: 3},
    )
    left_odd = send(from_even, up_inside)
    even_w = send(own_w, up_inside)

    left_even, start = kernel_call(
        in_order, [narrow, wide], [left_even, start], "even_first", 1, aliases={0: 0, 1: 1}
    )
    rhs, solved, c1 = kernel_call(
        second_sweep_lead,
        [wide, wide, narrow],
        [left_odd, own_w, later_w, start],
        "second_sweep_lead",
        40,
    )
    got3 = send(c1, [(1, 3)])
    rhs, first = kernel_call(
        second_sweep,
        [wide, wide],
        [left_odd, left_even, own_w, later_w, start, rhs],
        "second_sweep",
        4,
        aliases={5: 0},
    )
    first = send(first, [(4, 5), (8, 9)])
    even_rhs = send(rhs, up_inside)
    both = [even_rhs, rhs, even_w, own_w]
    got3, solved = kernel_call(
        in_order, [narrow, wide], [got3, solved], "lead_first", 10, aliases={0: 0, 1: 1}
    )

    def chained(body, args, name, steps, out=narrow):
        nonlocal solved
        value, solved = kernel_call(
            body, [out, wide], [*args, solved], name, steps, aliases={len(args): 1}
        )
        return value

    def pair(owners, keep, got, name):
        return chained(functools.partial(two_steps, owners, keep), [*both, got], name, 2)

    upper1 = pair((3,), True, got3, "relax_lead")
    got4 = send(upper1, [(3, 5)])
    c5 = chained(functools.partial(one_step, (5, 9)), [first, rhs, own_w], "relax_first", 1)
    got3_rest = send(c5, [(5, 7), (9, 11)])
    c5_lead = pair((5,), False, got4, "again_lead")
    got5 = send(c5_lead, [(5, 7)])
    upper = pair((7, 11), False, got3_rest, "relax_rest")
    got4_rest = send(upper, [(7, 9), (11, 13)])
    upper_prev = send(upper, [(7, 11), (11, 15)])
    z2 = pair((7,), True, got5, "again_end_lead")
    got6 = send(z2, [(7, 11)])
    c9 = pair((9, 13), False, got4_rest, "again_rest")
    got5_rest = send(c9, [(9, 11), (13, 15)])
    base = chained(
        functools.partial(coarse_base, (11, 15)), [upper_prev, own_w], "coarse_base", 1, wide
    )
    pair((11, 15), True, got5_rest, "again_end_rest")
    z3 = chained(lead_step, [got6, base, own_w, got3, got4, z2], "coarse_lead", 1)
    got7 = send(z3, [(11, 13), (7, 9)])
    got7b = send(z3, [(11, 15), (3, 2), (5, 4), (7, 8)])
    c13 = chained(lead_two_steps, [got7, z3, got5, *both], "final_lead", 2)
    got8 = send(c13, [(13, 15), (9, 11)])
    got8b = send(c13, [(13, 14), (9, 10), (11, 12), (7, 6)])
    (solved,) = kernel_call(
        end_step, [wide], [got7b, base, own_w, solved], "coarse_end", 1, aliases={3: 0}
    )
    return kernel_call(
        last_sweep,
        [jax.ShapeDtypeStruct((COARSEN, CHANS, CELLS), F32)],
        [start, got8b, got8, got3, got4, got5, got7, got7b, *both, later_w, solved],
        "last_sweep",
        4,
        scratch=[
            pltpu.VMEM(STATE, F32),
            pltpu.VMEM((COARSEN, CHANS, CELLS), F32),
            pltpu.SemaphoreType.DMA((COARSEN,)),
        ],
    )[0]


def solution(mesh):
    return jax.shard_map(
        per_device,
        mesh=mesh,
        in_specs=(P(None, "batch"), P("layer", None, "batch"), P("layer", None, None)),
        out_specs=P("layer", None, "batch"),
        check_vma=False,
    )
```

profile of v0, /device:TPU:248, one launch (start us, length us, event | category | flops | bytes accessed | tf_op | source)
XLA Modules:
  0.0 52.6 jit_solution(16237402786383908119)
XLA Ops:
  0.1 1.3 %collective-permute-start = (bf16[256,256]{1,0:T(8,128)(2,1)S(1)}, bf16[256,256]{1,0:T(8,128)(2,1)S(1)}, u32[]{:S(2)}, u32[]{:S(2)}) collective-permute-start(bf16[256,256]{1,0:T(8,128)(2,1)S(1)} %get-tuple-element.41), channel_id=1, source_target_pairs={{1,2},{3,4},{5,6},{7,8},{9,10},{11,12},{13,14},{17,18},{19,20},{21... | collective-permute-start | bytes 393224 | tf_op jit(solution)/shard_map/ppermute | solution.py:257
  1.4 4.6 %first_sweep_even.1 = (bf16[256,256]{1,0:T(8,128)(2,1)S(1)}, bf16[256,2304]{1,0:T(8,128)(2,1)S(1)}, bf16[3,256,2304]{2,1,0:T(8,128)(2,1)S(1)}, f32[256,256]{1,0:T(8,128)S(1)}) custom-call(f32[256,256]{1,0:T(8,128)} %refs_0_.3, f32[1,256,256]{2,1,0:T(8,128)} %refs_1_.3, ...), custom_call_target="tpu_custom_call", output_to_operand_aliasing={{1}: (3, {}), {2}: (4, {}), {3}: (5, {})} | custom-call | flops 1207959552 | bytes 1048576 | tf_op jit(solution)/shard_map/first_sweep_even/pallas_call | solution.py:51
  6.0 1.3 %collective-permute-start.1 = (bf16[256,256]{1,0:T(8,128)(2,1)S(1)}, bf16[256,256]{1,0:T(8,128)(2,1)S(1)}, u32[]{:S(2)}, u32[]{:S(2)}) collective-permute-start(bf16[256,256]{1,0:T(8,128)(2,1)S(1)} %get-tuple-element.47), channel_id=1, source_target_pairs={{0,1},{2,3},{4,5},{6,7},{8,9},{10,11},{12,13},{14,15},{16,17},{18,... | collective-permute-start | bytes 393224 | tf_op jit(solution)/shard_map/ppermute | solution.py:257
  7.3 1.4 %collective-permute-start.3 = (bf16[256,2304]{1,0:T(8,128)(2,1)S(1)}, bf16[256,2304]{1,0:T(8,128)(2,1)S(1)}, u32[]{:S(2)}, u32[]{:S(2)}) collective-permute-start(bf16[256,2304]{1,0:T(8,128)(2,1)S(1)} %get-tuple-element.49.own_w), channel_id=1, source_target_pairs={{0,1},{2,3},{4,5},{6,7},{8,9},{10,11},{12,13},{14,15},{16,17},{18,... | collective-permute-start | bytes 3538952 | tf_op jit(solution)/shard_map/ppermute | solution.py:257
  8.6 0.3 collective-permute-done.refs_0_
  9.0 0.0 collective-permute-done.1.left_odd
  9.0 0.7 %collective-permute-start.4 = (bf16[256,256]{1,0:T(8,128)(2,1)S(1)}, bf16[256,256]{1,0:T(8,128)(2,1)S(1)}, u32[]{:S(2)}, u32[]{:S(2)}) collective-permute-start(bf16[256,256]{1,0:T(8,128)(2,1)S(1)} %get-tuple-element.53), channel_id=1, source_target_pairs={{1,3},{17,19},{33,35},{49,51},{65,67},{81,83},{97,99},{113,115},{1... | collective-permute-start | bytes 393224 | tf_op jit(solution)/shard_map/ppermute | solution.py:257
  9.6 2.8 %second_sweep.1 = (f32[256,256]{1,0:T(8,128)S(1)}, f32[256,256]{1,0:T(8,128)S(1)}) custom-call(bf16[256,256]{1,0:T(8,128)(2,1)S(1)} %collective-permute-done.1.left_odd, bf16[256,256]{1,0:T(8,128)(2,1)S(1)} %get-tuple-element.48.left_even, bf16[256,2304]{1,0:T(8,128)(2,1)S(1)} %get-tuple-element.49.own_w, ...), custom_call_target="tpu_custom_call", output_to_operand_aliasing={{0}: (5, {})} | custom-call | flops 1207959552 | bytes 1048576 | tf_op jit(solution)/shard_map/second_sweep/pallas_call | solution.py:51
  12.4 0.7 %collective-permute-start.6 = (f32[256,256]{1,0:T(8,128)S(1)}, f32[256,256]{1,0:T(8,128)S(1)}, u32[]{:S(2)}, u32[]{:S(2)}) collective-permute-start(f32[256,256]{1,0:T(8,128)S(1)} %get-tuple-element.58), channel_id=1, source_target_pairs={{4,5},{8,9},{20,21},{24,25},{36,37},{40,41},{52,53},{56,57},{68,69... | collective-permute-start | bytes 786440 | tf_op jit(solution)/shard_map/ppermute | solution.py:257
  13.1 1.5 %collective-permute-start.2 = (f32[256,256]{1,0:T(8,128)S(1)}, f32[256,256]{1,0:T(8,128)S(1)}, u32[]{:S(2)}, u32[]{:S(2)}) collective-permute-start(f32[256,256]{1,0:T(8,128)S(1)} %get-tuple-element.52.rhs), channel_id=1, source_target_pairs={{0,1},{2,3},{4,5},{6,7},{8,9},{10,11},{12,13},{14,15},{16,17},{18,... | collective-permute-start | bytes 786440 | tf_op jit(solution)/shard_map/ppermute | solution.py:257
  14.7 0.0 collective-permute-done.4.refs_0_
  14.7 1.1 %collective-permute-done.2.even_rhs = f32[256,256]{1,0:T(8,128)S(1)} collective-permute-done((f32[256,256]{1,0:T(8,128)S(1)}, f32[256,256]{1,0:T(8,128)S(1)}, u32[]{:S(2)}, u32[]{:S(2)}) %collective-permute-start.2) | collective-permute-done | bytes 262176 | tf_op jit(solution)/shard_map/ppermute | solution.py:257
  15.8 0.7 %collective-permute-start.5 = (bf16[256,256]{1,0:T(8,128)(2,1)S(1)}, bf16[256,256]{1,0:T(8,128)(2,1)S(1)}, u32[]{:S(2)}, u32[]{:S(2)}) collective-permute-start(bf16[256,256]{1,0:T(8,128)(2,1)S(1)} %get-tuple-element.57), channel_id=1, source_target_pairs={{3,5},{19,21},{35,37},{51,53},{67,69},{83,85},{99,101},{115,117},{... | collective-permute-start | bytes 393224 | tf_op jit(solution)/shard_map/ppermute | solution.py:257
  16.5 0.7 %collective-permute-start.8 = (bf16[256,256]{1,0:T(8,128)(2,1)S(1)}, bf16[256,256]{1,0:T(8,128)(2,1)S(1)}, u32[]{:S(2)}, u32[]{:S(2)}) collective-permute-start(bf16[256,256]{1,0:T(8,128)(2,1)S(1)} %get-tuple-element.62), channel_id=1, source_target_pairs={{5,7},{9,11},{21,23},{25,27},{37,39},{41,43},{53,55},{57,59},{69,7... | collective-permute-start | bytes 393224 | tf_op jit(solution)/shard_map/ppermute | solution.py:257
  17.2 0.7 %collective-permute-start.7 = (bf16[256,256]{1,0:T(8,128)(2,1)S(1)}, bf16[256,256]{1,0:T(8,128)(2,1)S(1)}, u32[]{:S(2)}, u32[]{:S(2)}) collective-permute-start(bf16[256,256]{1,0:T(8,128)(2,1)S(1)} %get-tuple-element.61), channel_id=1, source_target_pairs={{5,7},{21,23},{37,39},{53,55},{69,71},{85,87},{101,103},{117,119},... | collective-permute-start | bytes 393224 | tf_op jit(solution)/shard_map/ppermute | solution.py:257
  17.9 0.7 %collective-permute-start.11 = (bf16[256,256]{1,0:T(8,128)(2,1)S(1)}, bf16[256,256]{1,0:T(8,128)(2,1)S(1)}, u32[]{:S(2)}, u32[]{:S(2)}) collective-permute-start(bf16[256,256]{1,0:T(8,128)(2,1)S(1)} %get-tuple-element.66), channel_id=1, source_target_pairs={{7,9},{11,13},{23,25},{27,29},{39,41},{43,45},{55,57},{59,61},{71,... | collective-permute-start | bytes 393224 | tf_op jit(solution)/shard_map/ppermute | solution.py:257
  18.6 0.7 %collective-permute-start.10 = (bf16[256,256]{1,0:T(8,128)(2,1)S(1)}, bf16[256,256]{1,0:T(8,128)(2,1)S(1)}, u32[]{:S(2)}, u32[]{:S(2)}) collective-permute-start(bf16[256,256]{1,0:T(8,128)(2,1)S(1)} %get-tuple-element.66), channel_id=1, source_target_pairs={{7,11},{11,15},{23,27},{27,31},{39,43},{43,47},{55,59},{59,63},{71... | collective-permute-start | bytes 393224 | tf_op jit(solution)/shard_map/ppermute | solution.py:257
  19.3 0.0 collective-permute-done.7.got.early5.got5
  19.3 0.0 collective-permute-done.11.got
  19.3 0.2 again_rest.1
  19.5 0.7 %collective-permute-start.12 = (bf16[256,256]{1,0:T(8,128)(2,1)S(1)}, bf16[256,256]{1,0:T(8,128)(2,1)S(1)}, u32[]{:S(2)}, u32[]{:S(2)}) collective-permute-start(bf16[256,256]{1,0:T(8,128)(2,1)S(1)} %get-tuple-element.70), channel_id=1, source_target_pairs={{9,11},{13,15},{25,27},{29,31},{41,43},{45,47},{57,59},{61,63},{73... | collective-permute-start | bytes 393224 | tf_op jit(solution)/shard_map/ppermute | solution.py:257
  20.2 0.7 %collective-permute-start.9 = (bf16[256,256]{1,0:T(8,128)(2,1)S(1)}, bf16[256,256]{1,0:T(8,128)(2,1)S(1)}, u32[]{:S(2)}, u32[]{:S(2)}) collective-permute-start(bf16[256,256]{1,0:T(8,128)(2,1)S(1)} %get-tuple-element.65.mine), channel_id=1, source_target_pairs={{7,11},{23,27},{39,43},{55,59},{71,75},{87,91},{103,107},{119,123}... | collective-permute-start | bytes 393224 | tf_op jit(solution)/shard_map/ppermute | solution.py:257
  20.9 0.0 collective-permute-done.12.got
  20.9 0.7 %again_end_rest.1 = (bf16[256,256]{1,0:T(8,128)(2,1)}, f32[256,256]{1,0:T(8,128)S(1)}) custom-call(f32[256,256]{1,0:T(8,128)S(1)} %collective-permute-done.2.even_rhs, f32[256,256]{1,0:T(8,128)S(1)} %get-tuple-element.52.rhs, bf16[256,2304]{1,0:T(8,128)(2,1)S(1)} %collective-permute-done.3.even_w, ...), custom_call_target="tpu_custom_call", output_to_operand_aliasing={{1}: (5, {})} | custom-call | flops 603979776 | bytes 1048576 | tf_op jit(solution)/shard_map/again_end_rest/pallas_call | solution.py:51
  21.6 0.0 collective-permute-done.9.got
  21.6 0.7 %collective-permute-start.13 = (bf16[256,256]{1,0:T(8,128)(2,1)S(1)}, bf16[256,256]{1,0:T(8,128)(2,1)S(1)}, u32[]{:S(2)}, u32[]{:S(2)}) collective-permute-start(bf16[256,256]{1,0:T(8,128)(2,1)S(1)} %get-tuple-element.73.mine), channel_id=1, source_target_pairs={{11,13},{7,9},{27,29},{23,25},{43,45},{39,41},{59,61},{55,57},{75,... | collective-permute-start | bytes 393224 | tf_op jit(solution)/shard_map/ppermute | solution.py:257
  22.3 0.7 %collective-permute-start.16 = (bf16[256,256]{1,0:T(8,128)(2,1)S(1)}, bf16[256,256]{1,0:T(8,128)(2,1)S(1)}, u32[]{:S(2)}, u32[]{:S(2)}) collective-permute-start(bf16[256,256]{1,0:T(8,128)(2,1)S(1)} %get-tuple-element.73.mine), channel_id=1, source_target_pairs={{11,15},{3,2},{5,4},{7,8},{27,31},{19,18},{21,20},{23,24},{43,47},... | collective-permute-start | bytes 393224 | tf_op jit(solution)/shard_map/ppermute | solution.py:257
  23.0 0.0 collective-permute-done.13.got.got7
  23.0 0.7 %collective-permute-start.15 = (bf16[256,256]{1,0:T(8,128)(2,1)S(1)}, bf16[256,256]{1,0:T(8,128)(2,1)S(1)}, u32[]{:S(2)}, u32[]{:S(2)}) collective-permute-start(bf16[256,256]{1,0:T(8,128)(2,1)S(1)} %get-tuple-element.75), channel_id=1, source_target_pairs={{13,15},{9,11},{29,31},{25,27},{45,47},{41,43},{61,63},{57,59},{77... | collective-permute-start | bytes 393224 | tf_op jit(solution)/shard_map/ppermute | solution.py:257
  23.7 1.3 %collective-permute-start.14 = (bf16[256,256]{1,0:T(8,128)(2,1)S(1)}, bf16[256,256]{1,0:T(8,128)(2,1)S(1)}, u32[]{:S(2)}, u32[]{:S(2)}) collective-permute-start(bf16[256,256]{1,0:T(8,128)(2,1)S(1)} %get-tuple-element.75), channel_id=1, source_target_pairs={{13,14},{9,10},{11,12},{7,6},{29,30},{25,26},{27,28},{23,22},{45,4... | collective-permute-start | bytes 393224 | tf_op jit(solution)/shard_map/ppermute | solution.py:257
  25.0 24.7 %collective-permute-done.14.got8b = bf16[256,256]{1,0:T(8,128)(2,1)S(1)} collective-permute-done((bf16[256,256]{1,0:T(8,128)(2,1)S(1)}, bf16[256,256]{1,0:T(8,128)(2,1)S(1)}, u32[]{:S(2)}, u32[]{:S(2)}) %collective-permute-start.14) | collective-permute-done | bytes 131104 | tf_op jit(solution)/shard_map/ppermute | solution.py:257
  49.7 2.7 %last_sweep.1 = f32[4,256,256]{2,1,0:T(8,128)} custom-call(f32[256,256]{1,0:T(8,128)S(1)} %get-tuple-element.46._.start, bf16[256,256]{1,0:T(8,128)(2,1)S(1)} %collective-permute-done.14.got8b, bf16[256,256]{1,0:T(8,128)(2,1)S(1)} %collective-permute-done.15.got8, bf16[256,256]{1,0:T(8,128)(2,1)S(1)} %get-tuple-element.55.got.early3.got3, ...), custom_call_target="tpu_custom_call" | custom-call | flops 1207959552 | bytes 1048576 | tf_op jit(solution)/shard_map/last_sweep/pallas_call | solution.py:51
  (20 shorter events, 0.2 us)
Async XLA Ops:
  0.1 8.9 %collective-permute-start = (bf16[256,256]{1,0:T(8,128)(2,1)S(1)}, bf16[256,256]{1,0:T(8,128)(2,1)S(1)}, u32[]{:S(2)}, u32[]{:S(2)}) collective-permute-start(bf16[256,256]{1,0:T(8,128)(2,1)S(1)} %get-tuple-element.41), channel_id=1, source_target_pairs={{1,2},{3,4},{5,6},{7,8},{9,10},{11,12},{13,14},{17,18},{19,20},{21... | collective-permute-start | bytes 393224 | tf_op jit(solution)/shard_map/ppermute | solution.py:257
  6.0 3.0 %collective-permute-start.1 = (bf16[256,256]{1,0:T(8,128)(2,1)S(1)}, bf16[256,256]{1,0:T(8,128)(2,1)S(1)}, u32[]{:S(2)}, u32[]{:S(2)}) collective-permute-start(bf16[256,256]{1,0:T(8,128)(2,1)S(1)} %get-tuple-element.47), channel_id=1, source_target_pairs={{0,1},{2,3},{4,5},{6,7},{8,9},{10,11},{12,13},{14,15},{16,17},{18,... | collective-permute-start | bytes 393224 | tf_op jit(solution)/shard_map/ppermute | solution.py:257
  7.3 8.5 %collective-permute-start.3 = (bf16[256,2304]{1,0:T(8,128)(2,1)S(1)}, bf16[256,2304]{1,0:T(8,128)(2,1)S(1)}, u32[]{:S(2)}, u32[]{:S(2)}) collective-permute-start(bf16[256,2304]{1,0:T(8,128)(2,1)S(1)} %get-tuple-element.49.own_w), channel_id=1, source_target_pairs={{0,1},{2,3},{4,5},{6,7},{8,9},{10,11},{12,13},{14,15},{16,17},{18,... | collective-permute-start | bytes 3538952 | tf_op jit(solution)/shard_map/ppermute | solution.py:257
  9.0 5.7 %collective-permute-start.4 = (bf16[256,256]{1,0:T(8,128)(2,1)S(1)}, bf16[256,256]{1,0:T(8,128)(2,1)S(1)}, u32[]{:S(2)}, u32[]{:S(2)}) collective-permute-start(bf16[256,256]{1,0:T(8,128)(2,1)S(1)} %get-tuple-element.53), channel_id=1, source_target_pairs={{1,3},{17,19},{33,35},{49,51},{65,67},{81,83},{97,99},{113,115},{1... | collective-permute-start | bytes 393224 | tf_op jit(solution)/shard_map/ppermute | solution.py:257
  12.4 4.0 %collective-permute-start.6 = (f32[256,256]{1,0:T(8,128)S(1)}, f32[256,256]{1,0:T(8,128)S(1)}, u32[]{:S(2)}, u32[]{:S(2)}) collective-permute-start(f32[256,256]{1,0:T(8,128)S(1)} %get-tuple-element.58), channel_id=1, source_target_pairs={{4,5},{8,9},{20,21},{24,25},{36,37},{40,41},{52,53},{56,57},{68,69... | collective-permute-start | bytes 786440 | tf_op jit(solution)/shard_map/ppermute | solution.py:257
  13.1 2.7 %collective-permute-start.2 = (f32[256,256]{1,0:T(8,128)S(1)}, f32[256,256]{1,0:T(8,128)S(1)}, u32[]{:S(2)}, u32[]{:S(2)}) collective-permute-start(f32[256,256]{1,0:T(8,128)S(1)} %get-tuple-element.52.rhs), channel_id=1, source_target_pairs={{0,1},{2,3},{4,5},{6,7},{8,9},{10,11},{12,13},{14,15},{16,17},{18,... | collective-permute-start | bytes 786440 | tf_op jit(solution)/shard_map/ppermute | solution.py:257
  15.8 1.4 %collective-permute-start.5 = (bf16[256,256]{1,0:T(8,128)(2,1)S(1)}, bf16[256,256]{1,0:T(8,128)(2,1)S(1)}, u32[]{:S(2)}, u32[]{:S(2)}) collective-permute-start(bf16[256,256]{1,0:T(8,128)(2,1)S(1)} %get-tuple-element.57), channel_id=1, source_target_pairs={{3,5},{19,21},{35,37},{51,53},{67,69},{83,85},{99,101},{115,117},{... | collective-permute-start | bytes 393224 | tf_op jit(solution)/shard_map/ppermute | solution.py:257
  16.5 1.4 %collective-permute-start.8 = (bf16[256,256]{1,0:T(8,128)(2,1)S(1)}, bf16[256,256]{1,0:T(8,128)(2,1)S(1)}, u32[]{:S(2)}, u32[]{:S(2)}) collective-permute-start(bf16[256,256]{1,0:T(8,128)(2,1)S(1)} %get-tuple-element.62), channel_id=1, source_target_pairs={{5,7},{9,11},{21,23},{25,27},{37,39},{41,43},{53,55},{57,59},{69,7... | collective-permute-start | bytes 393224 | tf_op jit(solution)/shard_map/ppermute | solution.py:257
  17.2 2.1 %collective-permute-start.7 = (bf16[256,256]{1,0:T(8,128)(2,1)S(1)}, bf16[256,256]{1,0:T(8,128)(2,1)S(1)}, u32[]{:S(2)}, u32[]{:S(2)}) collective-permute-start(bf16[256,256]{1,0:T(8,128)(2,1)S(1)} %get-tuple-element.61), channel_id=1, source_target_pairs={{5,7},{21,23},{37,39},{53,55},{69,71},{85,87},{101,103},{117,119},... | collective-permute-start | bytes 393224 | tf_op jit(solution)/shard_map/ppermute | solution.py:257
  17.9 1.4 %collective-permute-start.11 = (bf16[256,256]{1,0:T(8,128)(2,1)S(1)}, bf16[256,256]{1,0:T(8,128)(2,1)S(1)}, u32[]{:S(2)}, u32[]{:S(2)}) collective-permute-start(bf16[256,256]{1,0:T(8,128)(2,1)S(1)} %get-tuple-element.66), channel_id=1, source_target_pairs={{7,9},{11,13},{23,25},{27,29},{39,41},{43,45},{55,57},{59,61},{71,... | collective-permute-start | bytes 393224 | tf_op jit(solution)/shard_map/ppermute | solution.py:257
  18.6 2.3 %collective-permute-start.10 = (bf16[256,256]{1,0:T(8,128)(2,1)S(1)}, bf16[256,256]{1,0:T(8,128)(2,1)S(1)}, u32[]{:S(2)}, u32[]{:S(2)}) collective-permute-start(bf16[256,256]{1,0:T(8,128)(2,1)S(1)} %get-tuple-element.66), channel_id=1, source_target_pairs={{7,11},{11,15},{23,27},{27,31},{39,43},{43,47},{55,59},{59,63},{71... | collective-permute-start | bytes 393224 | tf_op jit(solution)/shard_map/ppermute | solution.py:257
  19.5 1.4 %collective-permute-start.12 = (bf16[256,256]{1,0:T(8,128)(2,1)S(1)}, bf16[256,256]{1,0:T(8,128)(2,1)S(1)}, u32[]{:S(2)}, u32[]{:S(2)}) collective-permute-start(bf16[256,256]{1,0:T(8,128)(2,1)S(1)} %get-tuple-element.70), channel_id=1, source_target_pairs={{9,11},{13,15},{25,27},{29,31},{41,43},{45,47},{57,59},{61,63},{73... | collective-permute-start | bytes 393224 | tf_op jit(solution)/shard_map/ppermute | solution.py:257
  20.2 1.4 %collective-permute-start.9 = (bf16[256,256]{1,0:T(8,128)(2,1)S(1)}, bf16[256,256]{1,0:T(8,128)(2,1)S(1)}, u32[]{:S(2)}, u32[]{:S(2)}) collective-permute-start(bf16[256,256]{1,0:T(8,128)(2,1)S(1)} %get-tuple-element.65.mine), channel_id=1, source_target_pairs={{7,11},{23,27},{39,43},{55,59},{71,75},{87,91},{103,107},{119,123}... | collective-permute-start | bytes 393224 | tf_op jit(solution)/shard_map/ppermute | solution.py:257
  21.6 1.3 %collective-permute-start.13 = (bf16[256,256]{1,0:T(8,128)(2,1)S(1)}, bf16[256,256]{1,0:T(8,128)(2,1)S(1)}, u32[]{:S(2)}, u32[]{:S(2)}) collective-permute-start(bf16[256,256]{1,0:T(8,128)(2,1)S(1)} %get-tuple-element.73.mine), channel_id=1, source_target_pairs={{11,13},{7,9},{27,29},{23,25},{43,45},{39,41},{59,61},{55,57},{75,... | collective-permute-start | bytes 393224 | tf_op jit(solution)/shard_map/ppermute | solution.py:257
  22.3 2.7 %collective-permute-start.16 = (bf16[256,256]{1,0:T(8,128)(2,1)S(1)}, bf16[256,256]{1,0:T(8,128)(2,1)S(1)}, u32[]{:S(2)}, u32[]{:S(2)}) collective-permute-start(bf16[256,256]{1,0:T(8,128)(2,1)S(1)} %get-tuple-element.73.mine), channel_id=1, source_target_pairs={{11,15},{3,2},{5,4},{7,8},{27,31},{19,18},{21,20},{23,24},{43,47},... | collective-permute-start | bytes 393224 | tf_op jit(solution)/shard_map/ppermute | solution.py:257
  23.0 2.0 %collective-permute-start.15 = (bf16[256,256]{1,0:T(8,128)(2,1)S(1)}, bf16[256,256]{1,0:T(8,128)(2,1)S(1)}, u32[]{:S(2)}, u32[]{:S(2)}) collective-permute-start(bf16[256,256]{1,0:T(8,128)(2,1)S(1)} %get-tuple-element.75), channel_id=1, source_target_pairs={{13,15},{9,11},{29,31},{25,27},{45,47},{41,43},{61,63},{57,59},{77... | collective-permute-start | bytes 393224 | tf_op jit(solution)/shard_map/ppermute | solution.py:257
  23.7 26.0 %collective-permute-start.14 = (bf16[256,256]{1,0:T(8,128)(2,1)S(1)}, bf16[256,256]{1,0:T(8,128)(2,1)S(1)}, u32[]{:S(2)}, u32[]{:S(2)}) collective-permute-start(bf16[256,256]{1,0:T(8,128)(2,1)S(1)} %get-tuple-element.75), channel_id=1, source_target_pairs={{13,14},{9,10},{11,12},{7,6},{29,30},{25,26},{27,28},{23,22},{45,4... | collective-permute-start | bytes 393224 | tf_op jit(solution)/shard_map/ppermute | solution.py:257
where the time goes:
time: 52.9 us; the launch traced here: 52.6 us
  waiting for transfers between devices  26.1 us (49%)
  starting transfers between devices  14.8 us (28%)
  Pallas kernels  11.2 us (21%)
    ppermute x17, waiting for transfers between devices, send(): return lax.ppermute(value, 'layer', pairs)  26.1 us
    ppermute x17, starting transfers between devices, send(): return lax.ppermute(value, 'layer', pairs)  14.8 us
    pallas_call x18, Pallas kernels, kernel_call(): pl.pallas_call(body, out_shape=outs, in_specs=[pl.BlockSpec(memory_space=...  11.2 us
  transfers between devices with their start and end apart: 17, of which 3 were waited for; matrix products, arithmetic and copies ran while one was open for 0% of the time, Pallas kernels for 16%

commit v1 on v0

--- a/solution.py
+++ b/solution.py
@@ -23,19 +23,26 @@
     column = lax.broadcasted_iota(jnp.int32, STATE, 0) % SIDE
     before = jnp.where(column == 0, 0.0, pltpu.roll(state, 1, 0)).astype(BF16)
     after = jnp.where(column == SIDE - 1, 0.0, pltpu.roll(state, CELLS - 1, 0)).astype(BF16)
-    trio = [before, state.astype(BF16), after]
+    here = state.astype(BF16)
     edge = jnp.zeros((SIDE, CHANS), BF16)
-    above = [jnp.concatenate([edge, x[:-SIDE]], 0) for x in trio]
-    below = [jnp.concatenate([x[SIDE:], edge], 0) for x in trio]
-    total = None
-    for tap, piece in enumerate(above + trio + below):
-        part = lax.dot_general(
+
+    def product(piece, row, column):
+        if row == 0:
+            piece = jnp.concatenate([edge, piece[:-SIDE]], 0)
+        if row == 2:
+            piece = jnp.concatenate([piece[SIDE:], edge], 0)
+        tap = 3 * row + column
+        return lax.dot_general(
             piece,
             weight[:, tap * CHANS : (tap + 1) * CHANS],
             (((1,), (1,)), ((), ())),
             preferred_element_type=F32,
         )
-        total = part if total is None else total + part
+
+    total = product(here, 1, 1)
+    for column, piece in ((1, -here), (0, -before), (2, -after)):
+        for row in (0, 2) if column == 1 else (1, 0, 2):
+            total = total - product(piece, row, column)
     return jnp.tanh(total)
 
 
@@ -147,17 +154,37 @@
     return chosen
 
 
+def both_steps(even_rhs, rhs, even_w, own_w, got):
+    value = got[...].astype(F32)
+    value = value + conv_tanh(value, even_w) + even_rhs[...]
+    return value + conv_tanh(value, own_w) + rhs[...]
+
+
 def two_steps(owners, keep, even_rhs, rhs, even_w, own_w, got, _, out, solved):
     @pl.when(either(place(), owners))
     def _():
-        value = got[...].astype(F32)
-        value = value + conv_tanh(value, even_w) + even_rhs[...]
-        value = value + conv_tanh(value, own_w) + rhs[...]
+        value = both_steps(even_rhs, rhs, even_w, own_w, got)
         if keep:
             solved[...] = value
         out[...] = value.astype(BF16)
 
 
+def lead_half(got, even_w, _, out, solved):
+    @pl.when(place() == 3)
+    def _():
+        value = got[...].astype(F32)
+        out[...] = value + conv_tanh(value, even_w)
+
+
+def lead_rest(rhs, own_w, even_rhs, part, _, out, solved):
+    @pl.when(place() == 3)
+    def _():
+        value = part[...] + even_rhs[...]
+        value = value + conv_tanh(value, own_w) + rhs[...]
+        solved[...] = value
+        out[...] = value.astype(BF16)
+
+
 def one_step(owners, first, rhs, own_w, _, out, solved):
     @pl.when(either(place(), owners))
     def _():
@@ -170,13 +197,29 @@
     return value + 4.0 * conv_tanh(value, own_w)
 
 
-def coarse_base(owners, upper, own_w, _, out, solved):
-    @pl.when(either(place(), owners))
+def steps_or_copy(owner, keep, upper, even_rhs, rhs, even_w, own_w, got, _, out, solved):
+    two_steps((owner,), keep, even_rhs, rhs, even_w, own_w, got, _, out, solved)
+
+    @pl.when(place() == 11)
+    def _():
+        out[...] = upper[...]
+
+
+def coarse_base(upper, own_w, _, out, solved):
+    @pl.when(place() == 11)
     def _():
         out[...] = coarse_step(upper, own_w)
 
 
-def lead_step(got, base, own_w, early3, early4, mine, _, out, solved):
+def again_end(even_rhs, rhs, even_w, own_w, got, _, out, solved):
+    @pl.when(either(place(), (11, 13)))
+    def _():
+        value = both_steps(even_rhs, rhs, even_w, own_w, got)
+        solved[...] = value
+        out[...] = value.astype(BF16)
+
+
+def lead_step(got, base, own_w, early3, early4, mine, behind, _, out, solved):
     me = place()
 
     @pl.when(me == 11)
@@ -185,7 +228,7 @@
         solved[...] = value
         out[...] = value.astype(BF16)
 
-    for owner, source in ((3, early3), (5, early4), (7, mine)):
+    for owner, source in ((3, early3), (5, early4), (7, mine), (13, behind)):
 
         @pl.when(me == owner)
         def _():
@@ -201,10 +244,11 @@
             out[...] = source[...]
 
 
-def end_step(got, base, own_w, _, solved):
+def end_step(upper, even_rhs, rhs, even_w, own_w, got, lead, _, solved):
     @pl.when(place() == 15)
     def _():
-        solved[...] = coarse_step(got, own_w) + (solved[...] - base[...])
+        value = both_steps(even_rhs, rhs, even_w, own_w, got) - coarse_step(upper, own_w)
+        solved[...] = value + coarse_step(lead, own_w)
 
 
 def last_sweep(
@@ -308,9 +352,6 @@
     first = send(first, [(4, 5), (8, 9)])
     even_rhs = send(rhs, up_inside)
     both = [even_rhs, rhs, even_w, own_w]
-    got3, solved = kernel_call(
-        in_order, [narrow, wide], [got3, solved], "lead_first", 10, aliases={0: 0, 1: 1}
-    )
 
     def chained(body, args, name, steps, out=narrow):
         nonlocal solved
@@ -322,31 +363,35 @@
     def pair(owners, keep, got, name):
         return chained(functools.partial(two_steps, owners, keep), [*both, got], name, 2)
 
-    upper1 = pair((3,), True, got3, "relax_lead")
+    part = chained(lead_half, [got3, even_w], "lead_first", 10, wide)
+    upper1 = chained(lead_rest, [rhs, own_w, even_rhs, part], "relax_lead", 1)
     got4 = send(upper1, [(3, 5)])
     c5 = chained(functools.partial(one_step, (5, 9)), [first, rhs, own_w], "relax_first", 1)
     got3_rest = send(c5, [(5, 7), (9, 11)])
     c5_lead = pair((5,), False, got4, "again_lead")
     got5 = send(c5_lead, [(5, 7)])
-    upper = pair((7, 11), False, got3_rest, "relax_rest")
-    got4_rest = send(upper, [(7, 9), (11, 13)])
-    upper_prev = send(upper, [(7, 11), (11, 15)])
-    z2 = pair((7,), True, got5, "again_end_lead")
-    got6 = send(z2, [(7, 11)])
-    c9 = pair((9, 13), False, got4_rest, "again_rest")
-    got5_rest = send(c9, [(9, 11), (13, 15)])
-    base = chained(
-        functools.partial(coarse_base, (11, 15)), [upper_prev, own_w], "coarse_base", 1, wide
-    )
-    pair((11, 15), True, got5_rest, "again_end_rest")
-    z3 = chained(lead_step, [got6, base, own_w, got3, got4, z2], "coarse_lead", 1)
-    got7 = send(z3, [(11, 13), (7, 9)])
+    upper7 = pair((7,), False, got3_rest, "relax_rest")
+    got4_rest = send(upper7, [(7, 9)])
+    upper_prev = send(upper7, [(7, 11)])
+    upper11 = pair((11,), False, got3_rest, "relax_last")
+    z2 = chained(
+        functools.partial(steps_or_copy, 7, True), [upper11, *both, got5], "again_end_lead", 2
+    )
+    got6 = send(z2, [(7, 11), (11, 15)])
+    c9 = chained(
+        functools.partial(steps_or_copy, 9, False), [upper11, *both, got4_rest], "again_rest", 2
+    )
+    got5_rest = send(c9, [(9, 11), (11, 13)])
+    base = chained(coarse_base, [upper_prev, own_w], "coarse_base", 1, wide)
+    c13 = chained(again_end, [*both, got5_rest], "again_end_rest", 2)
+    z3 = chained(lead_step, [got6, base, own_w, got3, got4, z2, c13], "coarse_lead", 1)
+    got7 = send(z3, [(11, 13), (7, 9), (13, 15)])
     got7b = send(z3, [(11, 15), (3, 2), (5, 4), (7, 8)])
     c13 = chained(lead_two_steps, [got7, z3, got5, *both], "final_lead", 2)
     got8 = send(c13, [(13, 15), (9, 11)])
     got8b = send(c13, [(13, 14), (9, 10), (11, 12), (7, 6)])
     (solved,) = kernel_call(
-        end_step, [wide], [got7b, base, own_w, solved], "coarse_end", 1, aliases={3: 0}
+        end_step, [wide], [got6, *both, got7, got7b, solved], "coarse_end", 4, aliases={7: 0}
     )
     return kernel_call(
         last_sweep,

time: 52.9 us -> 48.8 us (0.922)
  Pallas kernels: 11.2 us -> 8.09 us
  waiting for transfers between devices: 26.1 us -> 24.9 us
    pallas_call x18 -> x19, Pallas kernels: 11.2 us -> 8.09 us  [kernel_call(): pl.pallas_call(body, out_shape=outs, in_specs=[pl.BlockSpec(memory_space=...]
    ppermute x17, waiting for transfers between devices: 26.1 us -> 24.9 us  [send(): return lax.ppermute(value, 'layer', pairs)]
  transfers between devices with their start and end apart: 17 -> 17, of which waited for: 3 -> 3; matrix products, arithmetic and copies ran while one was open for 0% -> 0% of each run, Pallas kernels for 16% -> 12%
where the time goes in v1:
time: 48.8 us; the launch traced here: 48.5 us
  waiting for transfers between devices  24.9 us (51%)
  starting transfers between devices  15 us (31%)
  Pallas kernels  8.09 us (17%)
  between operations  0.52 us (1%)
    ppermute x17, waiting for transfers between devices, send(): return lax.ppermute(value, 'layer', pairs)  24.9 us
    ppermute x17, starting transfers between devices, send(): return lax.ppermute(value, 'layer', pairs)  15 us
    pallas_call x19, Pallas kernels, kernel_call(): pl.pallas_call(body, out_shape=outs, in_specs=[pl.BlockSpec(memory_space=...  8.09 us
  transfers between devices with their start and end apart: 17, of which 3 were waited for; matrix products, arithmetic and copies ran while one was open for 0% of the time, Pallas kernels for 12%

profile of v1, /device:TPU:248, one launch (start us, length us, event | category | flops | bytes accessed | tf_op | source)
XLA Modules:
  0.0 48.5 jit_solution(6847527899823567014)
XLA Ops:
  0.1 1.3 %collective-permute-start = (bf16[256,256]{1,0:T(8,128)(2,1)S(1)}, bf16[256,256]{1,0:T(8,128)(2,1)S(1)}, u32[]{:S(2)}, u32[]{:S(2)}) collective-permute-start(bf16[256,256]{1,0:T(8,128)(2,1)S(1)} %get-tuple-element.44), channel_id=1, source_target_pairs={{1,2},{3,4},{5,6},{7,8},{9,10},{11,12},{13,14},{17,18},{19,20},{21... | collective-permute-start | bytes 393224 | tf_op jit(solution)/shard_map/ppermute | solution.py:301
  1.4 3.6 %first_sweep_even.1 = (bf16[256,256]{1,0:T(8,128)(2,1)S(1)}, bf16[256,2304]{1,0:T(8,128)(2,1)S(1)}, bf16[3,256,2304]{2,1,0:T(8,128)(2,1)S(1)}, f32[256,256]{1,0:T(8,128)S(1)}) custom-call(f32[256,256]{1,0:T(8,128)} %refs_0_.3, f32[1,256,256]{2,1,0:T(8,128)} %refs_1_.3, ...), custom_call_target="tpu_custom_call", output_to_operand_aliasing={{1}: (3, {}), {2}: (4, {}), {3}: (5, {})} | custom-call | flops 1207959552 | bytes 1048576 | tf_op jit(solution)/shard_map/first_sweep_even/pallas_call | solution.py:58
  5.0 1.3 %collective-permute-start.1 = (bf16[256,256]{1,0:T(8,128)(2,1)S(1)}, bf16[256,256]{1,0:T(8,128)(2,1)S(1)}, u32[]{:S(2)}, u32[]{:S(2)}) collective-permute-start(bf16[256,256]{1,0:T(8,128)(2,1)S(1)} %get-tuple-element.50), channel_id=1, source_target_pairs={{0,1},{2,3},{4,5},{6,7},{8,9},{10,11},{12,13},{14,15},{16,17},{18,... | collective-permute-start | bytes 393224 | tf_op jit(solution)/shard_map/ppermute | solution.py:301
  6.3 1.4 %collective-permute-start.3 = (bf16[256,2304]{1,0:T(8,128)(2,1)S(1)}, bf16[256,2304]{1,0:T(8,128)(2,1)S(1)}, u32[]{:S(2)}, u32[]{:S(2)}) collective-permute-start(bf16[256,2304]{1,0:T(8,128)(2,1)S(1)} %get-tuple-element.52.own_w), channel_id=1, source_target_pairs={{0,1},{2,3},{4,5},{6,7},{8,9},{10,11},{12,13},{14,15},{16,17},{18,... | collective-permute-start | bytes 3538952 | tf_op jit(solution)/shard_map/ppermute | solution.py:301
  7.7 0.3 collective-permute-done.refs_0_
  8.0 0.7 %collective-permute-start.5 = (bf16[256,256]{1,0:T(8,128)(2,1)S(1)}, bf16[256,256]{1,0:T(8,128)(2,1)S(1)}, u32[]{:S(2)}, u32[]{:S(2)}) collective-permute-start(bf16[256,256]{1,0:T(8,128)(2,1)S(1)} %get-tuple-element.57), channel_id=1, source_target_pairs={{1,3},{17,19},{33,35},{49,51},{65,67},{81,83},{97,99},{113,115},{1... | collective-permute-start | bytes 393224 | tf_op jit(solution)/shard_map/ppermute | solution.py:301
  8.6 1.9 %second_sweep.1 = (f32[256,256]{1,0:T(8,128)S(1)}, f32[256,256]{1,0:T(8,128)S(1)}) custom-call(bf16[256,256]{1,0:T(8,128)(2,1)S(1)} %collective-permute-done.1.left_odd, bf16[256,256]{1,0:T(8,128)(2,1)S(1)} %get-tuple-element.51.left_even, bf16[256,2304]{1,0:T(8,128)(2,1)S(1)} %get-tuple-element.52.own_w, ...), custom_call_target="tpu_custom_call", output_to_operand_aliasing={{0}: (5, {})} | custom-call | flops 1207959552 | bytes 1048576 | tf_op jit(solution)/shard_map/second_sweep/pallas_call | solution.py:58
  10.5 0.7 %collective-permute-start.4 = (f32[256,256]{1,0:T(8,128)S(1)}, f32[256,256]{1,0:T(8,128)S(1)}, u32[]{:S(2)}, u32[]{:S(2)}) collective-permute-start(f32[256,256]{1,0:T(8,128)S(1)} %get-tuple-element.56), channel_id=1, source_target_pairs={{4,5},{8,9},{20,21},{24,25},{36,37},{40,41},{52,53},{56,57},{68,69... | collective-permute-start | bytes 786440 | tf_op jit(solution)/shard_map/ppermute | solution.py:301
  11.2 1.6 %collective-permute-start.2 = (f32[256,256]{1,0:T(8,128)S(1)}, f32[256,256]{1,0:T(8,128)S(1)}, u32[]{:S(2)}, u32[]{:S(2)}) collective-permute-start(f32[256,256]{1,0:T(8,128)S(1)} %get-tuple-element.55.rhs), channel_id=1, source_target_pairs={{0,1},{2,3},{4,5},{6,7},{8,9},{10,11},{12,13},{14,15},{16,17},{18,... | collective-permute-start | bytes 786440 | tf_op jit(solution)/shard_map/ppermute | solution.py:301
  12.8 0.0 collective-permute-done.5.got.early3.got3
  12.8 0.0 collective-permute-done.3.even_w
  12.8 1.1 %collective-permute-done.2.even_rhs = f32[256,256]{1,0:T(8,128)S(1)} collective-permute-done((f32[256,256]{1,0:T(8,128)S(1)}, f32[256,256]{1,0:T(8,128)S(1)}, u32[]{:S(2)}, u32[]{:S(2)}) %collective-permute-start.2) | collective-permute-done | bytes 262176 | tf_op jit(solution)/shard_map/ppermute | solution.py:301
  13.9 0.7 %collective-permute-start.7 = (bf16[256,256]{1,0:T(8,128)(2,1)S(1)}, bf16[256,256]{1,0:T(8,128)(2,1)S(1)}, u32[]{:S(2)}, u32[]{:S(2)}) collective-permute-start(bf16[256,256]{1,0:T(8,128)(2,1)S(1)} %get-tuple-element.63), channel_id=1, source_target_pairs={{3,5},{19,21},{35,37},{51,53},{67,69},{83,85},{99,101},{115,117},{... | collective-permute-start | bytes 393224 | tf_op jit(solution)/shard_map/ppermute | solution.py:301
  14.6 0.0 collective-permute-done.4.first
  14.6 0.7 %collective-permute-start.6 = (bf16[256,256]{1,0:T(8,128)(2,1)S(1)}, bf16[256,256]{1,0:T(8,128)(2,1)S(1)}, u32[]{:S(2)}, u32[]{:S(2)}) collective-permute-start(bf16[256,256]{1,0:T(8,128)(2,1)S(1)} %get-tuple-element.62), channel_id=1, source_target_pairs={{5,7},{9,11},{21,23},{25,27},{37,39},{41,43},{53,55},{57,59},{69,7... | collective-permute-start | bytes 393224 | tf_op jit(solution)/shard_map/ppermute | solution.py:301
  15.3 0.0 collective-permute-done.7.got.early4.got4
  15.3 0.7 %collective-permute-start.8 = (bf16[256,256]{1,0:T(8,128)(2,1)S(1)}, bf16[256,256]{1,0:T(8,128)(2,1)S(1)}, u32[]{:S(2)}, u32[]{:S(2)}) collective-permute-start(bf16[256,256]{1,0:T(8,128)(2,1)S(1)} %get-tuple-element.68), channel_id=1, source_target_pairs={{5,7},{21,23},{37,39},{53,55},{69,71},{85,87},{101,103},{117,119},... | collective-permute-start | bytes 393224 | tf_op jit(solution)/shard_map/ppermute | solution.py:301
  16.0 0.0 collective-permute-done.6.got
  16.0 0.8 %collective-permute-start.11 = (bf16[256,256]{1,0:T(8,128)(2,1)S(1)}, bf16[256,256]{1,0:T(8,128)(2,1)S(1)}, u32[]{:S(2)}, u32[]{:S(2)}) collective-permute-start(bf16[256,256]{1,0:T(8,128)(2,1)S(1)} %get-tuple-element.71), channel_id=1, source_target_pairs={{7,9},{23,25},{39,41},{55,57},{71,73},{87,89},{103,105},{119,121},... | collective-permute-start | bytes 393224 | tf_op jit(solution)/shard_map/ppermute | solution.py:301
  16.9 0.7 %collective-permute-start.10 = (bf16[256,256]{1,0:T(8,128)(2,1)S(1)}, bf16[256,256]{1,0:T(8,128)(2,1)S(1)}, u32[]{:S(2)}, u32[]{:S(2)}) collective-permute-start(bf16[256,256]{1,0:T(8,128)(2,1)S(1)} %get-tuple-element.71), channel_id=1, source_target_pairs={{7,11},{23,27},{39,43},{55,59},{71,75},{87,91},{103,107},{119,123}... | collective-permute-start | bytes 393224 | tf_op jit(solution)/shard_map/ppermute | solution.py:301
  17.6 0.0 collective-permute-done.8.got.early5.got5
  17.6 0.0 collective-permute-done.11.got
  17.7 0.7 %collective-permute-start.12 = (bf16[256,256]{1,0:T(8,128)(2,1)S(1)}, bf16[256,256]{1,0:T(8,128)(2,1)S(1)}, u32[]{:S(2)}, u32[]{:S(2)}) collective-permute-start(bf16[256,256]{1,0:T(8,128)(2,1)S(1)} %get-tuple-element.75), channel_id=1, source_target_pairs={{9,11},{11,13},{25,27},{27,29},{41,43},{43,45},{57,59},{59,61},{73... | collective-permute-start | bytes 393224 | tf_op jit(solution)/shard_map/ppermute | solution.py:301
  18.4 0.7 %collective-permute-start.9 = (bf16[256,256]{1,0:T(8,128)(2,1)S(1)}, bf16[256,256]{1,0:T(8,128)(2,1)S(1)}, u32[]{:S(2)}, u32[]{:S(2)}) collective-permute-start(bf16[256,256]{1,0:T(8,128)(2,1)S(1)} %get-tuple-element.70.mine), channel_id=1, source_target_pairs={{7,11},{11,15},{23,27},{27,31},{39,43},{43,47},{55,59},{59,63},{71... | collective-permute-start | bytes 393224 | tf_op jit(solution)/shard_map/ppermute | solution.py:301
  19.0 0.0 collective-permute-done.10.upper
  19.1 0.0 collective-permute-done.9.got.upper
  19.2 0.7 %collective-permute-start.13 = (bf16[256,256]{1,0:T(8,128)(2,1)S(1)}, bf16[256,256]{1,0:T(8,128)(2,1)S(1)}, u32[]{:S(2)}, u32[]{:S(2)}) collective-permute-start(bf16[256,256]{1,0:T(8,128)(2,1)S(1)} %get-tuple-element.79.mine), channel_id=1, source_target_pairs={{11,13},{7,9},{13,15},{27,29},{23,25},{29,31},{43,45},{39,41},{45,... | collective-permute-start | bytes 393224 | tf_op jit(solution)/shard_map/ppermute | solution.py:301
  19.8 0.7 %collective-permute-start.16 = (bf16[256,256]{1,0:T(8,128)(2,1)S(1)}, bf16[256,256]{1,0:T(8,128)(2,1)S(1)}, u32[]{:S(2)}, u32[]{:S(2)}) collective-permute-start(bf16[256,256]{1,0:T(8,128)(2,1)S(1)} %get-tuple-element.79.mine), channel_id=1, source_target_pairs={{11,15},{3,2},{5,4},{7,8},{27,31},{19,18},{21,20},{23,24},{43,47},... | collective-permute-start | bytes 393224 | tf_op jit(solution)/shard_map/ppermute | solution.py:301
  20.6 0.7 %collective-permute-start.15 = (bf16[256,256]{1,0:T(8,128)(2,1)S(1)}, bf16[256,256]{1,0:T(8,128)(2,1)S(1)}, u32[]{:S(2)}, u32[]{:S(2)}) collective-permute-start(bf16[256,256]{1,0:T(8,128)(2,1)S(1)} %get-tuple-element.81), channel_id=1, source_target_pairs={{13,15},{9,11},{29,31},{25,27},{45,47},{41,43},{61,63},{57,59},{77... | collective-permute-start | bytes 393224 | tf_op jit(solution)/shard_map/ppermute | solution.py:301
  21.2 1.3 %collective-permute-start.14 = (bf16[256,256]{1,0:T(8,128)(2,1)S(1)}, bf16[256,256]{1,0:T(8,128)(2,1)S(1)}, u32[]{:S(2)}, u32[]{:S(2)}) collective-permute-start(bf16[256,256]{1,0:T(8,128)(2,1)S(1)} %get-tuple-element.81), channel_id=1, source_target_pairs={{13,14},{9,10},{11,12},{7,6},{29,30},{25,26},{27,28},{23,22},{45,4... | collective-permute-start | bytes 393224 | tf_op jit(solution)/shard_map/ppermute | solution.py:301
  22.6 23.4 %collective-permute-done.14.got8b = bf16[256,256]{1,0:T(8,128)(2,1)S(1)} collective-permute-done((bf16[256,256]{1,0:T(8,128)(2,1)S(1)}, bf16[256,256]{1,0:T(8,128)(2,1)S(1)}, u32[]{:S(2)}, u32[]{:S(2)}) %collective-permute-start.14) | collective-permute-done | bytes 131104 | tf_op jit(solution)/shard_map/ppermute | solution.py:301
  46.0 2.3 %last_sweep.1 = f32[4,256,256]{2,1,0:T(8,128)} custom-call(f32[256,256]{1,0:T(8,128)S(1)} %get-tuple-element.49._.start, bf16[256,256]{1,0:T(8,128)(2,1)S(1)} %collective-permute-done.14.got8b, bf16[256,256]{1,0:T(8,128)(2,1)S(1)} %collective-permute-done.15.got8, bf16[256,256]{1,0:T(8,128)(2,1)S(1)} %collective-permute-done.5.got.early3.got3, ...), custom_call_target="tpu_custom_call" | custom-call | flops 1207959552 | bytes 1048576 | tf_op jit(solution)/shard_map/last_sweep/pallas_call | solution.py:58
  (21 shorter events, 0.3 us)
Async XLA Ops:
  0.1 7.9 %collective-permute-start = (bf16[256,256]{1,0:T(8,128)(2,1)S(1)}, bf16[256,256]{1,0:T(8,128)(2,1)S(1)}, u32[]{:S(2)}, u32[]{:S(2)}) collective-permute-start(bf16[256,256]{1,0:T(8,128)(2,1)S(1)} %get-tuple-element.44), channel_id=1, source_target_pairs={{1,2},{3,4},{5,6},{7,8},{9,10},{11,12},{13,14},{17,18},{19,20},{21... | collective-permute-start | bytes 393224 | tf_op jit(solution)/shard_map/ppermute | solution.py:301
  5.0 3.0 %collective-permute-start.1 = (bf16[256,256]{1,0:T(8,128)(2,1)S(1)}, bf16[256,256]{1,0:T(8,128)(2,1)S(1)}, u32[]{:S(2)}, u32[]{:S(2)}) collective-permute-start(bf16[256,256]{1,0:T(8,128)(2,1)S(1)} %get-tuple-element.50), channel_id=1, source_target_pairs={{0,1},{2,3},{4,5},{6,7},{8,9},{10,11},{12,13},{14,15},{16,17},{18,... | collective-permute-start | bytes 393224 | tf_op jit(solution)/shard_map/ppermute | solution.py:301
  6.3 6.5 %collective-permute-start.3 = (bf16[256,2304]{1,0:T(8,128)(2,1)S(1)}, bf16[256,2304]{1,0:T(8,128)(2,1)S(1)}, u32[]{:S(2)}, u32[]{:S(2)}) collective-permute-start(bf16[256,2304]{1,0:T(8,128)(2,1)S(1)} %get-tuple-element.52.own_w), channel_id=1, source_target_pairs={{0,1},{2,3},{4,5},{6,7},{8,9},{10,11},{12,13},{14,15},{16,17},{18,... | collective-permute-start | bytes 3538952 | tf_op jit(solution)/shard_map/ppermute | solution.py:301
  8.0 4.8 %collective-permute-start.5 = (bf16[256,256]{1,0:T(8,128)(2,1)S(1)}, bf16[256,256]{1,0:T(8,128)(2,1)S(1)}, u32[]{:S(2)}, u32[]{:S(2)}) collective-permute-start(bf16[256,256]{1,0:T(8,128)(2,1)S(1)} %get-tuple-element.57), channel_id=1, source_target_pairs={{1,3},{17,19},{33,35},{49,51},{65,67},{81,83},{97,99},{113,115},{1... | collective-permute-start | bytes 393224 | tf_op jit(solution)/shard_map/ppermute | solution.py:301
  10.5 4.1 %collective-permute-start.4 = (f32[256,256]{1,0:T(8,128)S(1)}, f32[256,256]{1,0:T(8,128)S(1)}, u32[]{:S(2)}, u32[]{:S(2)}) collective-permute-start(f32[256,256]{1,0:T(8,128)S(1)} %get-tuple-element.56), channel_id=1, source_target_pairs={{4,5},{8,9},{20,21},{24,25},{36,37},{40,41},{52,53},{56,57},{68,69... | collective-permute-start | bytes 786440 | tf_op jit(solution)/shard_map/ppermute | solution.py:301
  11.2 2.7 %collective-permute-start.2 = (f32[256,256]{1,0:T(8,128)S(1)}, f32[256,256]{1,0:T(8,128)S(1)}, u32[]{:S(2)}, u32[]{:S(2)}) collective-permute-start(f32[256,256]{1,0:T(8,128)S(1)} %get-tuple-element.55.rhs), channel_id=1, source_target_pairs={{0,1},{2,3},{4,5},{6,7},{8,9},{10,11},{12,13},{14,15},{16,17},{18,... | collective-permute-start | bytes 786440 | tf_op jit(solution)/shard_map/ppermute | solution.py:301
  13.9 1.4 %collective-permute-start.7 = (bf16[256,256]{1,0:T(8,128)(2,1)S(1)}, bf16[256,256]{1,0:T(8,128)(2,1)S(1)}, u32[]{:S(2)}, u32[]{:S(2)}) collective-permute-start(bf16[256,256]{1,0:T(8,128)(2,1)S(1)} %get-tuple-element.63), channel_id=1, source_target_pairs={{3,5},{19,21},{35,37},{51,53},{67,69},{83,85},{99,101},{115,117},{... | collective-permute-start | bytes 393224 | tf_op jit(solution)/shard_map/ppermute | solution.py:301
  14.6 1.4 %collective-permute-start.6 = (bf16[256,256]{1,0:T(8,128)(2,1)S(1)}, bf16[256,256]{1,0:T(8,128)(2,1)S(1)}, u32[]{:S(2)}, u32[]{:S(2)}) collective-permute-start(bf16[256,256]{1,0:T(8,128)(2,1)S(1)} %get-tuple-element.62), channel_id=1, source_target_pairs={{5,7},{9,11},{21,23},{25,27},{37,39},{41,43},{53,55},{57,59},{69,7... | collective-permute-start | bytes 393224 | tf_op jit(solution)/shard_map/ppermute | solution.py:301
  15.3 2.3 %collective-permute-start.8 = (bf16[256,256]{1,0:T(8,128)(2,1)S(1)}, bf16[256,256]{1,0:T(8,128)(2,1)S(1)}, u32[]{:S(2)}, u32[]{:S(2)}) collective-permute-start(bf16[256,256]{1,0:T(8,128)(2,1)S(1)} %get-tuple-element.68), channel_id=1, source_target_pairs={{5,7},{21,23},{37,39},{53,55},{69,71},{85,87},{101,103},{117,119},... | collective-permute-start | bytes 393224 | tf_op jit(solution)/shard_map/ppermute | solution.py:301
  16.0 1.6 %collective-permute-start.11 = (bf16[256,256]{1,0:T(8,128)(2,1)S(1)}, bf16[256,256]{1,0:T(8,128)(2,1)S(1)}, u32[]{:S(2)}, u32[]{:S(2)}) collective-permute-start(bf16[256,256]{1,0:T(8,128)(2,1)S(1)} %get-tuple-element.71), channel_id=1, source_target_pairs={{7,9},{23,25},{39,41},{55,57},{71,73},{87,89},{103,105},{119,121},... | collective-permute-start | bytes 393224 | tf_op jit(solution)/shard_map/ppermute | solution.py:301
  16.9 2.1 %collective-permute-start.10 = (bf16[256,256]{1,0:T(8,128)(2,1)S(1)}, bf16[256,256]{1,0:T(8,128)(2,1)S(1)}, u32[]{:S(2)}, u32[]{:S(2)}) collective-permute-start(bf16[256,256]{1,0:T(8,128)(2,1)S(1)} %get-tuple-element.71), channel_id=1, source_target_pairs={{7,11},{23,27},{39,43},{55,59},{71,75},{87,91},{103,107},{119,123}... | collective-permute-start | bytes 393224 | tf_op jit(solution)/shard_map/ppermute | solution.py:301
  17.7 1.4 %collective-permute-start.12 = (bf16[256,256]{1,0:T(8,128)(2,1)S(1)}, bf16[256,256]{1,0:T(8,128)(2,1)S(1)}, u32[]{:S(2)}, u32[]{:S(2)}) collective-permute-start(bf16[256,256]{1,0:T(8,128)(2,1)S(1)} %get-tuple-element.75), channel_id=1, source_target_pairs={{9,11},{11,13},{25,27},{27,29},{41,43},{43,45},{57,59},{59,61},{73... | collective-permute-start | bytes 393224 | tf_op jit(solution)/shard_map/ppermute | solution.py:301
  18.4 0.7 %collective-permute-start.9 = (bf16[256,256]{1,0:T(8,128)(2,1)S(1)}, bf16[256,256]{1,0:T(8,128)(2,1)S(1)}, u32[]{:S(2)}, u32[]{:S(2)}) collective-permute-start(bf16[256,256]{1,0:T(8,128)(2,1)S(1)} %get-tuple-element.70.mine), channel_id=1, source_target_pairs={{7,11},{11,15},{23,27},{27,31},{39,43},{43,47},{55,59},{59,63},{71... | collective-permute-start | bytes 393224 | tf_op jit(solution)/shard_map/ppermute | solution.py:301
  19.2 1.4 %collective-permute-start.13 = (bf16[256,256]{1,0:T(8,128)(2,1)S(1)}, bf16[256,256]{1,0:T(8,128)(2,1)S(1)}, u32[]{:S(2)}, u32[]{:S(2)}) collective-permute-start(bf16[256,256]{1,0:T(8,128)(2,1)S(1)} %get-tuple-element.79.mine), channel_id=1, source_target_pairs={{11,13},{7,9},{13,15},{27,29},{23,25},{29,31},{43,45},{39,41},{45,... | collective-permute-start | bytes 393224 | tf_op jit(solution)/shard_map/ppermute | solution.py:301
  19.8 2.7 %collective-permute-start.16 = (bf16[256,256]{1,0:T(8,128)(2,1)S(1)}, bf16[256,256]{1,0:T(8,128)(2,1)S(1)}, u32[]{:S(2)}, u32[]{:S(2)}) collective-permute-start(bf16[256,256]{1,0:T(8,128)(2,1)S(1)} %get-tuple-element.79.mine), channel_id=1, source_target_pairs={{11,15},{3,2},{5,4},{7,8},{27,31},{19,18},{21,20},{23,24},{43,47},... | collective-permute-start | bytes 393224 | tf_op jit(solution)/shard_map/ppermute | solution.py:301
  20.6 2.0 %collective-permute-start.15 = (bf16[256,256]{1,0:T(8,128)(2,1)S(1)}, bf16[256,256]{1,0:T(8,128)(2,1)S(1)}, u32[]{:S(2)}, u32[]{:S(2)}) collective-permute-start(bf16[256,256]{1,0:T(8,128)(2,1)S(1)} %get-tuple-element.81), channel_id=1, source_target_pairs={{13,15},{9,11},{29,31},{25,27},{45,47},{41,43},{61,63},{57,59},{77... | collective-permute-start | bytes 393224 | tf_op jit(solution)/shard_map/ppermute | solution.py:301
  21.2 24.8 %collective-permute-start.14 = (bf16[256,256]{1,0:T(8,128)(2,1)S(1)}, bf16[256,256]{1,0:T(8,128)(2,1)S(1)}, u32[]{:S(2)}, u32[]{:S(2)}) collective-permute-start(bf16[256,256]{1,0:T(8,128)(2,1)S(1)} %get-tuple-element.81), channel_id=1, source_target_pairs={{13,14},{9,10},{11,12},{7,6},{29,30},{25,26},{27,28},{23,22},{45,4... | collective-permute-start | bytes 393224 | tf_op jit(solution)/shard_map/ppermute | solution.py:301

commit v2 on v1

--- a/solution.py
+++ b/solution.py
@@ -77,12 +77,14 @@
     return lax.axis_index("layer")
 
 
-def first_sweep(parity, *refs):
+def first_sweep(first, *refs):
     inputs, guess, weights = refs[:3]
     cpoint, own_w, later_w, start, raw, sems = refs[-6:]
     me = place()
 
-    @pl.when(me % 2 == parity)
+    early = (me % 2 == 1) | (me == 0)
+
+    @pl.when(early if first else jnp.logical_not(early))
     def _():
         source = [pltpu.make_async_copy(weights.at[0], own_w, sems.at[1])]
         for i in range(COARSEN - 1):
@@ -112,11 +114,11 @@
             state = state + 0.25 * conv_tanh(state, own_w if i == 0 else later_w[i - 1])
         cpoint[...] = state.astype(BF16)
 
-        @pl.when(me == 1)
-        def _():
-            begin.start()
-            begin.wait()
-            start[...] = raw[...].T
+    if not first:
+
+        @pl.when(me == 0)
+        def _():
+            cpoint[...] = refs[6][...]
 
 
 def sweep(state, own_w, later_w, rhs):
@@ -134,13 +136,28 @@
         out[...] = sweep(left_odd[...].astype(F32), own_w, later_w, rhs).astype(BF16)
 
 
-def second_sweep(left_odd, left_even, own_w, later_w, start, _, rhs, first):
+def second_sweep_even(left_even, own_w, later_w, inputs, _, __, rhs, first, start, solved, raw, sem):
     me = place()
 
-    @pl.when(me != 1)
-    def _():
-        left = jnp.where(me % 2 == 0, left_even[...], left_odd[...]).astype(F32)
-        first[...] = sweep(jnp.where(me == 0, start[...], left), own_w, later_w, rhs)
+    @pl.when(me % 2 == 0)
+    def _():
+        left = jnp.where(me == 0, start[...], left_even[...].astype(F32))
+        first[...] = sweep(left, own_w, later_w, rhs)
+
+    @pl.when(me == 1)
+    def _():
+        copy = pltpu.make_async_copy(inputs, raw, sem)
+        copy.start()
+        copy.wait()
+        start[...] = raw[...].T
+
+
+def second_sweep_odd(left_odd, own_w, later_w, _, __, rhs, solved):
+    me = place()
+
+    @pl.when((me % 2 == 1) & (me > 1))
+    def _():
+        sweep(left_odd[...].astype(F32), own_w, later_w, rhs)
 
 
 def in_order(*refs):
@@ -253,7 +270,7 @@
 
 def last_sweep(
     start, got8b, got8, got3, got4, got5, got7, got7b,
-    even_rhs, rhs, even_w, own_w, later_w, solved, states, left, ready, sems,
+    even_rhs, rhs, even_w, own_w, rhs_of_even, later_w, solved, states, left, ready, sems,
 ):
     me = place()
     sources = (
@@ -285,7 +302,8 @@
 
     state = left[...]
     term = conv_tanh(state, own_w)
-    end = jnp.where(me % 4 == 3, solved[...], state + term + rhs[...])
+    own = jnp.where(me % 2 == 0, rhs_of_even[...], rhs[...])
+    end = jnp.where(me % 4 == 3, solved[...], state + term + own)
     copies = [store(COARSEN - 1, end)]
     state = state + 0.25 * term
     copies.append(store(0, state))
@@ -308,7 +326,7 @@
     scratch = [pltpu.VMEM((CHANS, CELLS), F32), pltpu.SemaphoreType.DMA((COARSEN + 1,))]
 
     from_odd, *kept = kernel_call(
-        functools.partial(first_sweep, 1),
+        functools.partial(first_sweep, True),
         [narrow, *held],
         [inputs, guess, weights],
         "first_sweep_odd",
@@ -318,9 +336,9 @@
     )
     left_even = send(from_odd, up_between)
     from_even, own_w, later_w, start = kernel_call(
-        functools.partial(first_sweep, 0),
+        functools.partial(first_sweep, False),
         [narrow, *held],
-        [inputs, guess, weights, *kept],
+        [inputs, guess, weights, *kept, from_odd],
         "first_sweep_even",
         4,
         hbm=(0, 1, 2),
@@ -341,16 +359,26 @@
         40,
     )
     got3 = send(c1, [(1, 3)])
-    rhs, first = kernel_call(
-        second_sweep,
+    rhs_of_even, first, start, solved = kernel_call(
+        second_sweep_even,
+        [wide, wide, wide, wide],
+        [left_even, own_w, later_w, inputs, start, solved],
+        "second_sweep_even",
+        4,
+        hbm=(3,),
+        scratch=[pltpu.VMEM((CHANS, CELLS), F32), pltpu.SemaphoreType.DMA(())],
+        aliases={4: 2, 5: 3},
+    )
+    first = send(first, [(4, 5), (8, 9)])
+    even_rhs = send(rhs_of_even, up_inside)
+    rhs, solved = kernel_call(
+        second_sweep_odd,
         [wide, wide],
-        [left_odd, left_even, own_w, later_w, start, rhs],
-        "second_sweep",
+        [left_odd, own_w, later_w, rhs, solved],
+        "second_sweep_odd",
         4,
-        aliases={5: 0},
-    )
-    first = send(first, [(4, 5), (8, 9)])
-    even_rhs = send(rhs, up_inside)
+        aliases={3: 0, 4: 1},
+    )
     both = [even_rhs, rhs, even_w, own_w]
 
     def chained(body, args, name, steps, out=narrow):
@@ -396,7 +424,7 @@
     return kernel_call(
         last_sweep,
         [jax.ShapeDtypeStruct((COARSEN, CHANS, CELLS), F32)],
-        [start, got8b, got8, got3, got4, got5, got7, got7b, *both, later_w, solved],
+        [start, got8b, got8, got3, got4, got5, got7, got7b, *both, rhs_of_even, later_w, solved],
         "last_sweep",
         4,
         scratch=[

time: 48.8 us -> 48.2 us (0.988)
  waiting for transfers between devices: 24.9 us -> 24.4 us
    pallas_call x19 -> x20, Pallas kernels: 8.09 us -> 8.31 us  [kernel_call(): pl.pallas_call(body, out_shape=outs, in_specs=[pl.BlockSpec(memory_space=...]
where the time goes in v2:
time: 48.2 us; the launch traced here: 47.8 us
  waiting for transfers between devices  24.4 us (51%)
  starting transfers between devices  14.6 us (30%)
  Pallas kernels  8.31 us (17%)
  between operations  0.53 us (1%)
    ppermute x17, waiting for transfers between devices, send(): return lax.ppermute(value, 'layer', pairs)  24.4 us
    ppermute x17, starting transfers between devices, send(): return lax.ppermute(value, 'layer', pairs)  14.6 us
    pallas_call x20, Pallas kernels, kernel_call(): pl.pallas_call(body, out_shape=outs, in_specs=[pl.BlockSpec(memory_space=...  8.31 us
  transfers between devices with their start and end apart: 17, of which 3 were waited for; matrix products, arithmetic and copies ran while one was open for 0% of the time, Pallas kernels for 12%

profile of v2, /device:TPU:248, one launch (start us, length us, event | category | flops | bytes accessed | tf_op | source)
XLA Modules:
  0.0 47.8 jit_solution(4879107005181519499)
XLA Ops:
  0.1 1.3 %collective-permute-start = (bf16[256,256]{1,0:T(8,128)(2,1)S(1)}, bf16[256,256]{1,0:T(8,128)(2,1)S(1)}, u32[]{:S(2)}, u32[]{:S(2)}) collective-permute-start(bf16[256,256]{1,0:T(8,128)(2,1)S(1)} %get-tuple-element.48.refs_6_), channel_id=1, source_target_pairs={{1,2},{3,4},{5,6},{7,8},{9,10},{11,12},{13,14},{17,18},{19,20},{21... | collective-permute-start | bytes 393224 | tf_op jit(solution)/shard_map/ppermute | solution.py:319
  1.4 3.7 %first_sweep_even.1 = (bf16[256,256]{1,0:T(8,128)(2,1)S(1)}, bf16[256,2304]{1,0:T(8,128)(2,1)S(1)}, bf16[3,256,2304]{2,1,0:T(8,128)(2,1)S(1)}, f32[256,256]{1,0:T(8,128)S(1)}) custom-call(f32[256,256]{1,0:T(8,128)} %inputs.1, f32[1,256,256]{2,1,0:T(8,128)} %refs_1_.3, ...), custom_call_target="tpu_custom_call", output_to_operand_aliasing={{1}: (3, {}), {2}: (4, {}), {3}: (5, {})} | custom-call | flops 1207959552 | bytes 1048576 | tf_op jit(solution)/shard_map/first_sweep_even/pallas_call | solution.py:58
  5.0 1.3 %collective-permute-start.1 = (bf16[256,256]{1,0:T(8,128)(2,1)S(1)}, bf16[256,256]{1,0:T(8,128)(2,1)S(1)}, u32[]{:S(2)}, u32[]{:S(2)}) collective-permute-start(bf16[256,256]{1,0:T(8,128)(2,1)S(1)} %get-tuple-element.57), channel_id=1, source_target_pairs={{0,1},{2,3},{4,5},{6,7},{8,9},{10,11},{12,13},{14,15},{16,17},{18,... | collective-permute-start | bytes 393224 | tf_op jit(solution)/shard_map/ppermute | solution.py:319
  6.3 1.4 %collective-permute-start.3 = (bf16[256,2304]{1,0:T(8,128)(2,1)S(1)}, bf16[256,2304]{1,0:T(8,128)(2,1)S(1)}, u32[]{:S(2)}, u32[]{:S(2)}) collective-permute-start(bf16[256,2304]{1,0:T(8,128)(2,1)S(1)} %get-tuple-element.54.own_w), channel_id=1, source_target_pairs={{0,1},{2,3},{4,5},{6,7},{8,9},{10,11},{12,13},{14,15},{16,17},{18,... | collective-permute-start | bytes 3538952 | tf_op jit(solution)/shard_map/ppermute | solution.py:319
  7.7 0.3 collective-permute-done.refs_0_
  8.0 0.0 collective-permute-done.1.left_odd
  8.0 0.7 %collective-permute-start.5 = (bf16[256,256]{1,0:T(8,128)(2,1)S(1)}, bf16[256,256]{1,0:T(8,128)(2,1)S(1)}, u32[]{:S(2)}, u32[]{:S(2)}) collective-permute-start(bf16[256,256]{1,0:T(8,128)(2,1)S(1)} %get-tuple-element.65), channel_id=1, source_target_pairs={{1,3},{17,19},{33,35},{49,51},{65,67},{81,83},{97,99},{113,115},{1... | collective-permute-start | bytes 393224 | tf_op jit(solution)/shard_map/ppermute | solution.py:319
  8.6 1.9 %second_sweep_even.1 = (f32[256,256]{1,0:T(8,128)S(1)}, f32[256,256]{1,0:T(8,128)S(1)}, f32[256,256]{1,0:T(8,128)S(1)}, f32[256,256]{1,0:T(8,128)S(1)}) custom-call(bf16[256,256]{1,0:T(8,128)(2,1)S(1)} %get-tuple-element.53.left_even, bf16[256,2304]{1,0:T(8,128)(2,1)S(1)} %get-tuple-element.54.own_w, ...), custom_call_target="tpu_custom_call", output_to_operand_aliasing={{2}: (4, {}), {3}: (5, {})} | custom-call | flops 1207959552 | bytes 1048576 | tf_op jit(solution)/shard_map/second_sweep_even/pallas_call | solution.py:58
  10.5 0.7 %collective-permute-start.4 = (f32[256,256]{1,0:T(8,128)S(1)}, f32[256,256]{1,0:T(8,128)S(1)}, u32[]{:S(2)}, u32[]{:S(2)}) collective-permute-start(f32[256,256]{1,0:T(8,128)S(1)} %get-tuple-element.64), channel_id=1, source_target_pairs={{4,5},{8,9},{20,21},{24,25},{36,37},{40,41},{52,53},{56,57},{68,69... | collective-permute-start | bytes 786440 | tf_op jit(solution)/shard_map/ppermute | solution.py:319
  11.2 1.3 %collective-permute-start.2 = (f32[256,256]{1,0:T(8,128)S(1)}, f32[256,256]{1,0:T(8,128)S(1)}, u32[]{:S(2)}, u32[]{:S(2)}) collective-permute-start(f32[256,256]{1,0:T(8,128)S(1)} %get-tuple-element.60.rhs_of_even), channel_id=1, source_target_pairs={{0,1},{2,3},{4,5},{6,7},{8,9},{10,11},{12,13},{14,15},{16,17},{18,... | collective-permute-start | bytes 786440 | tf_op jit(solution)/shard_map/ppermute | solution.py:319
  12.6 0.0 collective-permute-done.3.even_w
  12.6 1.1 %collective-permute-done.2.even_rhs = f32[256,256]{1,0:T(8,128)S(1)} collective-permute-done((f32[256,256]{1,0:T(8,128)S(1)}, f32[256,256]{1,0:T(8,128)S(1)}, u32[]{:S(2)}, u32[]{:S(2)}) %collective-permute-start.2) | collective-permute-done | bytes 262176 | tf_op jit(solution)/shard_map/ppermute | solution.py:319
  13.7 0.7 %collective-permute-start.7 = (bf16[256,256]{1,0:T(8,128)(2,1)S(1)}, bf16[256,256]{1,0:T(8,128)(2,1)S(1)}, u32[]{:S(2)}, u32[]{:S(2)}) collective-permute-start(bf16[256,256]{1,0:T(8,128)(2,1)S(1)} %get-tuple-element.71), channel_id=1, source_target_pairs={{3,5},{19,21},{35,37},{51,53},{67,69},{83,85},{99,101},{115,117},{... | collective-permute-start | bytes 393224 | tf_op jit(solution)/shard_map/ppermute | solution.py:319
  14.3 0.0 collective-permute-done.4.first
  14.4 0.7 %collective-permute-start.6 = (bf16[256,256]{1,0:T(8,128)(2,1)S(1)}, bf16[256,256]{1,0:T(8,128)(2,1)S(1)}, u32[]{:S(2)}, u32[]{:S(2)}) collective-permute-start(bf16[256,256]{1,0:T(8,128)(2,1)S(1)} %get-tuple-element.70), channel_id=1, source_target_pairs={{5,7},{9,11},{21,23},{25,27},{37,39},{41,43},{53,55},{57,59},{69,7... | collective-permute-start | bytes 393224 | tf_op jit(solution)/shard_map/ppermute | solution.py:319
  15.1 0.0 collective-permute-done.7.got.early4.got4
  15.1 0.2 again_lead.1
  15.3 0.7 %collective-permute-start.8 = (bf16[256,256]{1,0:T(8,128)(2,1)S(1)}, bf16[256,256]{1,0:T(8,128)(2,1)S(1)}, u32[]{:S(2)}, u32[]{:S(2)}) collective-permute-start(bf16[256,256]{1,0:T(8,128)(2,1)S(1)} %get-tuple-element.76), channel_id=1, source_target_pairs={{5,7},{21,23},{37,39},{53,55},{69,71},{85,87},{101,103},{117,119},... | collective-permute-start | bytes 393224 | tf_op jit(solution)/shard_map/ppermute | solution.py:319
  15.9 0.0 collective-permute-done.6.got
  16.0 0.7 %collective-permute-start.11 = (bf16[256,256]{1,0:T(8,128)(2,1)S(1)}, bf16[256,256]{1,0:T(8,128)(2,1)S(1)}, u32[]{:S(2)}, u32[]{:S(2)}) collective-permute-start(bf16[256,256]{1,0:T(8,128)(2,1)S(1)} %get-tuple-element.79), channel_id=1, source_target_pairs={{7,9},{23,25},{39,41},{55,57},{71,73},{87,89},{103,105},{119,121},... | collective-permute-start | bytes 393224 | tf_op jit(solution)/shard_map/ppermute | solution.py:319
  16.6 0.7 %collective-permute-start.10 = (bf16[256,256]{1,0:T(8,128)(2,1)S(1)}, bf16[256,256]{1,0:T(8,128)(2,1)S(1)}, u32[]{:S(2)}, u32[]{:S(2)}) collective-permute-start(bf16[256,256]{1,0:T(8,128)(2,1)S(1)} %get-tuple-element.79), channel_id=1, source_target_pairs={{7,11},{23,27},{39,43},{55,59},{71,75},{87,91},{103,107},{119,123}... | collective-permute-start | bytes 393224 | tf_op jit(solution)/shard_map/ppermute | solution.py:319
  17.4 0.0 collective-permute-done.11.got
  17.4 0.7 %collective-permute-start.12 = (bf16[256,256]{1,0:T(8,128)(2,1)S(1)}, bf16[256,256]{1,0:T(8,128)(2,1)S(1)}, u32[]{:S(2)}, u32[]{:S(2)}) collective-permute-start(bf16[256,256]{1,0:T(8,128)(2,1)S(1)} %get-tuple-element.83), channel_id=1, source_target_pairs={{9,11},{11,13},{25,27},{27,29},{41,43},{43,45},{57,59},{59,61},{73... | collective-permute-start | bytes 393224 | tf_op jit(solution)/shard_map/ppermute | solution.py:319
  18.1 0.7 %collective-permute-start.9 = (bf16[256,256]{1,0:T(8,128)(2,1)S(1)}, bf16[256,256]{1,0:T(8,128)(2,1)S(1)}, u32[]{:S(2)}, u32[]{:S(2)}) collective-permute-start(bf16[256,256]{1,0:T(8,128)(2,1)S(1)} %get-tuple-element.78.mine), channel_id=1, source_target_pairs={{7,11},{11,15},{23,27},{27,31},{39,43},{43,47},{55,59},{59,63},{71... | collective-permute-start | bytes 393224 | tf_op jit(solution)/shard_map/ppermute | solution.py:319
  18.8 0.0 collective-permute-done.10.upper
  18.8 0.0 collective-permute-done.9.got.upper
  18.9 0.7 %collective-permute-start.13 = (bf16[256,256]{1,0:T(8,128)(2,1)S(1)}, bf16[256,256]{1,0:T(8,128)(2,1)S(1)}, u32[]{:S(2)}, u32[]{:S(2)}) collective-permute-start(bf16[256,256]{1,0:T(8,128)(2,1)S(1)} %get-tuple-element.87.mine), channel_id=1, source_target_pairs={{11,13},{7,9},{13,15},{27,29},{23,25},{29,31},{43,45},{39,41},{45,... | collective-permute-start | bytes 393224 | tf_op jit(solution)/shard_map/ppermute | solution.py:319
  19.6 0.7 %collective-permute-start.16 = (bf16[256,256]{1,0:T(8,128)(2,1)S(1)}, bf16[256,256]{1,0:T(8,128)(2,1)S(1)}, u32[]{:S(2)}, u32[]{:S(2)}) collective-permute-start(bf16[256,256]{1,0:T(8,128)(2,1)S(1)} %get-tuple-element.87.mine), channel_id=1, source_target_pairs={{11,15},{3,2},{5,4},{7,8},{27,31},{19,18},{21,20},{23,24},{43,47},... | collective-permute-start | bytes 393224 | tf_op jit(solution)/shard_map/ppermute | solution.py:319
  20.3 0.7 %collective-permute-start.15 = (bf16[256,256]{1,0:T(8,128)(2,1)S(1)}, bf16[256,256]{1,0:T(8,128)(2,1)S(1)}, u32[]{:S(2)}, u32[]{:S(2)}) collective-permute-start(bf16[256,256]{1,0:T(8,128)(2,1)S(1)} %get-tuple-element.89), channel_id=1, source_target_pairs={{13,15},{9,11},{29,31},{25,27},{45,47},{41,43},{61,63},{57,59},{77... | collective-permute-start | bytes 393224 | tf_op jit(solution)/shard_map/ppermute | solution.py:319
  21.0 1.3 %collective-permute-start.14 = (bf16[256,256]{1,0:T(8,128)(2,1)S(1)}, bf16[256,256]{1,0:T(8,128)(2,1)S(1)}, u32[]{:S(2)}, u32[]{:S(2)}) collective-permute-start(bf16[256,256]{1,0:T(8,128)(2,1)S(1)} %get-tuple-element.89), channel_id=1, source_target_pairs={{13,14},{9,10},{11,12},{7,6},{29,30},{25,26},{27,28},{23,22},{45,4... | collective-permute-start | bytes 393224 | tf_op jit(solution)/shard_map/ppermute | solution.py:319
  22.3 23.0 %collective-permute-done.14.got8b = bf16[256,256]{1,0:T(8,128)(2,1)S(1)} collective-permute-done((bf16[256,256]{1,0:T(8,128)(2,1)S(1)}, bf16[256,256]{1,0:T(8,128)(2,1)S(1)}, u32[]{:S(2)}, u32[]{:S(2)}) %collective-permute-start.14) | collective-permute-done | bytes 131104 | tf_op jit(solution)/shard_map/ppermute | solution.py:319
  45.4 2.3 %last_sweep.1 = f32[4,256,256]{2,1,0:T(8,128)} custom-call(f32[256,256]{1,0:T(8,128)S(1)} %get-tuple-element.59.start, bf16[256,256]{1,0:T(8,128)(2,1)S(1)} %collective-permute-done.14.got8b, bf16[256,256]{1,0:T(8,128)(2,1)S(1)} %collective-permute-done.15.got8, bf16[256,256]{1,0:T(8,128)(2,1)S(1)} %collective-permute-done.5.got.early3.got3, ...), custom_call_target="tpu_custom_call" | custom-call | flops 1207959552 | bytes 1048576 | tf_op jit(solution)/shard_map/last_sweep/pallas_call | solution.py:58
  (22 shorter events, 0.3 us)
Async XLA Ops:
  0.1 7.9 %collective-permute-start = (bf16[256,256]{1,0:T(8,128)(2,1)S(1)}, bf16[256,256]{1,0:T(8,128)(2,1)S(1)}, u32[]{:S(2)}, u32[]{:S(2)}) collective-permute-start(bf16[256,256]{1,0:T(8,128)(2,1)S(1)} %get-tuple-element.48.refs_6_), channel_id=1, source_target_pairs={{1,2},{3,4},{5,6},{7,8},{9,10},{11,12},{13,14},{17,18},{19,20},{21... | collective-permute-start | bytes 393224 | tf_op jit(solution)/shard_map/ppermute | solution.py:319
  5.0 3.0 %collective-permute-start.1 = (bf16[256,256]{1,0:T(8,128)(2,1)S(1)}, bf16[256,256]{1,0:T(8,128)(2,1)S(1)}, u32[]{:S(2)}, u32[]{:S(2)}) collective-permute-start(bf16[256,256]{1,0:T(8,128)(2,1)S(1)} %get-tuple-element.57), channel_id=1, source_target_pairs={{0,1},{2,3},{4,5},{6,7},{8,9},{10,11},{12,13},{14,15},{16,17},{18,... | collective-permute-start | bytes 393224 | tf_op jit(solution)/shard_map/ppermute | solution.py:319
  6.3 6.3 %collective-permute-start.3 = (bf16[256,2304]{1,0:T(8,128)(2,1)S(1)}, bf16[256,2304]{1,0:T(8,128)(2,1)S(1)}, u32[]{:S(2)}, u32[]{:S(2)}) collective-permute-start(bf16[256,2304]{1,0:T(8,128)(2,1)S(1)} %get-tuple-element.54.own_w), channel_id=1, source_target_pairs={{0,1},{2,3},{4,5},{6,7},{8,9},{10,11},{12,13},{14,15},{16,17},{18,... | collective-permute-start | bytes 3538952 | tf_op jit(solution)/shard_map/ppermute | solution.py:319
  8.0 4.6 %collective-permute-start.5 = (bf16[256,256]{1,0:T(8,128)(2,1)S(1)}, bf16[256,256]{1,0:T(8,128)(2,1)S(1)}, u32[]{:S(2)}, u32[]{:S(2)}) collective-permute-start(bf16[256,256]{1,0:T(8,128)(2,1)S(1)} %get-tuple-element.65), channel_id=1, source_target_pairs={{1,3},{17,19},{33,35},{49,51},{65,67},{81,83},{97,99},{113,115},{1... | collective-permute-start | bytes 393224 | tf_op jit(solution)/shard_map/ppermute | solution.py:319
  10.5 3.8 %collective-permute-start.4 = (f32[256,256]{1,0:T(8,128)S(1)}, f32[256,256]{1,0:T(8,128)S(1)}, u32[]{:S(2)}, u32[]{:S(2)}) collective-permute-start(f32[256,256]{1,0:T(8,128)S(1)} %get-tuple-element.64), channel_id=1, source_target_pairs={{4,5},{8,9},{20,21},{24,25},{36,37},{40,41},{52,53},{56,57},{68,69... | collective-permute-start | bytes 786440 | tf_op jit(solution)/shard_map/ppermute | solution.py:319
  11.2 2.4 %collective-permute-start.2 = (f32[256,256]{1,0:T(8,128)S(1)}, f32[256,256]{1,0:T(8,128)S(1)}, u32[]{:S(2)}, u32[]{:S(2)}) collective-permute-start(f32[256,256]{1,0:T(8,128)S(1)} %get-tuple-element.60.rhs_of_even), channel_id=1, source_target_pairs={{0,1},{2,3},{4,5},{6,7},{8,9},{10,11},{12,13},{14,15},{16,17},{18,... | collective-permute-start | bytes 786440 | tf_op jit(solution)/shard_map/ppermute | solution.py:319
  13.7 1.4 %collective-permute-start.7 = (bf16[256,256]{1,0:T(8,128)(2,1)S(1)}, bf16[256,256]{1,0:T(8,128)(2,1)S(1)}, u32[]{:S(2)}, u32[]{:S(2)}) collective-permute-start(bf16[256,256]{1,0:T(8,128)(2,1)S(1)} %get-tuple-element.71), channel_id=1, source_target_pairs={{3,5},{19,21},{35,37},{51,53},{67,69},{83,85},{99,101},{115,117},{... | collective-permute-start | bytes 393224 | tf_op jit(solution)/shard_map/ppermute | solution.py:319
  14.4 1.6 %collective-permute-start.6 = (bf16[256,256]{1,0:T(8,128)(2,1)S(1)}, bf16[256,256]{1,0:T(8,128)(2,1)S(1)}, u32[]{:S(2)}, u32[]{:S(2)}) collective-permute-start(bf16[256,256]{1,0:T(8,128)(2,1)S(1)} %get-tuple-element.70), channel_id=1, source_target_pairs={{5,7},{9,11},{21,23},{25,27},{37,39},{41,43},{53,55},{57,59},{69,7... | collective-permute-start | bytes 393224 | tf_op jit(solution)/shard_map/ppermute | solution.py:319
  15.3 2.1 %collective-permute-start.8 = (bf16[256,256]{1,0:T(8,128)(2,1)S(1)}, bf16[256,256]{1,0:T(8,128)(2,1)S(1)}, u32[]{:S(2)}, u32[]{:S(2)}) collective-permute-start(bf16[256,256]{1,0:T(8,128)(2,1)S(1)} %get-tuple-element.76), channel_id=1, source_target_pairs={{5,7},{21,23},{37,39},{53,55},{69,71},{85,87},{101,103},{117,119},... | collective-permute-start | bytes 393224 | tf_op jit(solution)/shard_map/ppermute | solution.py:319
  16.0 1.4 %collective-permute-start.11 = (bf16[256,256]{1,0:T(8,128)(2,1)S(1)}, bf16[256,256]{1,0:T(8,128)(2,1)S(1)}, u32[]{:S(2)}, u32[]{:S(2)}) collective-permute-start(bf16[256,256]{1,0:T(8,128)(2,1)S(1)} %get-tuple-element.79), channel_id=1, source_target_pairs={{7,9},{23,25},{39,41},{55,57},{71,73},{87,89},{103,105},{119,121},... | collective-permute-start | bytes 393224 | tf_op jit(solution)/shard_map/ppermute | solution.py:319
  16.6 2.1 %collective-permute-start.10 = (bf16[256,256]{1,0:T(8,128)(2,1)S(1)}, bf16[256,256]{1,0:T(8,128)(2,1)S(1)}, u32[]{:S(2)}, u32[]{:S(2)}) collective-permute-start(bf16[256,256]{1,0:T(8,128)(2,1)S(1)} %get-tuple-element.79), channel_id=1, source_target_pairs={{7,11},{23,27},{39,43},{55,59},{71,75},{87,91},{103,107},{119,123}... | collective-permute-start | bytes 393224 | tf_op jit(solution)/shard_map/ppermute | solution.py:319
  17.4 1.4 %collective-permute-start.12 = (bf16[256,256]{1,0:T(8,128)(2,1)S(1)}, bf16[256,256]{1,0:T(8,128)(2,1)S(1)}, u32[]{:S(2)}, u32[]{:S(2)}) collective-permute-start(bf16[256,256]{1,0:T(8,128)(2,1)S(1)} %get-tuple-element.83), channel_id=1, source_target_pairs={{9,11},{11,13},{25,27},{27,29},{41,43},{43,45},{57,59},{59,61},{73... | collective-permute-start | bytes 393224 | tf_op jit(solution)/shard_map/ppermute | solution.py:319
  18.1 0.7 %collective-permute-start.9 = (bf16[256,256]{1,0:T(8,128)(2,1)S(1)}, bf16[256,256]{1,0:T(8,128)(2,1)S(1)}, u32[]{:S(2)}, u32[]{:S(2)}) collective-permute-start(bf16[256,256]{1,0:T(8,128)(2,1)S(1)} %get-tuple-element.78.mine), channel_id=1, source_target_pairs={{7,11},{11,15},{23,27},{27,31},{39,43},{43,47},{55,59},{59,63},{71... | collective-permute-start | bytes 393224 | tf_op jit(solution)/shard_map/ppermute | solution.py:319
  18.9 1.4 %collective-permute-start.13 = (bf16[256,256]{1,0:T(8,128)(2,1)S(1)}, bf16[256,256]{1,0:T(8,128)(2,1)S(1)}, u32[]{:S(2)}, u32[]{:S(2)}) collective-permute-start(bf16[256,256]{1,0:T(8,128)(2,1)S(1)} %get-tuple-element.87.mine), channel_id=1, source_target_pairs={{11,13},{7,9},{13,15},{27,29},{23,25},{29,31},{43,45},{39,41},{45,... | collective-permute-start | bytes 393224 | tf_op jit(solution)/shard_map/ppermute | solution.py:319
  19.6 2.7 %collective-permute-start.16 = (bf16[256,256]{1,0:T(8,128)(2,1)S(1)}, bf16[256,256]{1,0:T(8,128)(2,1)S(1)}, u32[]{:S(2)}, u32[]{:S(2)}) collective-permute-start(bf16[256,256]{1,0:T(8,128)(2,1)S(1)} %get-tuple-element.87.mine), channel_id=1, source_target_pairs={{11,15},{3,2},{5,4},{7,8},{27,31},{19,18},{21,20},{23,24},{43,47},... | collective-permute-start | bytes 393224 | tf_op jit(solution)/shard_map/ppermute | solution.py:319
  20.3 2.0 %collective-permute-start.15 = (bf16[256,256]{1,0:T(8,128)(2,1)S(1)}, bf16[256,256]{1,0:T(8,128)(2,1)S(1)}, u32[]{:S(2)}, u32[]{:S(2)}) collective-permute-start(bf16[256,256]{1,0:T(8,128)(2,1)S(1)} %get-tuple-element.89), channel_id=1, source_target_pairs={{13,15},{9,11},{29,31},{25,27},{45,47},{41,43},{61,63},{57,59},{77... | collective-permute-start | bytes 393224 | tf_op jit(solution)/shard_map/ppermute | solution.py:319
  21.0 24.4 %collective-permute-start.14 = (bf16[256,256]{1,0:T(8,128)(2,1)S(1)}, bf16[256,256]{1,0:T(8,128)(2,1)S(1)}, u32[]{:S(2)}, u32[]{:S(2)}) collective-permute-start(bf16[256,256]{1,0:T(8,128)(2,1)S(1)} %get-tuple-element.89), channel_id=1, source_target_pairs={{13,14},{9,10},{11,12},{7,6},{29,30},{25,26},{27,28},{23,22},{45,4... | collective-permute-start | bytes 393224 | tf_op jit(solution)/shard_map/ppermute | solution.py:319

commit v3 on v2

--- a/solution.py
+++ b/solution.py
@@ -222,6 +222,10 @@
         out[...] = upper[...]
 
 
+def again_rest(upper, even_rhs, rhs, even_w, own_w, got, _, __, out, solved, passed):
+    steps_or_copy(9, False, upper, even_rhs, rhs, even_w, own_w, got, _, out, solved)
+
+
 def coarse_base(upper, own_w, _, out, solved):
     @pl.when(place() == 11)
     def _():
@@ -369,14 +373,14 @@
         scratch=[pltpu.VMEM((CHANS, CELLS), F32), pltpu.SemaphoreType.DMA(())],
         aliases={4: 2, 5: 3},
     )
+    even_rhs = send(rhs_of_even, up_inside)
     first = send(first, [(4, 5), (8, 9)])
-    even_rhs = send(rhs_of_even, up_inside)
     rhs, solved = kernel_call(
         second_sweep_odd,
         [wide, wide],
         [left_odd, own_w, later_w, rhs, solved],
         "second_sweep_odd",
-        4,
+        0,
         aliases={3: 0, 4: 1},
     )
     both = [even_rhs, rhs, even_w, own_w]
@@ -391,27 +395,33 @@
     def pair(owners, keep, got, name):
         return chained(functools.partial(two_steps, owners, keep), [*both, got], name, 2)
 
-    part = chained(lead_half, [got3, even_w], "lead_first", 10, wide)
-    upper1 = chained(lead_rest, [rhs, own_w, even_rhs, part], "relax_lead", 1)
+    part = chained(lead_half, [got3, even_w], "lead_first", 7, wide)
+    upper1 = chained(lead_rest, [rhs, own_w, even_rhs, part], "relax_lead", 20)
     got4 = send(upper1, [(3, 5)])
     c5 = chained(functools.partial(one_step, (5, 9)), [first, rhs, own_w], "relax_first", 1)
-    got3_rest = send(c5, [(5, 7), (9, 11)])
+    got3_rest = send(c5, [(5, 7)])
+    got3_last = send(c5, [(9, 11)])
     c5_lead = pair((5,), False, got4, "again_lead")
     got5 = send(c5_lead, [(5, 7)])
     upper7 = pair((7,), False, got3_rest, "relax_rest")
     got4_rest = send(upper7, [(7, 9)])
-    upper_prev = send(upper7, [(7, 11)])
-    upper11 = pair((11,), False, got3_rest, "relax_last")
+    upper11 = pair((11,), False, got3_last, "relax_last")
     z2 = chained(
         functools.partial(steps_or_copy, 7, True), [upper11, *both, got5], "again_end_lead", 2
     )
     got6 = send(z2, [(7, 11), (11, 15)])
-    c9 = chained(
-        functools.partial(steps_or_copy, 9, False), [upper11, *both, got4_rest], "again_rest", 2
+    c9, solved, upper7 = kernel_call(
+        again_rest,
+        [narrow, wide, narrow],
+        [upper11, *both, got4_rest, solved, upper7],
+        "again_rest",
+        2,
+        aliases={6: 1, 7: 2},
     )
     got5_rest = send(c9, [(9, 11), (11, 13)])
+    upper_prev = send(upper7, [(7, 11)])
+    c13 = chained(again_end, [*both, got5_rest], "again_end_rest", 2)
     base = chained(coarse_base, [upper_prev, own_w], "coarse_base", 1, wide)
-    c13 = chained(again_end, [*both, got5_rest], "again_end_rest", 2)
     z3 = chained(lead_step, [got6, base, own_w, got3, got4, z2, c13], "coarse_lead", 1)
     got7 = send(z3, [(11, 13), (7, 9), (13, 15)])
     got7b = send(z3, [(11, 15), (3, 2), (5, 4), (7, 8)])

time: 48.2 us -> 49.9 us (1.035)
  waiting for transfers between devices: 24.4 us -> 25.4 us
  starting transfers between devices: 14.6 us -> 15.2 us
    ppermute x17 -> x18, waiting for transfers between devices: 24.4 us -> 25.4 us  [send(): return lax.ppermute(value, 'layer', pairs)]
    ppermute x17 -> x18, starting transfers between devices: 14.6 us -> 15.2 us  [send(): return lax.ppermute(value, 'layer', pairs)]
  transfers between devices with their start and end apart: 17 -> 18, of which waited for: 3 -> 3; matrix products, arithmetic and copies ran while one was open for 0% -> 0% of each run, Pallas kernels for 12% -> 12%
where the time goes in v3:
time: 49.9 us; the launch traced here: 49.5 us
  waiting for transfers between devices  25.4 us (51%)
  starting transfers between devices  15.2 us (30%)
  Pallas kernels  8.31 us (17%)
  between operations  0.54 us (1%)
    ppermute x18, waiting for transfers between devices, send(): return lax.ppermute(value, 'layer', pairs)  25.4 us
    ppermute x18, starting transfers between devices, send(): return lax.ppermute(value, 'layer', pairs)  15.2 us
    pallas_call x20, Pallas kernels, kernel_call(): pl.pallas_call(body, out_shape=outs, in_specs=[pl.BlockSpec(memory_space=...  8.31 us
  transfers between devices with their start and end apart: 18, of which 3 were waited for; matrix products, arithmetic and copies ran while one was open for 0% of the time, Pallas kernels for 12%

profile of v3, /device:TPU:248, one launch (start us, length us, event | category | flops | bytes accessed | tf_op | source)
XLA Modules:
  0.0 49.5 jit_solution(5078761126321052009)
XLA Ops:
  0.1 1.3 %collective-permute-start = (bf16[256,256]{1,0:T(8,128)(2,1)S(1)}, bf16[256,256]{1,0:T(8,128)(2,1)S(1)}, u32[]{:S(2)}, u32[]{:S(2)}) collective-permute-start(bf16[256,256]{1,0:T(8,128)(2,1)S(1)} %get-tuple-element.49.refs_6_), channel_id=1, source_target_pairs={{1,2},{3,4},{5,6},{7,8},{9,10},{11,12},{13,14},{17,18},{19,20},{21... | collective-permute-start | bytes 393224 | tf_op jit(solution)/shard_map/ppermute | solution.py:323
  1.4 3.7 %first_sweep_even.1 = (bf16[256,256]{1,0:T(8,128)(2,1)S(1)}, bf16[256,2304]{1,0:T(8,128)(2,1)S(1)}, bf16[3,256,2304]{2,1,0:T(8,128)(2,1)S(1)}, f32[256,256]{1,0:T(8,128)S(1)}) custom-call(f32[256,256]{1,0:T(8,128)} %inputs.1, f32[1,256,256]{2,1,0:T(8,128)} %refs_1_.3, ...), custom_call_target="tpu_custom_call", output_to_operand_aliasing={{1}: (3, {}), {2}: (4, {}), {3}: (5, {})} | custom-call | flops 1207959552 | bytes 1048576 | tf_op jit(solution)/shard_map/first_sweep_even/pallas_call | solution.py:58
  5.0 1.3 %collective-permute-start.1 = (bf16[256,256]{1,0:T(8,128)(2,1)S(1)}, bf16[256,256]{1,0:T(8,128)(2,1)S(1)}, u32[]{:S(2)}, u32[]{:S(2)}) collective-permute-start(bf16[256,256]{1,0:T(8,128)(2,1)S(1)} %get-tuple-element.58), channel_id=1, source_target_pairs={{0,1},{2,3},{4,5},{6,7},{8,9},{10,11},{12,13},{14,15},{16,17},{18,... | collective-permute-start | bytes 393224 | tf_op jit(solution)/shard_map/ppermute | solution.py:323
  6.3 1.4 %collective-permute-start.3 = (bf16[256,2304]{1,0:T(8,128)(2,1)S(1)}, bf16[256,2304]{1,0:T(8,128)(2,1)S(1)}, u32[]{:S(2)}, u32[]{:S(2)}) collective-permute-start(bf16[256,2304]{1,0:T(8,128)(2,1)S(1)} %get-tuple-element.55.own_w), channel_id=1, source_target_pairs={{0,1},{2,3},{4,5},{6,7},{8,9},{10,11},{12,13},{14,15},{16,17},{18,... | collective-permute-start | bytes 3538952 | tf_op jit(solution)/shard_map/ppermute | solution.py:323
  7.7 0.3 collective-permute-done.refs_0_
  8.0 0.0 collective-permute-done.1.left_odd
  8.0 0.7 %collective-permute-start.5 = (bf16[256,256]{1,0:T(8,128)(2,1)S(1)}, bf16[256,256]{1,0:T(8,128)(2,1)S(1)}, u32[]{:S(2)}, u32[]{:S(2)}) collective-permute-start(bf16[256,256]{1,0:T(8,128)(2,1)S(1)} %get-tuple-element.66), channel_id=1, source_target_pairs={{1,3},{17,19},{33,35},{49,51},{65,67},{81,83},{97,99},{113,115},{1... | collective-permute-start | bytes 393224 | tf_op jit(solution)/shard_map/ppermute | solution.py:323
  8.6 1.9 %second_sweep_even.1 = (f32[256,256]{1,0:T(8,128)S(1)}, f32[256,256]{1,0:T(8,128)S(1)}, f32[256,256]{1,0:T(8,128)S(1)}, f32[256,256]{1,0:T(8,128)S(1)}) custom-call(bf16[256,256]{1,0:T(8,128)(2,1)S(1)} %get-tuple-element.54.left_even, bf16[256,2304]{1,0:T(8,128)(2,1)S(1)} %get-tuple-element.55.own_w, ...), custom_call_target="tpu_custom_call", output_to_operand_aliasing={{2}: (4, {}), {3}: (5, {})} | custom-call | flops 1207959552 | bytes 1048576 | tf_op jit(solution)/shard_map/second_sweep_even/pallas_call | solution.py:58
  10.5 1.3 %collective-permute-start.2 = (f32[256,256]{1,0:T(8,128)S(1)}, f32[256,256]{1,0:T(8,128)S(1)}, u32[]{:S(2)}, u32[]{:S(2)}) collective-permute-start(f32[256,256]{1,0:T(8,128)S(1)} %get-tuple-element.61.rhs_of_even), channel_id=1, source_target_pairs={{0,1},{2,3},{4,5},{6,7},{8,9},{10,11},{12,13},{14,15},{16,17},{18,... | collective-permute-start | bytes 786440 | tf_op jit(solution)/shard_map/ppermute | solution.py:323
  11.9 0.7 %collective-permute-start.4 = (f32[256,256]{1,0:T(8,128)S(1)}, f32[256,256]{1,0:T(8,128)S(1)}, u32[]{:S(2)}, u32[]{:S(2)}) collective-permute-start(f32[256,256]{1,0:T(8,128)S(1)} %get-tuple-element.65), channel_id=1, source_target_pairs={{4,5},{8,9},{20,21},{24,25},{36,37},{40,41},{52,53},{56,57},{68,69... | collective-permute-start | bytes 786440 | tf_op jit(solution)/shard_map/ppermute | solution.py:323
  12.6 0.0 collective-permute-done.5.got.early3.got3
  12.6 0.4 collective-permute-done.2.even_rhs
  13.0 0.7 %collective-permute-start.8 = (bf16[256,256]{1,0:T(8,128)(2,1)S(1)}, bf16[256,256]{1,0:T(8,128)(2,1)S(1)}, u32[]{:S(2)}, u32[]{:S(2)}) collective-permute-start(bf16[256,256]{1,0:T(8,128)(2,1)S(1)} %get-tuple-element.72), channel_id=1, source_target_pairs={{3,5},{19,21},{35,37},{51,53},{67,69},{83,85},{99,101},{115,117},{... | collective-permute-start | bytes 393224 | tf_op jit(solution)/shard_map/ppermute | solution.py:323
  13.7 0.7 %collective-permute-start.7 = (bf16[256,256]{1,0:T(8,128)(2,1)S(1)}, bf16[256,256]{1,0:T(8,128)(2,1)S(1)}, u32[]{:S(2)}, u32[]{:S(2)}) collective-permute-start(bf16[256,256]{1,0:T(8,128)(2,1)S(1)} %get-tuple-element.71), channel_id=1, source_target_pairs={{5,7},{21,23},{37,39},{53,55},{69,71},{85,87},{101,103},{117,119},... | collective-permute-start | bytes 393224 | tf_op jit(solution)/shard_map/ppermute | solution.py:323
  14.4 0.7 %collective-permute-start.6 = (bf16[256,256]{1,0:T(8,128)(2,1)S(1)}, bf16[256,256]{1,0:T(8,128)(2,1)S(1)}, u32[]{:S(2)}, u32[]{:S(2)}) collective-permute-start(bf16[256,256]{1,0:T(8,128)(2,1)S(1)} %get-tuple-element.71), channel_id=1, source_target_pairs={{9,11},{25,27},{41,43},{57,59},{73,75},{89,91},{105,107},{121,123}... | collective-permute-start | bytes 393224 | tf_op jit(solution)/shard_map/ppermute | solution.py:323
  15.1 0.2 again_lead.1
  15.3 0.7 %collective-permute-start.9 = (bf16[256,256]{1,0:T(8,128)(2,1)S(1)}, bf16[256,256]{1,0:T(8,128)(2,1)S(1)}, u32[]{:S(2)}, u32[]{:S(2)}) collective-permute-start(bf16[256,256]{1,0:T(8,128)(2,1)S(1)} %get-tuple-element.77), channel_id=1, source_target_pairs={{5,7},{21,23},{37,39},{53,55},{69,71},{85,87},{101,103},{117,119},... | collective-permute-start | bytes 393224 | tf_op jit(solution)/shard_map/ppermute | solution.py:323
  16.0 0.7 %collective-permute-start.11 = (bf16[256,256]{1,0:T(8,128)(2,1)S(1)}, bf16[256,256]{1,0:T(8,128)(2,1)S(1)}, u32[]{:S(2)}, u32[]{:S(2)}) collective-permute-start(bf16[256,256]{1,0:T(8,128)(2,1)S(1)} %get-tuple-element.80.__), channel_id=1, source_target_pairs={{7,9},{23,25},{39,41},{55,57},{71,73},{87,89},{103,105},{119,121},... | collective-permute-start | bytes 393224 | tf_op jit(solution)/shard_map/ppermute | solution.py:323
  16.8 0.7 %collective-permute-start.13 = (bf16[256,256]{1,0:T(8,128)(2,1)S(1)}, bf16[256,256]{1,0:T(8,128)(2,1)S(1)}, u32[]{:S(2)}, u32[]{:S(2)}) collective-permute-start(bf16[256,256]{1,0:T(8,128)(2,1)S(1)} %get-tuple-element.83), channel_id=1, source_target_pairs={{9,11},{11,13},{25,27},{27,29},{41,43},{43,45},{57,59},{59,61},{73... | collective-permute-start | bytes 393224 | tf_op jit(solution)/shard_map/ppermute | solution.py:323
  17.4 0.7 %collective-permute-start.12 = (bf16[256,256]{1,0:T(8,128)(2,1)S(1)}, bf16[256,256]{1,0:T(8,128)(2,1)S(1)}, u32[]{:S(2)}, u32[]{:S(2)}) collective-permute-start(bf16[256,256]{1,0:T(8,128)(2,1)S(1)} %get-tuple-element.82), channel_id=1, source_target_pairs={{7,11},{23,27},{39,43},{55,59},{71,75},{87,91},{103,107},{119,123}... | collective-permute-start | bytes 393224 | tf_op jit(solution)/shard_map/ppermute | solution.py:323
  18.1 0.7 %collective-permute-start.10 = (bf16[256,256]{1,0:T(8,128)(2,1)S(1)}, bf16[256,256]{1,0:T(8,128)(2,1)S(1)}, u32[]{:S(2)}, u32[]{:S(2)}) collective-permute-start(bf16[256,256]{1,0:T(8,128)(2,1)S(1)} %get-tuple-element.79.mine), channel_id=1, source_target_pairs={{7,11},{11,15},{23,27},{27,31},{39,43},{43,47},{55,59},{59,63},{71... | collective-permute-start | bytes 393224 | tf_op jit(solution)/shard_map/ppermute | solution.py:323
  18.8 0.0 collective-permute-done.13.got
  18.8 0.0 collective-permute-done.12.upper
  18.8 0.0 collective-permute-done.10.got.upper
  18.9 0.7 %collective-permute-start.14 = (bf16[256,256]{1,0:T(8,128)(2,1)S(1)}, bf16[256,256]{1,0:T(8,128)(2,1)S(1)}, u32[]{:S(2)}, u32[]{:S(2)}) collective-permute-start(bf16[256,256]{1,0:T(8,128)(2,1)S(1)} %get-tuple-element.89.mine), channel_id=1, source_target_pairs={{11,13},{7,9},{13,15},{27,29},{23,25},{29,31},{43,45},{39,41},{45,... | collective-permute-start | bytes 393224 | tf_op jit(solution)/shard_map/ppermute | solution.py:323
  19.6 0.7 %collective-permute-start.17 = (bf16[256,256]{1,0:T(8,128)(2,1)S(1)}, bf16[256,256]{1,0:T(8,128)(2,1)S(1)}, u32[]{:S(2)}, u32[]{:S(2)}) collective-permute-start(bf16[256,256]{1,0:T(8,128)(2,1)S(1)} %get-tuple-element.89.mine), channel_id=1, source_target_pairs={{11,15},{3,2},{5,4},{7,8},{27,31},{19,18},{21,20},{23,24},{43,47},... | collective-permute-start | bytes 393224 | tf_op jit(solution)/shard_map/ppermute | solution.py:323
  20.3 0.7 %collective-permute-start.16 = (bf16[256,256]{1,0:T(8,128)(2,1)S(1)}, bf16[256,256]{1,0:T(8,128)(2,1)S(1)}, u32[]{:S(2)}, u32[]{:S(2)}) collective-permute-start(bf16[256,256]{1,0:T(8,128)(2,1)S(1)} %get-tuple-element.91), channel_id=1, source_target_pairs={{13,15},{9,11},{29,31},{25,27},{45,47},{41,43},{61,63},{57,59},{77... | collective-permute-start | bytes 393224 | tf_op jit(solution)/shard_map/ppermute | solution.py:323
  21.0 1.3 %collective-permute-start.15 = (bf16[256,256]{1,0:T(8,128)(2,1)S(1)}, bf16[256,256]{1,0:T(8,128)(2,1)S(1)}, u32[]{:S(2)}, u32[]{:S(2)}) collective-permute-start(bf16[256,256]{1,0:T(8,128)(2,1)S(1)} %get-tuple-element.91), channel_id=1, source_target_pairs={{13,14},{9,10},{11,12},{7,6},{29,30},{25,26},{27,28},{23,22},{45,4... | collective-permute-start | bytes 393224 | tf_op jit(solution)/shard_map/ppermute | solution.py:323
  22.3 0.0 collective-permute-done.17.lead.got7b
  22.3 0.0 collective-permute-done.16.got8
  22.3 24.7 %collective-permute-done.15.got8b = bf16[256,256]{1,0:T(8,128)(2,1)S(1)} collective-permute-done((bf16[256,256]{1,0:T(8,128)(2,1)S(1)}, bf16[256,256]{1,0:T(8,128)(2,1)S(1)}, u32[]{:S(2)}, u32[]{:S(2)}) %collective-permute-start.15) | collective-permute-done | bytes 131104 | tf_op jit(solution)/shard_map/ppermute | solution.py:323
  47.1 2.3 %last_sweep.1 = f32[4,256,256]{2,1,0:T(8,128)} custom-call(f32[256,256]{1,0:T(8,128)S(1)} %get-tuple-element.60.start, bf16[256,256]{1,0:T(8,128)(2,1)S(1)} %collective-permute-done.15.got8b, bf16[256,256]{1,0:T(8,128)(2,1)S(1)} %collective-permute-done.16.got8, bf16[256,256]{1,0:T(8,128)(2,1)S(1)} %collective-permute-done.5.got.early3.got3, ...), custom_call_target="tpu_custom_call" | custom-call | flops 1207959552 | bytes 1048576 | tf_op jit(solution)/shard_map/last_sweep/pallas_call | solution.py:58
  (24 shorter events, 0.3 us)
Async XLA Ops:
  0.1 7.9 %collective-permute-start = (bf16[256,256]{1,0:T(8,128)(2,1)S(1)}, bf16[256,256]{1,0:T(8,128)(2,1)S(1)}, u32[]{:S(2)}, u32[]{:S(2)}) collective-permute-start(bf16[256,256]{1,0:T(8,128)(2,1)S(1)} %get-tuple-element.49.refs_6_), channel_id=1, source_target_pairs={{1,2},{3,4},{5,6},{7,8},{9,10},{11,12},{13,14},{17,18},{19,20},{21... | collective-permute-start | bytes 393224 | tf_op jit(solution)/shard_map/ppermute | solution.py:323
  5.0 3.0 %collective-permute-start.1 = (bf16[256,256]{1,0:T(8,128)(2,1)S(1)}, bf16[256,256]{1,0:T(8,128)(2,1)S(1)}, u32[]{:S(2)}, u32[]{:S(2)}) collective-permute-start(bf16[256,256]{1,0:T(8,128)(2,1)S(1)} %get-tuple-element.58), channel_id=1, source_target_pairs={{0,1},{2,3},{4,5},{6,7},{8,9},{10,11},{12,13},{14,15},{16,17},{18,... | collective-permute-start | bytes 393224 | tf_op jit(solution)/shard_map/ppermute | solution.py:323
  6.3 6.3 %collective-permute-start.3 = (bf16[256,2304]{1,0:T(8,128)(2,1)S(1)}, bf16[256,2304]{1,0:T(8,128)(2,1)S(1)}, u32[]{:S(2)}, u32[]{:S(2)}) collective-permute-start(bf16[256,2304]{1,0:T(8,128)(2,1)S(1)} %get-tuple-element.55.own_w), channel_id=1, source_target_pairs={{0,1},{2,3},{4,5},{6,7},{8,9},{10,11},{12,13},{14,15},{16,17},{18,... | collective-permute-start | bytes 3538952 | tf_op jit(solution)/shard_map/ppermute | solution.py:323
  8.0 4.6 %collective-permute-start.5 = (bf16[256,256]{1,0:T(8,128)(2,1)S(1)}, bf16[256,256]{1,0:T(8,128)(2,1)S(1)}, u32[]{:S(2)}, u32[]{:S(2)}) collective-permute-start(bf16[256,256]{1,0:T(8,128)(2,1)S(1)} %get-tuple-element.66), channel_id=1, source_target_pairs={{1,3},{17,19},{33,35},{49,51},{65,67},{81,83},{97,99},{113,115},{1... | collective-permute-start | bytes 393224 | tf_op jit(solution)/shard_map/ppermute | solution.py:323
  10.5 2.4 %collective-permute-start.2 = (f32[256,256]{1,0:T(8,128)S(1)}, f32[256,256]{1,0:T(8,128)S(1)}, u32[]{:S(2)}, u32[]{:S(2)}) collective-permute-start(f32[256,256]{1,0:T(8,128)S(1)} %get-tuple-element.61.rhs_of_even), channel_id=1, source_target_pairs={{0,1},{2,3},{4,5},{6,7},{8,9},{10,11},{12,13},{14,15},{16,17},{18,... | collective-permute-start | bytes 786440 | tf_op jit(solution)/shard_map/ppermute | solution.py:323
  11.9 1.8 %collective-permute-start.4 = (f32[256,256]{1,0:T(8,128)S(1)}, f32[256,256]{1,0:T(8,128)S(1)}, u32[]{:S(2)}, u32[]{:S(2)}) collective-permute-start(f32[256,256]{1,0:T(8,128)S(1)} %get-tuple-element.65), channel_id=1, source_target_pairs={{4,5},{8,9},{20,21},{24,25},{36,37},{40,41},{52,53},{56,57},{68,69... | collective-permute-start | bytes 786440 | tf_op jit(solution)/shard_map/ppermute | solution.py:323
  13.0 2.1 %collective-permute-start.8 = (bf16[256,256]{1,0:T(8,128)(2,1)S(1)}, bf16[256,256]{1,0:T(8,128)(2,1)S(1)}, u32[]{:S(2)}, u32[]{:S(2)}) collective-permute-start(bf16[256,256]{1,0:T(8,128)(2,1)S(1)} %get-tuple-element.72), channel_id=1, source_target_pairs={{3,5},{19,21},{35,37},{51,53},{67,69},{83,85},{99,101},{115,117},{... | collective-permute-start | bytes 393224 | tf_op jit(solution)/shard_map/ppermute | solution.py:323
  13.7 2.2 %collective-permute-start.7 = (bf16[256,256]{1,0:T(8,128)(2,1)S(1)}, bf16[256,256]{1,0:T(8,128)(2,1)S(1)}, u32[]{:S(2)}, u32[]{:S(2)}) collective-permute-start(bf16[256,256]{1,0:T(8,128)(2,1)S(1)} %get-tuple-element.71), channel_id=1, source_target_pairs={{5,7},{21,23},{37,39},{53,55},{69,71},{85,87},{101,103},{117,119},... | collective-permute-start | bytes 393224 | tf_op jit(solution)/shard_map/ppermute | solution.py:323
  14.4 2.3 %collective-permute-start.6 = (bf16[256,256]{1,0:T(8,128)(2,1)S(1)}, bf16[256,256]{1,0:T(8,128)(2,1)S(1)}, u32[]{:S(2)}, u32[]{:S(2)}) collective-permute-start(bf16[256,256]{1,0:T(8,128)(2,1)S(1)} %get-tuple-element.71), channel_id=1, source_target_pairs={{9,11},{25,27},{41,43},{57,59},{73,75},{89,91},{105,107},{121,123}... | collective-permute-start | bytes 393224 | tf_op jit(solution)/shard_map/ppermute | solution.py:323
  15.3 1.4 %collective-permute-start.9 = (bf16[256,256]{1,0:T(8,128)(2,1)S(1)}, bf16[256,256]{1,0:T(8,128)(2,1)S(1)}, u32[]{:S(2)}, u32[]{:S(2)}) collective-permute-start(bf16[256,256]{1,0:T(8,128)(2,1)S(1)} %get-tuple-element.77), channel_id=1, source_target_pairs={{5,7},{21,23},{37,39},{53,55},{69,71},{85,87},{101,103},{117,119},... | collective-permute-start | bytes 393224 | tf_op jit(solution)/shard_map/ppermute | solution.py:323
  16.0 0.8 %collective-permute-start.11 = (bf16[256,256]{1,0:T(8,128)(2,1)S(1)}, bf16[256,256]{1,0:T(8,128)(2,1)S(1)}, u32[]{:S(2)}, u32[]{:S(2)}) collective-permute-start(bf16[256,256]{1,0:T(8,128)(2,1)S(1)} %get-tuple-element.80.__), channel_id=1, source_target_pairs={{7,9},{23,25},{39,41},{55,57},{71,73},{87,89},{103,105},{119,121},... | collective-permute-start | bytes 393224 | tf_op jit(solution)/shard_map/ppermute | solution.py:323
  16.8 2.0 %collective-permute-start.13 = (bf16[256,256]{1,0:T(8,128)(2,1)S(1)}, bf16[256,256]{1,0:T(8,128)(2,1)S(1)}, u32[]{:S(2)}, u32[]{:S(2)}) collective-permute-start(bf16[256,256]{1,0:T(8,128)(2,1)S(1)} %get-tuple-element.83), channel_id=1, source_target_pairs={{9,11},{11,13},{25,27},{27,29},{41,43},{43,45},{57,59},{59,61},{73... | collective-permute-start | bytes 393224 | tf_op jit(solution)/shard_map/ppermute | solution.py:323
  17.4 1.4 %collective-permute-start.12 = (bf16[256,256]{1,0:T(8,128)(2,1)S(1)}, bf16[256,256]{1,0:T(8,128)(2,1)S(1)}, u32[]{:S(2)}, u32[]{:S(2)}) collective-permute-start(bf16[256,256]{1,0:T(8,128)(2,1)S(1)} %get-tuple-element.82), channel_id=1, source_target_pairs={{7,11},{23,27},{39,43},{55,59},{71,75},{87,91},{103,107},{119,123}... | collective-permute-start | bytes 393224 | tf_op jit(solution)/shard_map/ppermute | solution.py:323
  18.1 0.7 %collective-permute-start.10 = (bf16[256,256]{1,0:T(8,128)(2,1)S(1)}, bf16[256,256]{1,0:T(8,128)(2,1)S(1)}, u32[]{:S(2)}, u32[]{:S(2)}) collective-permute-start(bf16[256,256]{1,0:T(8,128)(2,1)S(1)} %get-tuple-element.79.mine), channel_id=1, source_target_pairs={{7,11},{11,15},{23,27},{27,31},{39,43},{43,47},{55,59},{59,63},{71... | collective-permute-start | bytes 393224 | tf_op jit(solution)/shard_map/ppermute | solution.py:323
  18.9 1.4 %collective-permute-start.14 = (bf16[256,256]{1,0:T(8,128)(2,1)S(1)}, bf16[256,256]{1,0:T(8,128)(2,1)S(1)}, u32[]{:S(2)}, u32[]{:S(2)}) collective-permute-start(bf16[256,256]{1,0:T(8,128)(2,1)S(1)} %get-tuple-element.89.mine), channel_id=1, source_target_pairs={{11,13},{7,9},{13,15},{27,29},{23,25},{29,31},{43,45},{39,41},{45,... | collective-permute-start | bytes 393224 | tf_op jit(solution)/shard_map/ppermute | solution.py:323
  19.6 2.7 %collective-permute-start.17 = (bf16[256,256]{1,0:T(8,128)(2,1)S(1)}, bf16[256,256]{1,0:T(8,128)(2,1)S(1)}, u32[]{:S(2)}, u32[]{:S(2)}) collective-permute-start(bf16[256,256]{1,0:T(8,128)(2,1)S(1)} %get-tuple-element.89.mine), channel_id=1, source_target_pairs={{11,15},{3,2},{5,4},{7,8},{27,31},{19,18},{21,20},{23,24},{43,47},... | collective-permute-start | bytes 393224 | tf_op jit(solution)/shard_map/ppermute | solution.py:323
  20.3 2.0 %collective-permute-start.16 = (bf16[256,256]{1,0:T(8,128)(2,1)S(1)}, bf16[256,256]{1,0:T(8,128)(2,1)S(1)}, u32[]{:S(2)}, u32[]{:S(2)}) collective-permute-start(bf16[256,256]{1,0:T(8,128)(2,1)S(1)} %get-tuple-element.91), channel_id=1, source_target_pairs={{13,15},{9,11},{29,31},{25,27},{45,47},{41,43},{61,63},{57,59},{77... | collective-permute-start | bytes 393224 | tf_op jit(solution)/shard_map/ppermute | solution.py:323
  21.0 26.1 %collective-permute-start.15 = (bf16[256,256]{1,0:T(8,128)(2,1)S(1)}, bf16[256,256]{1,0:T(8,128)(2,1)S(1)}, u32[]{:S(2)}, u32[]{:S(2)}) collective-permute-start(bf16[256,256]{1,0:T(8,128)(2,1)S(1)} %get-tuple-element.91), channel_id=1, source_target_pairs={{13,14},{9,10},{11,12},{7,6},{29,30},{25,26},{27,28},{23,22},{45,4... | collective-permute-start | bytes 393224 | tf_op jit(solution)/shard_map/ppermute | solution.py:323

commit v4 on v2

--- a/solution.py
+++ b/solution.py
@@ -369,14 +369,14 @@
         scratch=[pltpu.VMEM((CHANS, CELLS), F32), pltpu.SemaphoreType.DMA(())],
         aliases={4: 2, 5: 3},
     )
+    even_rhs = send(rhs_of_even, up_inside)
     first = send(first, [(4, 5), (8, 9)])
-    even_rhs = send(rhs_of_even, up_inside)
     rhs, solved = kernel_call(
         second_sweep_odd,
         [wide, wide],
         [left_odd, own_w, later_w, rhs, solved],
         "second_sweep_odd",
-        4,
+        0,
         aliases={3: 0, 4: 1},
     )
     both = [even_rhs, rhs, even_w, own_w]
@@ -391,17 +391,18 @@
     def pair(owners, keep, got, name):
         return chained(functools.partial(two_steps, owners, keep), [*both, got], name, 2)
 
-    part = chained(lead_half, [got3, even_w], "lead_first", 10, wide)
-    upper1 = chained(lead_rest, [rhs, own_w, even_rhs, part], "relax_lead", 1)
+    part = chained(lead_half, [got3, even_w], "lead_first", 7, wide)
+    upper1 = chained(lead_rest, [rhs, own_w, even_rhs, part], "relax_lead", 20)
     got4 = send(upper1, [(3, 5)])
     c5 = chained(functools.partial(one_step, (5, 9)), [first, rhs, own_w], "relax_first", 1)
-    got3_rest = send(c5, [(5, 7), (9, 11)])
+    got3_rest = send(c5, [(5, 7)])
+    got3_last = send(c5, [(9, 11)])
     c5_lead = pair((5,), False, got4, "again_lead")
     got5 = send(c5_lead, [(5, 7)])
     upper7 = pair((7,), False, got3_rest, "relax_rest")
     got4_rest = send(upper7, [(7, 9)])
     upper_prev = send(upper7, [(7, 11)])
-    upper11 = pair((11,), False, got3_rest, "relax_last")
+    upper11 = pair((11,), False, got3_last, "relax_last")
     z2 = chained(
         functools.partial(steps_or_copy, 7, True), [upper11, *both, got5], "again_end_lead", 2
     )

time: 48.2 us -> 47.9 us (level)
  waiting for transfers between devices: 24.4 us -> 23.5 us
  starting transfers between devices: 14.6 us -> 15.2 us
    ppermute x17 -> x18, waiting for transfers between devices: 24.4 us -> 23.5 us  [send(): return lax.ppermute(value, 'layer', pairs)]
    ppermute x17 -> x18, starting transfers between devices: 14.6 us -> 15.2 us  [send(): return lax.ppermute(value, 'layer', pairs)]
  transfers between devices with their start and end apart: 17 -> 18, of which waited for: 3 -> 3; matrix products, arithmetic and copies ran while one was open for 0% -> 0% of each run, Pallas kernels for 12% -> 12%
where the time goes in v4:
time: 47.9 us; the launch traced here: 47.6 us
  waiting for transfers between devices  23.5 us (49%)
  starting transfers between devices  15.2 us (32%)
  Pallas kernels  8.31 us (17%)
  between operations  0.54 us (1%)
    ppermute x18, waiting for transfers between devices, send(): return lax.ppermute(value, 'layer', pairs)  23.5 us
    ppermute x18, starting transfers between devices, send(): return lax.ppermute(value, 'layer', pairs)  15.2 us
    pallas_call x20, Pallas kernels, kernel_call(): pl.pallas_call(body, out_shape=outs, in_specs=[pl.BlockSpec(memory_space=...  8.31 us
  transfers between devices with their start and end apart: 18, of which 3 were waited for; matrix products, arithmetic and copies ran while one was open for 0% of the time, Pallas kernels for 12%

profile of v4, /device:TPU:248, one launch (start us, length us, event | category | flops | bytes accessed | tf_op | source)
XLA Modules:
  0.0 47.6 jit_solution(5614771365673892384)
XLA Ops:
  0.1 1.3 %collective-permute-start = (bf16[256,256]{1,0:T(8,128)(2,1)S(1)}, bf16[256,256]{1,0:T(8,128)(2,1)S(1)}, u32[]{:S(2)}, u32[]{:S(2)}) collective-permute-start(bf16[256,256]{1,0:T(8,128)(2,1)S(1)} %get-tuple-element.48.refs_6_), channel_id=1, source_target_pairs={{1,2},{3,4},{5,6},{7,8},{9,10},{11,12},{13,14},{17,18},{19,20},{21... | collective-permute-start | bytes 393224 | tf_op jit(solution)/shard_map/ppermute | solution.py:319
  1.4 3.7 %first_sweep_even.1 = (bf16[256,256]{1,0:T(8,128)(2,1)S(1)}, bf16[256,2304]{1,0:T(8,128)(2,1)S(1)}, bf16[3,256,2304]{2,1,0:T(8,128)(2,1)S(1)}, f32[256,256]{1,0:T(8,128)S(1)}) custom-call(f32[256,256]{1,0:T(8,128)} %inputs.1, f32[1,256,256]{2,1,0:T(8,128)} %refs_1_.3, ...), custom_call_target="tpu_custom_call", output_to_operand_aliasing={{1}: (3, {}), {2}: (4, {}), {3}: (5, {})} | custom-call | flops 1207959552 | bytes 1048576 | tf_op jit(solution)/shard_map/first_sweep_even/pallas_call | solution.py:58
  5.0 1.3 %collective-permute-start.1 = (bf16[256,256]{1,0:T(8,128)(2,1)S(1)}, bf16[256,256]{1,0:T(8,128)(2,1)S(1)}, u32[]{:S(2)}, u32[]{:S(2)}) collective-permute-start(bf16[256,256]{1,0:T(8,128)(2,1)S(1)} %get-tuple-element.57), channel_id=1, source_target_pairs={{0,1},{2,3},{4,5},{6,7},{8,9},{10,11},{12,13},{14,15},{16,17},{18,... | collective-permute-start | bytes 393224 | tf_op jit(solution)/shard_map/ppermute | solution.py:319
  6.3 1.4 %collective-permute-start.3 = (bf16[256,2304]{1,0:T(8,128)(2,1)S(1)}, bf16[256,2304]{1,0:T(8,128)(2,1)S(1)}, u32[]{:S(2)}, u32[]{:S(2)}) collective-permute-start(bf16[256,2304]{1,0:T(8,128)(2,1)S(1)} %get-tuple-element.54.own_w), channel_id=1, source_target_pairs={{0,1},{2,3},{4,5},{6,7},{8,9},{10,11},{12,13},{14,15},{16,17},{18,... | collective-permute-start | bytes 3538952 | tf_op jit(solution)/shard_map/ppermute | solution.py:319
  7.7 0.3 collective-permute-done.refs_0_
  8.0 0.7 %collective-permute-start.5 = (bf16[256,256]{1,0:T(8,128)(2,1)S(1)}, bf16[256,256]{1,0:T(8,128)(2,1)S(1)}, u32[]{:S(2)}, u32[]{:S(2)}) collective-permute-start(bf16[256,256]{1,0:T(8,128)(2,1)S(1)} %get-tuple-element.65), channel_id=1, source_target_pairs={{1,3},{17,19},{33,35},{49,51},{65,67},{81,83},{97,99},{113,115},{1... | collective-permute-start | bytes 393224 | tf_op jit(solution)/shard_map/ppermute | solution.py:319
  8.6 1.9 %second_sweep_even.1 = (f32[256,256]{1,0:T(8,128)S(1)}, f32[256,256]{1,0:T(8,128)S(1)}, f32[256,256]{1,0:T(8,128)S(1)}, f32[256,256]{1,0:T(8,128)S(1)}) custom-call(bf16[256,256]{1,0:T(8,128)(2,1)S(1)} %get-tuple-element.53.left_even, bf16[256,2304]{1,0:T(8,128)(2,1)S(1)} %get-tuple-element.54.own_w, ...), custom_call_target="tpu_custom_call", output_to_operand_aliasing={{2}: (4, {}), {3}: (5, {})} | custom-call | flops 1207959552 | bytes 1048576 | tf_op jit(solution)/shard_map/second_sweep_even/pallas_call | solution.py:58
  10.5 1.3 %collective-permute-start.2 = (f32[256,256]{1,0:T(8,128)S(1)}, f32[256,256]{1,0:T(8,128)S(1)}, u32[]{:S(2)}, u32[]{:S(2)}) collective-permute-start(f32[256,256]{1,0:T(8,128)S(1)} %get-tuple-element.60.rhs_of_even), channel_id=1, source_target_pairs={{0,1},{2,3},{4,5},{6,7},{8,9},{10,11},{12,13},{14,15},{16,17},{18,... | collective-permute-start | bytes 786440 | tf_op jit(solution)/shard_map/ppermute | solution.py:319
  11.9 0.7 %collective-permute-start.4 = (f32[256,256]{1,0:T(8,128)S(1)}, f32[256,256]{1,0:T(8,128)S(1)}, u32[]{:S(2)}, u32[]{:S(2)}) collective-permute-start(f32[256,256]{1,0:T(8,128)S(1)} %get-tuple-element.64), channel_id=1, source_target_pairs={{4,5},{8,9},{20,21},{24,25},{36,37},{40,41},{52,53},{56,57},{68,69... | collective-permute-start | bytes 786440 | tf_op jit(solution)/shard_map/ppermute | solution.py:319
  12.6 0.0 collective-permute-done.5.got.early3.got3
  12.6 0.0 collective-permute-done.3.even_w
  12.6 0.4 collective-permute-done.2.even_rhs
  13.0 0.7 %collective-permute-start.8 = (bf16[256,256]{1,0:T(8,128)(2,1)S(1)}, bf16[256,256]{1,0:T(8,128)(2,1)S(1)}, u32[]{:S(2)}, u32[]{:S(2)}) collective-permute-start(bf16[256,256]{1,0:T(8,128)(2,1)S(1)} %get-tuple-element.71), channel_id=1, source_target_pairs={{3,5},{19,21},{35,37},{51,53},{67,69},{83,85},{99,101},{115,117},{... | collective-permute-start | bytes 393224 | tf_op jit(solution)/shard_map/ppermute | solution.py:319
  13.7 0.0 collective-permute-done.4.first
  13.7 0.7 %collective-permute-start.7 = (bf16[256,256]{1,0:T(8,128)(2,1)S(1)}, bf16[256,256]{1,0:T(8,128)(2,1)S(1)}, u32[]{:S(2)}, u32[]{:S(2)}) collective-permute-start(bf16[256,256]{1,0:T(8,128)(2,1)S(1)} %get-tuple-element.70), channel_id=1, source_target_pairs={{5,7},{21,23},{37,39},{53,55},{69,71},{85,87},{101,103},{117,119},... | collective-permute-start | bytes 393224 | tf_op jit(solution)/shard_map/ppermute | solution.py:319
  14.4 0.7 %collective-permute-start.6 = (bf16[256,256]{1,0:T(8,128)(2,1)S(1)}, bf16[256,256]{1,0:T(8,128)(2,1)S(1)}, u32[]{:S(2)}, u32[]{:S(2)}) collective-permute-start(bf16[256,256]{1,0:T(8,128)(2,1)S(1)} %get-tuple-element.70), channel_id=1, source_target_pairs={{9,11},{25,27},{41,43},{57,59},{73,75},{89,91},{105,107},{121,123}... | collective-permute-start | bytes 393224 | tf_op jit(solution)/shard_map/ppermute | solution.py:319
  15.0 0.0 collective-permute-done.8.got.early4.got4
  15.1 0.2 again_lead.1
  15.3 0.7 %collective-permute-start.9 = (bf16[256,256]{1,0:T(8,128)(2,1)S(1)}, bf16[256,256]{1,0:T(8,128)(2,1)S(1)}, u32[]{:S(2)}, u32[]{:S(2)}) collective-permute-start(bf16[256,256]{1,0:T(8,128)(2,1)S(1)} %get-tuple-element.76), channel_id=1, source_target_pairs={{5,7},{21,23},{37,39},{53,55},{69,71},{85,87},{101,103},{117,119},... | collective-permute-start | bytes 393224 | tf_op jit(solution)/shard_map/ppermute | solution.py:319
  15.9 0.0 collective-permute-done.7.got
  16.0 0.7 %collective-permute-start.12 = (bf16[256,256]{1,0:T(8,128)(2,1)S(1)}, bf16[256,256]{1,0:T(8,128)(2,1)S(1)}, u32[]{:S(2)}, u32[]{:S(2)}) collective-permute-start(bf16[256,256]{1,0:T(8,128)(2,1)S(1)} %get-tuple-element.79), channel_id=1, source_target_pairs={{7,9},{23,25},{39,41},{55,57},{71,73},{87,89},{103,105},{119,121},... | collective-permute-start | bytes 393224 | tf_op jit(solution)/shard_map/ppermute | solution.py:319
  16.6 0.7 %collective-permute-start.11 = (bf16[256,256]{1,0:T(8,128)(2,1)S(1)}, bf16[256,256]{1,0:T(8,128)(2,1)S(1)}, u32[]{:S(2)}, u32[]{:S(2)}) collective-permute-start(bf16[256,256]{1,0:T(8,128)(2,1)S(1)} %get-tuple-element.79), channel_id=1, source_target_pairs={{7,11},{23,27},{39,43},{55,59},{71,75},{87,91},{103,107},{119,123}... | collective-permute-start | bytes 393224 | tf_op jit(solution)/shard_map/ppermute | solution.py:319
  17.4 0.0 collective-permute-done.9.got.early5.got5
  17.4 0.7 %collective-permute-start.13 = (bf16[256,256]{1,0:T(8,128)(2,1)S(1)}, bf16[256,256]{1,0:T(8,128)(2,1)S(1)}, u32[]{:S(2)}, u32[]{:S(2)}) collective-permute-start(bf16[256,256]{1,0:T(8,128)(2,1)S(1)} %get-tuple-element.83), channel_id=1, source_target_pairs={{9,11},{11,13},{25,27},{27,29},{41,43},{43,45},{57,59},{59,61},{73... | collective-permute-start | bytes 393224 | tf_op jit(solution)/shard_map/ppermute | solution.py:319
  18.1 0.7 %collective-permute-start.10 = (bf16[256,256]{1,0:T(8,128)(2,1)S(1)}, bf16[256,256]{1,0:T(8,128)(2,1)S(1)}, u32[]{:S(2)}, u32[]{:S(2)}) collective-permute-start(bf16[256,256]{1,0:T(8,128)(2,1)S(1)} %get-tuple-element.78.mine), channel_id=1, source_target_pairs={{7,11},{11,15},{23,27},{27,31},{39,43},{43,47},{55,59},{59,63},{71... | collective-permute-start | bytes 393224 | tf_op jit(solution)/shard_map/ppermute | solution.py:319
  18.8 0.0 collective-permute-done.13.got
  18.9 0.7 %collective-permute-start.14 = (bf16[256,256]{1,0:T(8,128)(2,1)S(1)}, bf16[256,256]{1,0:T(8,128)(2,1)S(1)}, u32[]{:S(2)}, u32[]{:S(2)}) collective-permute-start(bf16[256,256]{1,0:T(8,128)(2,1)S(1)} %get-tuple-element.87.mine), channel_id=1, source_target_pairs={{11,13},{7,9},{13,15},{27,29},{23,25},{29,31},{43,45},{39,41},{45,... | collective-permute-start | bytes 393224 | tf_op jit(solution)/shard_map/ppermute | solution.py:319
  19.6 0.7 %collective-permute-start.17 = (bf16[256,256]{1,0:T(8,128)(2,1)S(1)}, bf16[256,256]{1,0:T(8,128)(2,1)S(1)}, u32[]{:S(2)}, u32[]{:S(2)}) collective-permute-start(bf16[256,256]{1,0:T(8,128)(2,1)S(1)} %get-tuple-element.87.mine), channel_id=1, source_target_pairs={{11,15},{3,2},{5,4},{7,8},{27,31},{19,18},{21,20},{23,24},{43,47},... | collective-permute-start | bytes 393224 | tf_op jit(solution)/shard_map/ppermute | solution.py:319
  20.3 0.7 %collective-permute-start.16 = (bf16[256,256]{1,0:T(8,128)(2,1)S(1)}, bf16[256,256]{1,0:T(8,128)(2,1)S(1)}, u32[]{:S(2)}, u32[]{:S(2)}) collective-permute-start(bf16[256,256]{1,0:T(8,128)(2,1)S(1)} %get-tuple-element.89), channel_id=1, source_target_pairs={{13,15},{9,11},{29,31},{25,27},{45,47},{41,43},{61,63},{57,59},{77... | collective-permute-start | bytes 393224 | tf_op jit(solution)/shard_map/ppermute | solution.py:319
  21.0 1.3 %collective-permute-start.15 = (bf16[256,256]{1,0:T(8,128)(2,1)S(1)}, bf16[256,256]{1,0:T(8,128)(2,1)S(1)}, u32[]{:S(2)}, u32[]{:S(2)}) collective-permute-start(bf16[256,256]{1,0:T(8,128)(2,1)S(1)} %get-tuple-element.89), channel_id=1, source_target_pairs={{13,14},{9,10},{11,12},{7,6},{29,30},{25,26},{27,28},{23,22},{45,4... | collective-permute-start | bytes 393224 | tf_op jit(solution)/shard_map/ppermute | solution.py:319
  22.3 22.8 %collective-permute-done.15.got8b = bf16[256,256]{1,0:T(8,128)(2,1)S(1)} collective-permute-done((bf16[256,256]{1,0:T(8,128)(2,1)S(1)}, bf16[256,256]{1,0:T(8,128)(2,1)S(1)}, u32[]{:S(2)}, u32[]{:S(2)}) %collective-permute-start.15) | collective-permute-done | bytes 131104 | tf_op jit(solution)/shard_map/ppermute | solution.py:319
  45.1 2.3 %last_sweep.1 = f32[4,256,256]{2,1,0:T(8,128)} custom-call(f32[256,256]{1,0:T(8,128)S(1)} %get-tuple-element.59.start, bf16[256,256]{1,0:T(8,128)(2,1)S(1)} %collective-permute-done.15.got8b, bf16[256,256]{1,0:T(8,128)(2,1)S(1)} %collective-permute-done.16.got8, bf16[256,256]{1,0:T(8,128)(2,1)S(1)} %collective-permute-done.5.got.early3.got3, ...), custom_call_target="tpu_custom_call" | custom-call | flops 1207959552 | bytes 1048576 | tf_op jit(solution)/shard_map/last_sweep/pallas_call | solution.py:58
  (24 shorter events, 0.3 us)
Async XLA Ops:
  0.1 7.9 %collective-permute-start = (bf16[256,256]{1,0:T(8,128)(2,1)S(1)}, bf16[256,256]{1,0:T(8,128)(2,1)S(1)}, u32[]{:S(2)}, u32[]{:S(2)}) collective-permute-start(bf16[256,256]{1,0:T(8,128)(2,1)S(1)} %get-tuple-element.48.refs_6_), channel_id=1, source_target_pairs={{1,2},{3,4},{5,6},{7,8},{9,10},{11,12},{13,14},{17,18},{19,20},{21... | collective-permute-start | bytes 393224 | tf_op jit(solution)/shard_map/ppermute | solution.py:319
  5.0 3.0 %collective-permute-start.1 = (bf16[256,256]{1,0:T(8,128)(2,1)S(1)}, bf16[256,256]{1,0:T(8,128)(2,1)S(1)}, u32[]{:S(2)}, u32[]{:S(2)}) collective-permute-start(bf16[256,256]{1,0:T(8,128)(2,1)S(1)} %get-tuple-element.57), channel_id=1, source_target_pairs={{0,1},{2,3},{4,5},{6,7},{8,9},{10,11},{12,13},{14,15},{16,17},{18,... | collective-permute-start | bytes 393224 | tf_op jit(solution)/shard_map/ppermute | solution.py:319
  6.3 6.3 %collective-permute-start.3 = (bf16[256,2304]{1,0:T(8,128)(2,1)S(1)}, bf16[256,2304]{1,0:T(8,128)(2,1)S(1)}, u32[]{:S(2)}, u32[]{:S(2)}) collective-permute-start(bf16[256,2304]{1,0:T(8,128)(2,1)S(1)} %get-tuple-element.54.own_w), channel_id=1, source_target_pairs={{0,1},{2,3},{4,5},{6,7},{8,9},{10,11},{12,13},{14,15},{16,17},{18,... | collective-permute-start | bytes 3538952 | tf_op jit(solution)/shard_map/ppermute | solution.py:319
  8.0 4.6 %collective-permute-start.5 = (bf16[256,256]{1,0:T(8,128)(2,1)S(1)}, bf16[256,256]{1,0:T(8,128)(2,1)S(1)}, u32[]{:S(2)}, u32[]{:S(2)}) collective-permute-start(bf16[256,256]{1,0:T(8,128)(2,1)S(1)} %get-tuple-element.65), channel_id=1, source_target_pairs={{1,3},{17,19},{33,35},{49,51},{65,67},{81,83},{97,99},{113,115},{1... | collective-permute-start | bytes 393224 | tf_op jit(solution)/shard_map/ppermute | solution.py:319
  10.5 2.4 %collective-permute-start.2 = (f32[256,256]{1,0:T(8,128)S(1)}, f32[256,256]{1,0:T(8,128)S(1)}, u32[]{:S(2)}, u32[]{:S(2)}) collective-permute-start(f32[256,256]{1,0:T(8,128)S(1)} %get-tuple-element.60.rhs_of_even), channel_id=1, source_target_pairs={{0,1},{2,3},{4,5},{6,7},{8,9},{10,11},{12,13},{14,15},{16,17},{18,... | collective-permute-start | bytes 786440 | tf_op jit(solution)/shard_map/ppermute | solution.py:319
  11.9 1.8 %collective-permute-start.4 = (f32[256,256]{1,0:T(8,128)S(1)}, f32[256,256]{1,0:T(8,128)S(1)}, u32[]{:S(2)}, u32[]{:S(2)}) collective-permute-start(f32[256,256]{1,0:T(8,128)S(1)} %get-tuple-element.64), channel_id=1, source_target_pairs={{4,5},{8,9},{20,21},{24,25},{36,37},{40,41},{52,53},{56,57},{68,69... | collective-permute-start | bytes 786440 | tf_op jit(solution)/shard_map/ppermute | solution.py:319
  13.0 2.1 %collective-permute-start.8 = (bf16[256,256]{1,0:T(8,128)(2,1)S(1)}, bf16[256,256]{1,0:T(8,128)(2,1)S(1)}, u32[]{:S(2)}, u32[]{:S(2)}) collective-permute-start(bf16[256,256]{1,0:T(8,128)(2,1)S(1)} %get-tuple-element.71), channel_id=1, source_target_pairs={{3,5},{19,21},{35,37},{51,53},{67,69},{83,85},{99,101},{115,117},{... | collective-permute-start | bytes 393224 | tf_op jit(solution)/shard_map/ppermute | solution.py:319
  13.7 2.2 %collective-permute-start.7 = (bf16[256,256]{1,0:T(8,128)(2,1)S(1)}, bf16[256,256]{1,0:T(8,128)(2,1)S(1)}, u32[]{:S(2)}, u32[]{:S(2)}) collective-permute-start(bf16[256,256]{1,0:T(8,128)(2,1)S(1)} %get-tuple-element.70), channel_id=1, source_target_pairs={{5,7},{21,23},{37,39},{53,55},{69,71},{85,87},{101,103},{117,119},... | collective-permute-start | bytes 393224 | tf_op jit(solution)/shard_map/ppermute | solution.py:319
  14.4 3.0 %collective-permute-start.6 = (bf16[256,256]{1,0:T(8,128)(2,1)S(1)}, bf16[256,256]{1,0:T(8,128)(2,1)S(1)}, u32[]{:S(2)}, u32[]{:S(2)}) collective-permute-start(bf16[256,256]{1,0:T(8,128)(2,1)S(1)} %get-tuple-element.70), channel_id=1, source_target_pairs={{9,11},{25,27},{41,43},{57,59},{73,75},{89,91},{105,107},{121,123}... | collective-permute-start | bytes 393224 | tf_op jit(solution)/shard_map/ppermute | solution.py:319
  15.3 2.1 %collective-permute-start.9 = (bf16[256,256]{1,0:T(8,128)(2,1)S(1)}, bf16[256,256]{1,0:T(8,128)(2,1)S(1)}, u32[]{:S(2)}, u32[]{:S(2)}) collective-permute-start(bf16[256,256]{1,0:T(8,128)(2,1)S(1)} %get-tuple-element.76), channel_id=1, source_target_pairs={{5,7},{21,23},{37,39},{53,55},{69,71},{85,87},{101,103},{117,119},... | collective-permute-start | bytes 393224 | tf_op jit(solution)/shard_map/ppermute | solution.py:319
  16.0 1.4 %collective-permute-start.12 = (bf16[256,256]{1,0:T(8,128)(2,1)S(1)}, bf16[256,256]{1,0:T(8,128)(2,1)S(1)}, u32[]{:S(2)}, u32[]{:S(2)}) collective-permute-start(bf16[256,256]{1,0:T(8,128)(2,1)S(1)} %get-tuple-element.79), channel_id=1, source_target_pairs={{7,9},{23,25},{39,41},{55,57},{71,73},{87,89},{103,105},{119,121},... | collective-permute-start | bytes 393224 | tf_op jit(solution)/shard_map/ppermute | solution.py:319
  16.6 2.1 %collective-permute-start.11 = (bf16[256,256]{1,0:T(8,128)(2,1)S(1)}, bf16[256,256]{1,0:T(8,128)(2,1)S(1)}, u32[]{:S(2)}, u32[]{:S(2)}) collective-permute-start(bf16[256,256]{1,0:T(8,128)(2,1)S(1)} %get-tuple-element.79), channel_id=1, source_target_pairs={{7,11},{23,27},{39,43},{55,59},{71,75},{87,91},{103,107},{119,123}... | collective-permute-start | bytes 393224 | tf_op jit(solution)/shard_map/ppermute | solution.py:319
  17.4 1.4 %collective-permute-start.13 = (bf16[256,256]{1,0:T(8,128)(2,1)S(1)}, bf16[256,256]{1,0:T(8,128)(2,1)S(1)}, u32[]{:S(2)}, u32[]{:S(2)}) collective-permute-start(bf16[256,256]{1,0:T(8,128)(2,1)S(1)} %get-tuple-element.83), channel_id=1, source_target_pairs={{9,11},{11,13},{25,27},{27,29},{41,43},{43,45},{57,59},{59,61},{73... | collective-permute-start | bytes 393224 | tf_op jit(solution)/shard_map/ppermute | solution.py:319
  18.1 0.7 %collective-permute-start.10 = (bf16[256,256]{1,0:T(8,128)(2,1)S(1)}, bf16[256,256]{1,0:T(8,128)(2,1)S(1)}, u32[]{:S(2)}, u32[]{:S(2)}) collective-permute-start(bf16[256,256]{1,0:T(8,128)(2,1)S(1)} %get-tuple-element.78.mine), channel_id=1, source_target_pairs={{7,11},{11,15},{23,27},{27,31},{39,43},{43,47},{55,59},{59,63},{71... | collective-permute-start | bytes 393224 | tf_op jit(solution)/shard_map/ppermute | solution.py:319
  18.9 1.4 %collective-permute-start.14 = (bf16[256,256]{1,0:T(8,128)(2,1)S(1)}, bf16[256,256]{1,0:T(8,128)(2,1)S(1)}, u32[]{:S(2)}, u32[]{:S(2)}) collective-permute-start(bf16[256,256]{1,0:T(8,128)(2,1)S(1)} %get-tuple-element.87.mine), channel_id=1, source_target_pairs={{11,13},{7,9},{13,15},{27,29},{23,25},{29,31},{43,45},{39,41},{45,... | collective-permute-start | bytes 393224 | tf_op jit(solution)/shard_map/ppermute | solution.py:319
  19.6 2.7 %collective-permute-start.17 = (bf16[256,256]{1,0:T(8,128)(2,1)S(1)}, bf16[256,256]{1,0:T(8,128)(2,1)S(1)}, u32[]{:S(2)}, u32[]{:S(2)}) collective-permute-start(bf16[256,256]{1,0:T(8,128)(2,1)S(1)} %get-tuple-element.87.mine), channel_id=1, source_target_pairs={{11,15},{3,2},{5,4},{7,8},{27,31},{19,18},{21,20},{23,24},{43,47},... | collective-permute-start | bytes 393224 | tf_op jit(solution)/shard_map/ppermute | solution.py:319
  20.3 2.0 %collective-permute-start.16 = (bf16[256,256]{1,0:T(8,128)(2,1)S(1)}, bf16[256,256]{1,0:T(8,128)(2,1)S(1)}, u32[]{:S(2)}, u32[]{:S(2)}) collective-permute-start(bf16[256,256]{1,0:T(8,128)(2,1)S(1)} %get-tuple-element.89), channel_id=1, source_target_pairs={{13,15},{9,11},{29,31},{25,27},{45,47},{41,43},{61,63},{57,59},{77... | collective-permute-start | bytes 393224 | tf_op jit(solution)/shard_map/ppermute | solution.py:319
  21.0 24.1 %collective-permute-start.15 = (bf16[256,256]{1,0:T(8,128)(2,1)S(1)}, bf16[256,256]{1,0:T(8,128)(2,1)S(1)}, u32[]{:S(2)}, u32[]{:S(2)}) collective-permute-start(bf16[256,256]{1,0:T(8,128)(2,1)S(1)} %get-tuple-element.89), channel_id=1, source_target_pairs={{13,14},{9,10},{11,12},{7,6},{29,30},{25,26},{27,28},{23,22},{45,4... | collective-permute-start | bytes 393224 | tf_op jit(solution)/shard_map/ppermute | solution.py:319

commit v5 on v4

--- a/solution.py
+++ b/solution.py
@@ -228,24 +228,23 @@
         out[...] = coarse_step(upper, own_w)
 
 
-def again_end(even_rhs, rhs, even_w, own_w, got, _, out, solved):
-    @pl.when(either(place(), (11, 13)))
+def lead_base(base, own_w, lead, _, out, solved):
+    @pl.when(place() == 11)
+    def _():
+        out[...] = coarse_step(lead, own_w) - base[...]
+
+
+def again_end(even_rhs, rhs, even_w, own_w, base, early3, early4, mine, got, _, out, solved):
+    me = place()
+
+    @pl.when(either(me, (11, 13)))
     def _():
         value = both_steps(even_rhs, rhs, even_w, own_w, got)
+        value = value + jnp.where(me == 11, base[...], 0.0)
         solved[...] = value
         out[...] = value.astype(BF16)
 
-
-def lead_step(got, base, own_w, early3, early4, mine, behind, _, out, solved):
-    me = place()
-
-    @pl.when(me == 11)
-    def _():
-        value = coarse_step(got, own_w) + (solved[...] - base[...])
-        solved[...] = value
-        out[...] = value.astype(BF16)
-
-    for owner, source in ((3, early3), (5, early4), (7, mine), (13, behind)):
+    for owner, source in ((3, early3), (5, early4), (7, mine)):
 
         @pl.when(me == owner)
         def _():
@@ -412,8 +411,8 @@
     )
     got5_rest = send(c9, [(9, 11), (11, 13)])
     base = chained(coarse_base, [upper_prev, own_w], "coarse_base", 1, wide)
-    c13 = chained(again_end, [*both, got5_rest], "again_end_rest", 2)
-    z3 = chained(lead_step, [got6, base, own_w, got3, got4, z2, c13], "coarse_lead", 1)
+    base = chained(lead_base, [base, own_w, got6], "lead_base", 10, wide)
+    z3 = chained(again_end, [*both, base, got3, got4, z2, got5_rest], "again_end_rest", 2)
     got7 = send(z3, [(11, 13), (7, 9), (13, 15)])
     got7b = send(z3, [(11, 15), (3, 2), (5, 4), (7, 8)])
     c13 = chained(lead_two_steps, [got7, z3, got5, *both], "final_lead", 2)

time: 47.9 us -> 46.5 us (0.971)
  waiting for transfers between devices: 23.5 us -> 21.6 us
    ppermute x18, waiting for transfers between devices: 23.5 us -> 21.6 us  [send(): return lax.ppermute(value, 'layer', pairs)]
  transfers between devices with their start and end apart: 18 -> 18, of which waited for: 3 -> 3; matrix products, arithmetic and copies ran while one was open for 0% -> 0% of each run, Pallas kernels for 12% -> 13%
where the time goes in v5:
time: 46.5 us; the launch traced here: 45.7 us
  waiting for transfers between devices  21.6 us (46%)
  starting transfers between devices  15.2 us (33%)
  Pallas kernels  8.3 us (18%)
  between operations  0.54 us (1%)
    ppermute x18, waiting for transfers between devices, send(): return lax.ppermute(value, 'layer', pairs)  21.6 us
    ppermute x18, starting transfers between devices, send(): return lax.ppermute(value, 'layer', pairs)  15.2 us
    pallas_call x20, Pallas kernels, kernel_call(): pl.pallas_call(body, out_shape=outs, in_specs=[pl.BlockSpec(memory_space=...  8.3 us
  transfers between devices with their start and end apart: 18, of which 3 were waited for; matrix products, arithmetic and copies ran while one was open for 0% of the time, Pallas kernels for 13%

profile of v5, /device:TPU:248, one launch (start us, length us, event | category | flops | bytes accessed | tf_op | source)
XLA Modules:
  0.0 45.7 jit_solution(17340596840117115407)
XLA Ops:
  0.1 1.3 %collective-permute-start = (bf16[256,256]{1,0:T(8,128)(2,1)S(1)}, bf16[256,256]{1,0:T(8,128)(2,1)S(1)}, u32[]{:S(2)}, u32[]{:S(2)}) collective-permute-start(bf16[256,256]{1,0:T(8,128)(2,1)S(1)} %get-tuple-element.48.refs_6_), channel_id=1, source_target_pairs={{1,2},{3,4},{5,6},{7,8},{9,10},{11,12},{13,14},{17,18},{19,20},{21... | collective-permute-start | bytes 393224 | tf_op jit(solution)/shard_map/ppermute | solution.py:318
  1.4 3.7 %first_sweep_even.1 = (bf16[256,256]{1,0:T(8,128)(2,1)S(1)}, bf16[256,2304]{1,0:T(8,128)(2,1)S(1)}, bf16[3,256,2304]{2,1,0:T(8,128)(2,1)S(1)}, f32[256,256]{1,0:T(8,128)S(1)}) custom-call(f32[256,256]{1,0:T(8,128)} %inputs.1, f32[1,256,256]{2,1,0:T(8,128)} %refs_1_.3, ...), custom_call_target="tpu_custom_call", output_to_operand_aliasing={{1}: (3, {}), {2}: (4, {}), {3}: (5, {})} | custom-call | flops 1207959552 | bytes 1048576 | tf_op jit(solution)/shard_map/first_sweep_even/pallas_call | solution.py:58
  5.0 1.3 %collective-permute-start.1 = (bf16[256,256]{1,0:T(8,128)(2,1)S(1)}, bf16[256,256]{1,0:T(8,128)(2,1)S(1)}, u32[]{:S(2)}, u32[]{:S(2)}) collective-permute-start(bf16[256,256]{1,0:T(8,128)(2,1)S(1)} %get-tuple-element.57), channel_id=1, source_target_pairs={{0,1},{2,3},{4,5},{6,7},{8,9},{10,11},{12,13},{14,15},{16,17},{18,... | collective-permute-start | bytes 393224 | tf_op jit(solution)/shard_map/ppermute | solution.py:318
  6.3 1.4 %collective-permute-start.3 = (bf16[256,2304]{1,0:T(8,128)(2,1)S(1)}, bf16[256,2304]{1,0:T(8,128)(2,1)S(1)}, u32[]{:S(2)}, u32[]{:S(2)}) collective-permute-start(bf16[256,2304]{1,0:T(8,128)(2,1)S(1)} %get-tuple-element.54.own_w), channel_id=1, source_target_pairs={{0,1},{2,3},{4,5},{6,7},{8,9},{10,11},{12,13},{14,15},{16,17},{18,... | collective-permute-start | bytes 3538952 | tf_op jit(solution)/shard_map/ppermute | solution.py:318
  7.7 0.3 collective-permute-done.refs_0_
  8.0 0.0 collective-permute-done.1.left_odd
  8.0 0.7 %collective-permute-start.5 = (bf16[256,256]{1,0:T(8,128)(2,1)S(1)}, bf16[256,256]{1,0:T(8,128)(2,1)S(1)}, u32[]{:S(2)}, u32[]{:S(2)}) collective-permute-start(bf16[256,256]{1,0:T(8,128)(2,1)S(1)} %get-tuple-element.65), channel_id=1, source_target_pairs={{1,3},{17,19},{33,35},{49,51},{65,67},{81,83},{97,99},{113,115},{1... | collective-permute-start | bytes 393224 | tf_op jit(solution)/shard_map/ppermute | solution.py:318
  8.6 1.9 %second_sweep_even.1 = (f32[256,256]{1,0:T(8,128)S(1)}, f32[256,256]{1,0:T(8,128)S(1)}, f32[256,256]{1,0:T(8,128)S(1)}, f32[256,256]{1,0:T(8,128)S(1)}) custom-call(bf16[256,256]{1,0:T(8,128)(2,1)S(1)} %get-tuple-element.53.left_even, bf16[256,2304]{1,0:T(8,128)(2,1)S(1)} %get-tuple-element.54.own_w, ...), custom_call_target="tpu_custom_call", output_to_operand_aliasing={{2}: (4, {}), {3}: (5, {})} | custom-call | flops 1207959552 | bytes 1048576 | tf_op jit(solution)/shard_map/second_sweep_even/pallas_call | solution.py:58
  10.5 1.3 %collective-permute-start.2 = (f32[256,256]{1,0:T(8,128)S(1)}, f32[256,256]{1,0:T(8,128)S(1)}, u32[]{:S(2)}, u32[]{:S(2)}) collective-permute-start(f32[256,256]{1,0:T(8,128)S(1)} %get-tuple-element.60.rhs_of_even), channel_id=1, source_target_pairs={{0,1},{2,3},{4,5},{6,7},{8,9},{10,11},{12,13},{14,15},{16,17},{18,... | collective-permute-start | bytes 786440 | tf_op jit(solution)/shard_map/ppermute | solution.py:318
  11.9 0.7 %collective-permute-start.4 = (f32[256,256]{1,0:T(8,128)S(1)}, f32[256,256]{1,0:T(8,128)S(1)}, u32[]{:S(2)}, u32[]{:S(2)}) collective-permute-start(f32[256,256]{1,0:T(8,128)S(1)} %get-tuple-element.64), channel_id=1, source_target_pairs={{4,5},{8,9},{20,21},{24,25},{36,37},{40,41},{52,53},{56,57},{68,69... | collective-permute-start | bytes 786440 | tf_op jit(solution)/shard_map/ppermute | solution.py:318
  12.6 0.0 collective-permute-done.3.even_w
  12.6 0.4 collective-permute-done.2.even_rhs
  13.0 0.7 %collective-permute-start.7 = (bf16[256,256]{1,0:T(8,128)(2,1)S(1)}, bf16[256,256]{1,0:T(8,128)(2,1)S(1)}, u32[]{:S(2)}, u32[]{:S(2)}) collective-permute-start(bf16[256,256]{1,0:T(8,128)(2,1)S(1)} %get-tuple-element.71), channel_id=1, source_target_pairs={{3,5},{19,21},{35,37},{51,53},{67,69},{83,85},{99,101},{115,117},{... | collective-permute-start | bytes 393224 | tf_op jit(solution)/shard_map/ppermute | solution.py:318
  13.7 0.0 collective-permute-done.4.first
  13.7 0.7 %collective-permute-start.6 = (bf16[256,256]{1,0:T(8,128)(2,1)S(1)}, bf16[256,256]{1,0:T(8,128)(2,1)S(1)}, u32[]{:S(2)}, u32[]{:S(2)}) collective-permute-start(bf16[256,256]{1,0:T(8,128)(2,1)S(1)} %get-tuple-element.70), channel_id=1, source_target_pairs={{5,7},{21,23},{37,39},{53,55},{69,71},{85,87},{101,103},{117,119},... | collective-permute-start | bytes 393224 | tf_op jit(solution)/shard_map/ppermute | solution.py:318
  14.4 0.7 %collective-permute-start.9 = (bf16[256,256]{1,0:T(8,128)(2,1)S(1)}, bf16[256,256]{1,0:T(8,128)(2,1)S(1)}, u32[]{:S(2)}, u32[]{:S(2)}) collective-permute-start(bf16[256,256]{1,0:T(8,128)(2,1)S(1)} %get-tuple-element.70), channel_id=1, source_target_pairs={{9,11},{25,27},{41,43},{57,59},{73,75},{89,91},{105,107},{121,123}... | collective-permute-start | bytes 393224 | tf_op jit(solution)/shard_map/ppermute | solution.py:318
  15.0 0.0 collective-permute-done.7.got.early4.got4
  15.1 0.2 again_lead.1
  15.3 0.7 %collective-permute-start.11 = (bf16[256,256]{1,0:T(8,128)(2,1)S(1)}, bf16[256,256]{1,0:T(8,128)(2,1)S(1)}, u32[]{:S(2)}, u32[]{:S(2)}) collective-permute-start(bf16[256,256]{1,0:T(8,128)(2,1)S(1)} %get-tuple-element.77), channel_id=1, source_target_pairs={{5,7},{21,23},{37,39},{53,55},{69,71},{85,87},{101,103},{117,119},... | collective-permute-start | bytes 393224 | tf_op jit(solution)/shard_map/ppermute | solution.py:318
  15.9 0.0 collective-permute-done.6.got
  16.0 0.7 %collective-permute-start.10 = (bf16[256,256]{1,0:T(8,128)(2,1)S(1)}, bf16[256,256]{1,0:T(8,128)(2,1)S(1)}, u32[]{:S(2)}, u32[]{:S(2)}) collective-permute-start(bf16[256,256]{1,0:T(8,128)(2,1)S(1)} %get-tuple-element.74), channel_id=1, source_target_pairs={{7,9},{23,25},{39,41},{55,57},{71,73},{87,89},{103,105},{119,121},... | collective-permute-start | bytes 393224 | tf_op jit(solution)/shard_map/ppermute | solution.py:318
  16.6 0.7 %collective-permute-start.8 = (bf16[256,256]{1,0:T(8,128)(2,1)S(1)}, bf16[256,256]{1,0:T(8,128)(2,1)S(1)}, u32[]{:S(2)}, u32[]{:S(2)}) collective-permute-start(bf16[256,256]{1,0:T(8,128)(2,1)S(1)} %get-tuple-element.74), channel_id=1, source_target_pairs={{7,11},{23,27},{39,43},{55,59},{71,75},{87,91},{103,107},{119,123}... | collective-permute-start | bytes 393224 | tf_op jit(solution)/shard_map/ppermute | solution.py:318
  17.3 0.0 collective-permute-done.9.got
  17.4 0.0 collective-permute-done.11.got.early5.got5
  17.4 0.7 %collective-permute-start.12 = (bf16[256,256]{1,0:T(8,128)(2,1)S(1)}, bf16[256,256]{1,0:T(8,128)(2,1)S(1)}, u32[]{:S(2)}, u32[]{:S(2)}) collective-permute-start(bf16[256,256]{1,0:T(8,128)(2,1)S(1)} %get-tuple-element.82.mine), channel_id=1, source_target_pairs={{7,11},{11,15},{23,27},{27,31},{39,43},{43,47},{55,59},{59,63},{71... | collective-permute-start | bytes 393224 | tf_op jit(solution)/shard_map/ppermute | solution.py:318
  18.1 0.7 %collective-permute-start.13 = (bf16[256,256]{1,0:T(8,128)(2,1)S(1)}, bf16[256,256]{1,0:T(8,128)(2,1)S(1)}, u32[]{:S(2)}, u32[]{:S(2)}) collective-permute-start(bf16[256,256]{1,0:T(8,128)(2,1)S(1)} %get-tuple-element.85), channel_id=1, source_target_pairs={{9,11},{11,13},{25,27},{27,29},{41,43},{43,45},{57,59},{59,61},{73... | collective-permute-start | bytes 393224 | tf_op jit(solution)/shard_map/ppermute | solution.py:318
  18.9 0.7 %collective-permute-start.14 = (bf16[256,256]{1,0:T(8,128)(2,1)S(1)}, bf16[256,256]{1,0:T(8,128)(2,1)S(1)}, u32[]{:S(2)}, u32[]{:S(2)}) collective-permute-start(bf16[256,256]{1,0:T(8,128)(2,1)S(1)} %get-tuple-element.87.mine), channel_id=1, source_target_pairs={{11,13},{7,9},{13,15},{27,29},{23,25},{29,31},{43,45},{39,41},{45,... | collective-permute-start | bytes 393224 | tf_op jit(solution)/shard_map/ppermute | solution.py:318
  19.6 0.7 %collective-permute-start.17 = (bf16[256,256]{1,0:T(8,128)(2,1)S(1)}, bf16[256,256]{1,0:T(8,128)(2,1)S(1)}, u32[]{:S(2)}, u32[]{:S(2)}) collective-permute-start(bf16[256,256]{1,0:T(8,128)(2,1)S(1)} %get-tuple-element.87.mine), channel_id=1, source_target_pairs={{11,15},{3,2},{5,4},{7,8},{27,31},{19,18},{21,20},{23,24},{43,47},... | collective-permute-start | bytes 393224 | tf_op jit(solution)/shard_map/ppermute | solution.py:318
  20.3 0.7 %collective-permute-start.16 = (bf16[256,256]{1,0:T(8,128)(2,1)S(1)}, bf16[256,256]{1,0:T(8,128)(2,1)S(1)}, u32[]{:S(2)}, u32[]{:S(2)}) collective-permute-start(bf16[256,256]{1,0:T(8,128)(2,1)S(1)} %get-tuple-element.89), channel_id=1, source_target_pairs={{13,15},{9,11},{29,31},{25,27},{45,47},{41,43},{61,63},{57,59},{77... | collective-permute-start | bytes 393224 | tf_op jit(solution)/shard_map/ppermute | solution.py:318
  21.0 1.3 %collective-permute-start.15 = (bf16[256,256]{1,0:T(8,128)(2,1)S(1)}, bf16[256,256]{1,0:T(8,128)(2,1)S(1)}, u32[]{:S(2)}, u32[]{:S(2)}) collective-permute-start(bf16[256,256]{1,0:T(8,128)(2,1)S(1)} %get-tuple-element.89), channel_id=1, source_target_pairs={{13,14},{9,10},{11,12},{7,6},{29,30},{25,26},{27,28},{23,22},{45,4... | collective-permute-start | bytes 393224 | tf_op jit(solution)/shard_map/ppermute | solution.py:318
  22.3 20.9 %collective-permute-done.15.got8b = bf16[256,256]{1,0:T(8,128)(2,1)S(1)} collective-permute-done((bf16[256,256]{1,0:T(8,128)(2,1)S(1)}, bf16[256,256]{1,0:T(8,128)(2,1)S(1)}, u32[]{:S(2)}, u32[]{:S(2)}) %collective-permute-start.15) | collective-permute-done | bytes 131104 | tf_op jit(solution)/shard_map/ppermute | solution.py:318
  43.3 2.3 %last_sweep.1 = f32[4,256,256]{2,1,0:T(8,128)} custom-call(f32[256,256]{1,0:T(8,128)S(1)} %get-tuple-element.59.start, bf16[256,256]{1,0:T(8,128)(2,1)S(1)} %collective-permute-done.15.got8b, bf16[256,256]{1,0:T(8,128)(2,1)S(1)} %collective-permute-done.16.got8, bf16[256,256]{1,0:T(8,128)(2,1)S(1)} %collective-permute-done.5.got.early3.got3, ...), custom_call_target="tpu_custom_call" | custom-call | flops 1207959552 | bytes 1048576 | tf_op jit(solution)/shard_map/last_sweep/pallas_call | solution.py:58
  (24 shorter events, 0.3 us)
Async XLA Ops:
  0.1 7.9 %collective-permute-start = (bf16[256,256]{1,0:T(8,128)(2,1)S(1)}, bf16[256,256]{1,0:T(8,128)(2,1)S(1)}, u32[]{:S(2)}, u32[]{:S(2)}) collective-permute-start(bf16[256,256]{1,0:T(8,128)(2,1)S(1)} %get-tuple-element.48.refs_6_), channel_id=1, source_target_pairs={{1,2},{3,4},{5,6},{7,8},{9,10},{11,12},{13,14},{17,18},{19,20},{21... | collective-permute-start | bytes 393224 | tf_op jit(solution)/shard_map/ppermute | solution.py:318
  5.0 3.0 %collective-permute-start.1 = (bf16[256,256]{1,0:T(8,128)(2,1)S(1)}, bf16[256,256]{1,0:T(8,128)(2,1)S(1)}, u32[]{:S(2)}, u32[]{:S(2)}) collective-permute-start(bf16[256,256]{1,0:T(8,128)(2,1)S(1)} %get-tuple-element.57), channel_id=1, source_target_pairs={{0,1},{2,3},{4,5},{6,7},{8,9},{10,11},{12,13},{14,15},{16,17},{18,... | collective-permute-start | bytes 393224 | tf_op jit(solution)/shard_map/ppermute | solution.py:318
  6.3 6.3 %collective-permute-start.3 = (bf16[256,2304]{1,0:T(8,128)(2,1)S(1)}, bf16[256,2304]{1,0:T(8,128)(2,1)S(1)}, u32[]{:S(2)}, u32[]{:S(2)}) collective-permute-start(bf16[256,2304]{1,0:T(8,128)(2,1)S(1)} %get-tuple-element.54.own_w), channel_id=1, source_target_pairs={{0,1},{2,3},{4,5},{6,7},{8,9},{10,11},{12,13},{14,15},{16,17},{18,... | collective-permute-start | bytes 3538952 | tf_op jit(solution)/shard_map/ppermute | solution.py:318
  8.0 4.6 %collective-permute-start.5 = (bf16[256,256]{1,0:T(8,128)(2,1)S(1)}, bf16[256,256]{1,0:T(8,128)(2,1)S(1)}, u32[]{:S(2)}, u32[]{:S(2)}) collective-permute-start(bf16[256,256]{1,0:T(8,128)(2,1)S(1)} %get-tuple-element.65), channel_id=1, source_target_pairs={{1,3},{17,19},{33,35},{49,51},{65,67},{81,83},{97,99},{113,115},{1... | collective-permute-start | bytes 393224 | tf_op jit(solution)/shard_map/ppermute | solution.py:318
  10.5 2.4 %collective-permute-start.2 = (f32[256,256]{1,0:T(8,128)S(1)}, f32[256,256]{1,0:T(8,128)S(1)}, u32[]{:S(2)}, u32[]{:S(2)}) collective-permute-start(f32[256,256]{1,0:T(8,128)S(1)} %get-tuple-element.60.rhs_of_even), channel_id=1, source_target_pairs={{0,1},{2,3},{4,5},{6,7},{8,9},{10,11},{12,13},{14,15},{16,17},{18,... | collective-permute-start | bytes 786440 | tf_op jit(solution)/shard_map/ppermute | solution.py:318
  11.9 1.8 %collective-permute-start.4 = (f32[256,256]{1,0:T(8,128)S(1)}, f32[256,256]{1,0:T(8,128)S(1)}, u32[]{:S(2)}, u32[]{:S(2)}) collective-permute-start(f32[256,256]{1,0:T(8,128)S(1)} %get-tuple-element.64), channel_id=1, source_target_pairs={{4,5},{8,9},{20,21},{24,25},{36,37},{40,41},{52,53},{56,57},{68,69... | collective-permute-start | bytes 786440 | tf_op jit(solution)/shard_map/ppermute | solution.py:318
  13.0 2.1 %collective-permute-start.7 = (bf16[256,256]{1,0:T(8,128)(2,1)S(1)}, bf16[256,256]{1,0:T(8,128)(2,1)S(1)}, u32[]{:S(2)}, u32[]{:S(2)}) collective-permute-start(bf16[256,256]{1,0:T(8,128)(2,1)S(1)} %get-tuple-element.71), channel_id=1, source_target_pairs={{3,5},{19,21},{35,37},{51,53},{67,69},{83,85},{99,101},{115,117},{... | collective-permute-start | bytes 393224 | tf_op jit(solution)/shard_map/ppermute | solution.py:318
  13.7 2.2 %collective-permute-start.6 = (bf16[256,256]{1,0:T(8,128)(2,1)S(1)}, bf16[256,256]{1,0:T(8,128)(2,1)S(1)}, u32[]{:S(2)}, u32[]{:S(2)}) collective-permute-start(bf16[256,256]{1,0:T(8,128)(2,1)S(1)} %get-tuple-element.70), channel_id=1, source_target_pairs={{5,7},{21,23},{37,39},{53,55},{69,71},{85,87},{101,103},{117,119},... | collective-permute-start | bytes 393224 | tf_op jit(solution)/shard_map/ppermute | solution.py:318
  14.4 3.0 %collective-permute-start.9 = (bf16[256,256]{1,0:T(8,128)(2,1)S(1)}, bf16[256,256]{1,0:T(8,128)(2,1)S(1)}, u32[]{:S(2)}, u32[]{:S(2)}) collective-permute-start(bf16[256,256]{1,0:T(8,128)(2,1)S(1)} %get-tuple-element.70), channel_id=1, source_target_pairs={{9,11},{25,27},{41,43},{57,59},{73,75},{89,91},{105,107},{121,123}... | collective-permute-start | bytes 393224 | tf_op jit(solution)/shard_map/ppermute | solution.py:318
  15.3 2.1 %collective-permute-start.11 = (bf16[256,256]{1,0:T(8,128)(2,1)S(1)}, bf16[256,256]{1,0:T(8,128)(2,1)S(1)}, u32[]{:S(2)}, u32[]{:S(2)}) collective-permute-start(bf16[256,256]{1,0:T(8,128)(2,1)S(1)} %get-tuple-element.77), channel_id=1, source_target_pairs={{5,7},{21,23},{37,39},{53,55},{69,71},{85,87},{101,103},{117,119},... | collective-permute-start | bytes 393224 | tf_op jit(solution)/shard_map/ppermute | solution.py:318
  16.0 2.1 %collective-permute-start.10 = (bf16[256,256]{1,0:T(8,128)(2,1)S(1)}, bf16[256,256]{1,0:T(8,128)(2,1)S(1)}, u32[]{:S(2)}, u32[]{:S(2)}) collective-permute-start(bf16[256,256]{1,0:T(8,128)(2,1)S(1)} %get-tuple-element.74), channel_id=1, source_target_pairs={{7,9},{23,25},{39,41},{55,57},{71,73},{87,89},{103,105},{119,121},... | collective-permute-start | bytes 393224 | tf_op jit(solution)/shard_map/ppermute | solution.py:318
  16.6 2.1 %collective-permute-start.8 = (bf16[256,256]{1,0:T(8,128)(2,1)S(1)}, bf16[256,256]{1,0:T(8,128)(2,1)S(1)}, u32[]{:S(2)}, u32[]{:S(2)}) collective-permute-start(bf16[256,256]{1,0:T(8,128)(2,1)S(1)} %get-tuple-element.74), channel_id=1, source_target_pairs={{7,11},{23,27},{39,43},{55,59},{71,75},{87,91},{103,107},{119,123}... | collective-permute-start | bytes 393224 | tf_op jit(solution)/shard_map/ppermute | solution.py:318
  17.4 1.4 %collective-permute-start.12 = (bf16[256,256]{1,0:T(8,128)(2,1)S(1)}, bf16[256,256]{1,0:T(8,128)(2,1)S(1)}, u32[]{:S(2)}, u32[]{:S(2)}) collective-permute-start(bf16[256,256]{1,0:T(8,128)(2,1)S(1)} %get-tuple-element.82.mine), channel_id=1, source_target_pairs={{7,11},{11,15},{23,27},{27,31},{39,43},{43,47},{55,59},{59,63},{71... | collective-permute-start | bytes 393224 | tf_op jit(solution)/shard_map/ppermute | solution.py:318
  18.1 0.7 %collective-permute-start.13 = (bf16[256,256]{1,0:T(8,128)(2,1)S(1)}, bf16[256,256]{1,0:T(8,128)(2,1)S(1)}, u32[]{:S(2)}, u32[]{:S(2)}) collective-permute-start(bf16[256,256]{1,0:T(8,128)(2,1)S(1)} %get-tuple-element.85), channel_id=1, source_target_pairs={{9,11},{11,13},{25,27},{27,29},{41,43},{43,45},{57,59},{59,61},{73... | collective-permute-start | bytes 393224 | tf_op jit(solution)/shard_map/ppermute | solution.py:318
  18.9 1.4 %collective-permute-start.14 = (bf16[256,256]{1,0:T(8,128)(2,1)S(1)}, bf16[256,256]{1,0:T(8,128)(2,1)S(1)}, u32[]{:S(2)}, u32[]{:S(2)}) collective-permute-start(bf16[256,256]{1,0:T(8,128)(2,1)S(1)} %get-tuple-element.87.mine), channel_id=1, source_target_pairs={{11,13},{7,9},{13,15},{27,29},{23,25},{29,31},{43,45},{39,41},{45,... | collective-permute-start | bytes 393224 | tf_op jit(solution)/shard_map/ppermute | solution.py:318
  19.6 2.7 %collective-permute-start.17 = (bf16[256,256]{1,0:T(8,128)(2,1)S(1)}, bf16[256,256]{1,0:T(8,128)(2,1)S(1)}, u32[]{:S(2)}, u32[]{:S(2)}) collective-permute-start(bf16[256,256]{1,0:T(8,128)(2,1)S(1)} %get-tuple-element.87.mine), channel_id=1, source_target_pairs={{11,15},{3,2},{5,4},{7,8},{27,31},{19,18},{21,20},{23,24},{43,47},... | collective-permute-start | bytes 393224 | tf_op jit(solution)/shard_map/ppermute | solution.py:318
  20.3 2.0 %collective-permute-start.16 = (bf16[256,256]{1,0:T(8,128)(2,1)S(1)}, bf16[256,256]{1,0:T(8,128)(2,1)S(1)}, u32[]{:S(2)}, u32[]{:S(2)}) collective-permute-start(bf16[256,256]{1,0:T(8,128)(2,1)S(1)} %get-tuple-element.89), channel_id=1, source_target_pairs={{13,15},{9,11},{29,31},{25,27},{45,47},{41,43},{61,63},{57,59},{77... | collective-permute-start | bytes 393224 | tf_op jit(solution)/shard_map/ppermute | solution.py:318
  21.0 22.3 %collective-permute-start.15 = (bf16[256,256]{1,0:T(8,128)(2,1)S(1)}, bf16[256,256]{1,0:T(8,128)(2,1)S(1)}, u32[]{:S(2)}, u32[]{:S(2)}) collective-permute-start(bf16[256,256]{1,0:T(8,128)(2,1)S(1)} %get-tuple-element.89), channel_id=1, source_target_pairs={{13,14},{9,10},{11,12},{7,6},{29,30},{25,26},{27,28},{23,22},{45,4... | collective-permute-start | bytes 393224 | tf_op jit(solution)/shard_map/ppermute | solution.py:318

commit v6 on v5

--- a/solution.py
+++ b/solution.py
@@ -214,12 +214,12 @@
     return value + 4.0 * conv_tanh(value, own_w)
 
 
-def steps_or_copy(owner, keep, upper, even_rhs, rhs, even_w, own_w, got, _, out, solved):
-    two_steps((owner,), keep, even_rhs, rhs, even_w, own_w, got, _, out, solved)
-
-    @pl.when(place() == 11)
-    def _():
-        out[...] = upper[...]
+def steps_or_copy(owner, copier, other, even_rhs, rhs, even_w, own_w, got, _, out, solved):
+    two_steps((owner,), False, even_rhs, rhs, even_w, own_w, got, _, out, solved)
+
+    @pl.when(place() == copier)
+    def _():
+        out[...] = other[...]
 
 
 def coarse_base(upper, own_w, _, out, solved):
@@ -251,8 +251,9 @@
             out[...] = source[...]
 
 
-def lead_two_steps(got, mine, early5, even_rhs, rhs, even_w, own_w, _, out, solved):
-    two_steps((9, 13), False, even_rhs, rhs, even_w, own_w, got, _, out, solved)
+def lead_two_steps(mine, early5, even_rhs, rhs, even_w, own_w, rest, got, _, out, solved):
+    two_steps((9,), False, even_rhs, rhs, even_w, own_w, rest, _, out, solved)
+    two_steps((13,), False, even_rhs, rhs, even_w, own_w, got, _, out, solved)
     for owner, source in ((11, mine), (7, early5)):
 
         @pl.when(place() == owner)
@@ -268,7 +269,7 @@
 
 
 def last_sweep(
-    start, got8b, got8, got3, got4, got5, got7, got7b,
+    start, got8b, got8, got3, got4, got5, got6, got7, got7b,
     even_rhs, rhs, even_w, own_w, rhs_of_even, later_w, solved, states, left, ready, sems,
 ):
     me = place()
@@ -279,7 +280,8 @@
         (got3, (3,)),
         (got4, (5,)),
         (got5, (7,)),
-        (got7, (9, 13)),
+        (got6, (9,)),
+        (got7, (13,)),
         (got8, (11, 15)),
     )
     for source, owners in sources:
@@ -401,30 +403,34 @@
     upper7 = pair((7,), False, got3_rest, "relax_rest")
     got4_rest = send(upper7, [(7, 9)])
     upper_prev = send(upper7, [(7, 11)])
-    upper11 = pair((11,), False, got3_last, "relax_last")
-    z2 = chained(
-        functools.partial(steps_or_copy, 7, True), [upper11, *both, got5], "again_end_lead", 2
-    )
-    got6 = send(z2, [(7, 11), (11, 15)])
+    z2 = pair((7,), True, got5, "again_end_lead")
+    got6 = send(z2, [(7, 11)])
+    got4_rest, solved = kernel_call(
+        in_order, [narrow, wide], [got4_rest, solved], "upper_first", 10, aliases={0: 0, 1: 1}
+    )
+    upper11 = chained(
+        functools.partial(steps_or_copy, 11, 7), [z2, *both, got3_last], "relax_last", 2
+    )
+    got6_rest = send(upper11, [(7, 9), (11, 15)])
     c9 = chained(
-        functools.partial(steps_or_copy, 9, False), [upper11, *both, got4_rest], "again_rest", 2
+        functools.partial(steps_or_copy, 9, 11), [upper11, *both, got4_rest], "again_rest", 2
     )
     got5_rest = send(c9, [(9, 11), (11, 13)])
     base = chained(coarse_base, [upper_prev, own_w], "coarse_base", 1, wide)
-    base = chained(lead_base, [base, own_w, got6], "lead_base", 10, wide)
+    base = chained(lead_base, [base, own_w, got6], "lead_base", 2, wide)
     z3 = chained(again_end, [*both, base, got3, got4, z2, got5_rest], "again_end_rest", 2)
-    got7 = send(z3, [(11, 13), (7, 9), (13, 15)])
+    got7 = send(z3, [(11, 13), (13, 15)])
     got7b = send(z3, [(11, 15), (3, 2), (5, 4), (7, 8)])
-    c13 = chained(lead_two_steps, [got7, z3, got5, *both], "final_lead", 2)
+    c13 = chained(lead_two_steps, [z3, got5, *both, got6_rest, got7], "final_lead", 2)
     got8 = send(c13, [(13, 15), (9, 11)])
     got8b = send(c13, [(13, 14), (9, 10), (11, 12), (7, 6)])
     (solved,) = kernel_call(
-        end_step, [wide], [got6, *both, got7, got7b, solved], "coarse_end", 4, aliases={7: 0}
+        end_step, [wide], [got6_rest, *both, got7, got7b, solved], "coarse_end", 4, aliases={7: 0}
     )
     return kernel_call(
         last_sweep,
         [jax.ShapeDtypeStruct((COARSEN, CHANS, CELLS), F32)],
-        [start, got8b, got8, got3, got4, got5, got7, got7b, *both, rhs_of_even, later_w, solved],
+        [start, got8b, got8, got3, got4, got5, got6_rest, got7, got7b, *both, rhs_of_even, later_w, solved],
         "last_sweep",
         4,
         scratch=[

time: 46.5 us -> 46.2 us (level)
  starting transfers between devices: 15.2 us -> 15.9 us
  waiting for transfers between devices: 21.6 us -> 21 us
    ppermute x18 -> x19, starting transfers between devices: 15.2 us -> 15.9 us  [send(): return lax.ppermute(value, 'layer', pairs)]
    ppermute x18 -> x19, waiting for transfers between devices: 21.6 us -> 21 us  [send(): return lax.ppermute(value, 'layer', pairs)]
    pallas_call x20 -> x21, Pallas kernels: 8.3 us -> 8.32 us  [kernel_call(): pl.pallas_call(body, out_shape=outs, in_specs=[pl.BlockSpec(memory_space=...]
  transfers between devices with their start and end apart: 18 -> 19, of which waited for: 3 -> 3; matrix products, arithmetic and copies ran while one was open for 0% -> 0% of each run, Pallas kernels for 13% -> 13%
where the time goes in v6:
time: 46.2 us; the launch traced here: 45.8 us
  waiting for transfers between devices  21 us (45%)
  starting transfers between devices  15.9 us (34%)
  Pallas kernels  8.32 us (18%)
  between operations  0.57 us (1%)
    ppermute x19, waiting for transfers between devices, send(): return lax.ppermute(value, 'layer', pairs)  21 us
    ppermute x19, starting transfers between devices, send(): return lax.ppermute(value, 'layer', pairs)  15.9 us
    pallas_call x21, Pallas kernels, kernel_call(): pl.pallas_call(body, out_shape=outs, in_specs=[pl.BlockSpec(memory_space=...  8.32 us
  transfers between devices with their start and end apart: 19, of which 3 were waited for; matrix products, arithmetic and copies ran while one was open for 0% of the time, Pallas kernels for 13%

profile of v6, /device:TPU:248, one launch (start us, length us, event | category | flops | bytes accessed | tf_op | source)
XLA Modules:
  0.0 45.8 jit_solution(11585633365888851334)
XLA Ops:
  0.1 1.3 %collective-permute-start = (bf16[256,256]{1,0:T(8,128)(2,1)S(1)}, bf16[256,256]{1,0:T(8,128)(2,1)S(1)}, u32[]{:S(2)}, u32[]{:S(2)}) collective-permute-start(bf16[256,256]{1,0:T(8,128)(2,1)S(1)} %get-tuple-element.50.refs_6_), channel_id=1, source_target_pairs={{1,2},{3,4},{5,6},{7,8},{9,10},{11,12},{13,14},{17,18},{19,20},{21... | collective-permute-start | bytes 393224 | tf_op jit(solution)/shard_map/ppermute | solution.py:320
  1.4 3.7 %first_sweep_even.1 = (bf16[256,256]{1,0:T(8,128)(2,1)S(1)}, bf16[256,2304]{1,0:T(8,128)(2,1)S(1)}, bf16[3,256,2304]{2,1,0:T(8,128)(2,1)S(1)}, f32[256,256]{1,0:T(8,128)S(1)}) custom-call(f32[256,256]{1,0:T(8,128)} %inputs.1, f32[1,256,256]{2,1,0:T(8,128)} %refs_1_.3, ...), custom_call_target="tpu_custom_call", output_to_operand_aliasing={{1}: (3, {}), {2}: (4, {}), {3}: (5, {})} | custom-call | flops 1207959552 | bytes 1048576 | tf_op jit(solution)/shard_map/first_sweep_even/pallas_call | solution.py:58
  5.0 1.3 %collective-permute-start.1 = (bf16[256,256]{1,0:T(8,128)(2,1)S(1)}, bf16[256,256]{1,0:T(8,128)(2,1)S(1)}, u32[]{:S(2)}, u32[]{:S(2)}) collective-permute-start(bf16[256,256]{1,0:T(8,128)(2,1)S(1)} %get-tuple-element.59), channel_id=1, source_target_pairs={{0,1},{2,3},{4,5},{6,7},{8,9},{10,11},{12,13},{14,15},{16,17},{18,... | collective-permute-start | bytes 393224 | tf_op jit(solution)/shard_map/ppermute | solution.py:320
  6.3 1.4 %collective-permute-start.3 = (bf16[256,2304]{1,0:T(8,128)(2,1)S(1)}, bf16[256,2304]{1,0:T(8,128)(2,1)S(1)}, u32[]{:S(2)}, u32[]{:S(2)}) collective-permute-start(bf16[256,2304]{1,0:T(8,128)(2,1)S(1)} %get-tuple-element.56.own_w), channel_id=1, source_target_pairs={{0,1},{2,3},{4,5},{6,7},{8,9},{10,11},{12,13},{14,15},{16,17},{18,... | collective-permute-start | bytes 3538952 | tf_op jit(solution)/shard_map/ppermute | solution.py:320
  7.7 0.3 collective-permute-done.refs_0_
  8.0 0.0 collective-permute-done.1.left_odd
  8.0 0.7 %collective-permute-start.5 = (bf16[256,256]{1,0:T(8,128)(2,1)S(1)}, bf16[256,256]{1,0:T(8,128)(2,1)S(1)}, u32[]{:S(2)}, u32[]{:S(2)}) collective-permute-start(bf16[256,256]{1,0:T(8,128)(2,1)S(1)} %get-tuple-element.67), channel_id=1, source_target_pairs={{1,3},{17,19},{33,35},{49,51},{65,67},{81,83},{97,99},{113,115},{1... | collective-permute-start | bytes 393224 | tf_op jit(solution)/shard_map/ppermute | solution.py:320
  8.6 1.9 %second_sweep_even.1 = (f32[256,256]{1,0:T(8,128)S(1)}, f32[256,256]{1,0:T(8,128)S(1)}, f32[256,256]{1,0:T(8,128)S(1)}, f32[256,256]{1,0:T(8,128)S(1)}) custom-call(bf16[256,256]{1,0:T(8,128)(2,1)S(1)} %get-tuple-element.55.left_even, bf16[256,2304]{1,0:T(8,128)(2,1)S(1)} %get-tuple-element.56.own_w, ...), custom_call_target="tpu_custom_call", output_to_operand_aliasing={{2}: (4, {}), {3}: (5, {})} | custom-call | flops 1207959552 | bytes 1048576 | tf_op jit(solution)/shard_map/second_sweep_even/pallas_call | solution.py:58
  10.5 1.3 %collective-permute-start.2 = (f32[256,256]{1,0:T(8,128)S(1)}, f32[256,256]{1,0:T(8,128)S(1)}, u32[]{:S(2)}, u32[]{:S(2)}) collective-permute-start(f32[256,256]{1,0:T(8,128)S(1)} %get-tuple-element.62.rhs_of_even), channel_id=1, source_target_pairs={{0,1},{2,3},{4,5},{6,7},{8,9},{10,11},{12,13},{14,15},{16,17},{18,... | collective-permute-start | bytes 786440 | tf_op jit(solution)/shard_map/ppermute | solution.py:320
  11.9 0.7 %collective-permute-start.4 = (f32[256,256]{1,0:T(8,128)S(1)}, f32[256,256]{1,0:T(8,128)S(1)}, u32[]{:S(2)}, u32[]{:S(2)}) collective-permute-start(f32[256,256]{1,0:T(8,128)S(1)} %get-tuple-element.66), channel_id=1, source_target_pairs={{4,5},{8,9},{20,21},{24,25},{36,37},{40,41},{52,53},{56,57},{68,69... | collective-permute-start | bytes 786440 | tf_op jit(solution)/shard_map/ppermute | solution.py:320
  12.6 0.0 collective-permute-done.5.got.early3.got3
  12.6 0.4 collective-permute-done.2.even_rhs
  13.0 0.7 %collective-permute-start.7 = (bf16[256,256]{1,0:T(8,128)(2,1)S(1)}, bf16[256,256]{1,0:T(8,128)(2,1)S(1)}, u32[]{:S(2)}, u32[]{:S(2)}) collective-permute-start(bf16[256,256]{1,0:T(8,128)(2,1)S(1)} %get-tuple-element.73), channel_id=1, source_target_pairs={{3,5},{19,21},{35,37},{51,53},{67,69},{83,85},{99,101},{115,117},{... | collective-permute-start | bytes 393224 | tf_op jit(solution)/shard_map/ppermute | solution.py:320
  13.7 0.7 %collective-permute-start.6 = (bf16[256,256]{1,0:T(8,128)(2,1)S(1)}, bf16[256,256]{1,0:T(8,128)(2,1)S(1)}, u32[]{:S(2)}, u32[]{:S(2)}) collective-permute-start(bf16[256,256]{1,0:T(8,128)(2,1)S(1)} %get-tuple-element.72), channel_id=1, source_target_pairs={{5,7},{21,23},{37,39},{53,55},{69,71},{85,87},{101,103},{117,119},... | collective-permute-start | bytes 393224 | tf_op jit(solution)/shard_map/ppermute | solution.py:320
  14.4 0.2 again_lead.1
  14.6 0.7 %collective-permute-start.9 = (bf16[256,256]{1,0:T(8,128)(2,1)S(1)}, bf16[256,256]{1,0:T(8,128)(2,1)S(1)}, u32[]{:S(2)}, u32[]{:S(2)}) collective-permute-start(bf16[256,256]{1,0:T(8,128)(2,1)S(1)} %get-tuple-element.77), channel_id=1, source_target_pairs={{5,7},{21,23},{37,39},{53,55},{69,71},{85,87},{101,103},{117,119},... | collective-permute-start | bytes 393224 | tf_op jit(solution)/shard_map/ppermute | solution.py:320
  15.3 0.7 %collective-permute-start.11 = (bf16[256,256]{1,0:T(8,128)(2,1)S(1)}, bf16[256,256]{1,0:T(8,128)(2,1)S(1)}, u32[]{:S(2)}, u32[]{:S(2)}) collective-permute-start(bf16[256,256]{1,0:T(8,128)(2,1)S(1)} %get-tuple-element.76), channel_id=1, source_target_pairs={{7,9},{23,25},{39,41},{55,57},{71,73},{87,89},{103,105},{119,121},... | collective-permute-start | bytes 393224 | tf_op jit(solution)/shard_map/ppermute | solution.py:320
  16.0 0.7 %collective-permute-start.10 = (bf16[256,256]{1,0:T(8,128)(2,1)S(1)}, bf16[256,256]{1,0:T(8,128)(2,1)S(1)}, u32[]{:S(2)}, u32[]{:S(2)}) collective-permute-start(bf16[256,256]{1,0:T(8,128)(2,1)S(1)} %get-tuple-element.72), channel_id=1, source_target_pairs={{9,11},{25,27},{41,43},{57,59},{73,75},{89,91},{105,107},{121,123}... | collective-permute-start | bytes 393224 | tf_op jit(solution)/shard_map/ppermute | solution.py:320
  16.6 0.7 %collective-permute-start.8 = (bf16[256,256]{1,0:T(8,128)(2,1)S(1)}, bf16[256,256]{1,0:T(8,128)(2,1)S(1)}, u32[]{:S(2)}, u32[]{:S(2)}) collective-permute-start(bf16[256,256]{1,0:T(8,128)(2,1)S(1)} %get-tuple-element.76), channel_id=1, source_target_pairs={{7,11},{23,27},{39,43},{55,59},{71,75},{87,91},{103,107},{119,123}... | collective-permute-start | bytes 393224 | tf_op jit(solution)/shard_map/ppermute | solution.py:320
  17.4 0.7 %collective-permute-start.12 = (bf16[256,256]{1,0:T(8,128)(2,1)S(1)}, bf16[256,256]{1,0:T(8,128)(2,1)S(1)}, u32[]{:S(2)}, u32[]{:S(2)}) collective-permute-start(bf16[256,256]{1,0:T(8,128)(2,1)S(1)} %get-tuple-element.79.other.mine), channel_id=1, source_target_pairs={{7,11},{23,27},{39,43},{55,59},{71,75},{87,91},{103,107},{119,123}... | collective-permute-start | bytes 393224 | tf_op jit(solution)/shard_map/ppermute | solution.py:320
  18.0 0.0 collective-permute-done.10.got
  18.1 0.7 %collective-permute-start.13 = (bf16[256,256]{1,0:T(8,128)(2,1)S(1)}, bf16[256,256]{1,0:T(8,128)(2,1)S(1)}, u32[]{:S(2)}, u32[]{:S(2)}) collective-permute-start(bf16[256,256]{1,0:T(8,128)(2,1)S(1)} %get-tuple-element.89), channel_id=1, source_target_pairs={{9,11},{11,13},{25,27},{27,29},{41,43},{43,45},{57,59},{59,61},{73... | collective-permute-start | bytes 393224 | tf_op jit(solution)/shard_map/ppermute | solution.py:320
  18.8 0.7 %collective-permute-start.14 = (bf16[256,256]{1,0:T(8,128)(2,1)S(1)}, bf16[256,256]{1,0:T(8,128)(2,1)S(1)}, u32[]{:S(2)}, u32[]{:S(2)}) collective-permute-start(bf16[256,256]{1,0:T(8,128)(2,1)S(1)} %get-tuple-element.82.other), channel_id=1, source_target_pairs={{7,9},{11,15},{23,25},{27,31},{39,41},{43,47},{55,57},{59,63},{71,... | collective-permute-start | bytes 393224 | tf_op jit(solution)/shard_map/ppermute | solution.py:320
  19.5 0.0 collective-permute-done.8.upper
  19.5 0.0 collective-permute-done.13.got
  19.6 0.7 %collective-permute-start.15 = (bf16[256,256]{1,0:T(8,128)(2,1)S(1)}, bf16[256,256]{1,0:T(8,128)(2,1)S(1)}, u32[]{:S(2)}, u32[]{:S(2)}) collective-permute-start(bf16[256,256]{1,0:T(8,128)(2,1)S(1)} %get-tuple-element.91.mine), channel_id=1, source_target_pairs={{11,13},{13,15},{27,29},{29,31},{43,45},{45,47},{59,61},{61,63},{7... | collective-permute-start | bytes 393224 | tf_op jit(solution)/shard_map/ppermute | solution.py:320
  20.3 0.7 %collective-permute-start.18 = (bf16[256,256]{1,0:T(8,128)(2,1)S(1)}, bf16[256,256]{1,0:T(8,128)(2,1)S(1)}, u32[]{:S(2)}, u32[]{:S(2)}) collective-permute-start(bf16[256,256]{1,0:T(8,128)(2,1)S(1)} %get-tuple-element.91.mine), channel_id=1, source_target_pairs={{11,15},{3,2},{5,4},{7,8},{27,31},{19,18},{21,20},{23,24},{43,47},... | collective-permute-start | bytes 393224 | tf_op jit(solution)/shard_map/ppermute | solution.py:320
  20.9 0.0 collective-permute-done.14.rest.upper.got6
  21.0 0.7 %collective-permute-start.17 = (bf16[256,256]{1,0:T(8,128)(2,1)S(1)}, bf16[256,256]{1,0:T(8,128)(2,1)S(1)}, u32[]{:S(2)}, u32[]{:S(2)}) collective-permute-start(bf16[256,256]{1,0:T(8,128)(2,1)S(1)} %get-tuple-element.93), channel_id=1, source_target_pairs={{13,15},{9,11},{29,31},{25,27},{45,47},{41,43},{61,63},{57,59},{77... | collective-permute-start | bytes 393224 | tf_op jit(solution)/shard_map/ppermute | solution.py:320
  21.7 1.3 %collective-permute-start.16 = (bf16[256,256]{1,0:T(8,128)(2,1)S(1)}, bf16[256,256]{1,0:T(8,128)(2,1)S(1)}, u32[]{:S(2)}, u32[]{:S(2)}) collective-permute-start(bf16[256,256]{1,0:T(8,128)(2,1)S(1)} %get-tuple-element.93), channel_id=1, source_target_pairs={{13,14},{9,10},{11,12},{7,6},{29,30},{25,26},{27,28},{23,22},{45,4... | collective-permute-start | bytes 393224 | tf_op jit(solution)/shard_map/ppermute | solution.py:320
  23.0 20.3 %collective-permute-done.16.got8b = bf16[256,256]{1,0:T(8,128)(2,1)S(1)} collective-permute-done((bf16[256,256]{1,0:T(8,128)(2,1)S(1)}, bf16[256,256]{1,0:T(8,128)(2,1)S(1)}, u32[]{:S(2)}, u32[]{:S(2)}) %collective-permute-start.16) | collective-permute-done | bytes 131104 | tf_op jit(solution)/shard_map/ppermute | solution.py:320
  43.3 2.3 %last_sweep.1 = f32[4,256,256]{2,1,0:T(8,128)} custom-call(f32[256,256]{1,0:T(8,128)S(1)} %get-tuple-element.61.start, bf16[256,256]{1,0:T(8,128)(2,1)S(1)} %collective-permute-done.16.got8b, bf16[256,256]{1,0:T(8,128)(2,1)S(1)} %collective-permute-done.17.got8, bf16[256,256]{1,0:T(8,128)(2,1)S(1)} %collective-permute-done.5.got.early3.got3, ...), custom_call_target="tpu_custom_call" | custom-call | flops 1207959552 | bytes 1048576 | tf_op jit(solution)/shard_map/last_sweep/pallas_call | solution.py:58
  (27 shorter events, 0.3 us)
Async XLA Ops:
  0.1 7.9 %collective-permute-start = (bf16[256,256]{1,0:T(8,128)(2,1)S(1)}, bf16[256,256]{1,0:T(8,128)(2,1)S(1)}, u32[]{:S(2)}, u32[]{:S(2)}) collective-permute-start(bf16[256,256]{1,0:T(8,128)(2,1)S(1)} %get-tuple-element.50.refs_6_), channel_id=1, source_target_pairs={{1,2},{3,4},{5,6},{7,8},{9,10},{11,12},{13,14},{17,18},{19,20},{21... | collective-permute-start | bytes 393224 | tf_op jit(solution)/shard_map/ppermute | solution.py:320
  5.0 3.0 %collective-permute-start.1 = (bf16[256,256]{1,0:T(8,128)(2,1)S(1)}, bf16[256,256]{1,0:T(8,128)(2,1)S(1)}, u32[]{:S(2)}, u32[]{:S(2)}) collective-permute-start(bf16[256,256]{1,0:T(8,128)(2,1)S(1)} %get-tuple-element.59), channel_id=1, source_target_pairs={{0,1},{2,3},{4,5},{6,7},{8,9},{10,11},{12,13},{14,15},{16,17},{18,... | collective-permute-start | bytes 393224 | tf_op jit(solution)/shard_map/ppermute | solution.py:320
  6.3 6.3 %collective-permute-start.3 = (bf16[256,2304]{1,0:T(8,128)(2,1)S(1)}, bf16[256,2304]{1,0:T(8,128)(2,1)S(1)}, u32[]{:S(2)}, u32[]{:S(2)}) collective-permute-start(bf16[256,2304]{1,0:T(8,128)(2,1)S(1)} %get-tuple-element.56.own_w), channel_id=1, source_target_pairs={{0,1},{2,3},{4,5},{6,7},{8,9},{10,11},{12,13},{14,15},{16,17},{18,... | collective-permute-start | bytes 3538952 | tf_op jit(solution)/shard_map/ppermute | solution.py:320
  8.0 4.6 %collective-permute-start.5 = (bf16[256,256]{1,0:T(8,128)(2,1)S(1)}, bf16[256,256]{1,0:T(8,128)(2,1)S(1)}, u32[]{:S(2)}, u32[]{:S(2)}) collective-permute-start(bf16[256,256]{1,0:T(8,128)(2,1)S(1)} %get-tuple-element.67), channel_id=1, source_target_pairs={{1,3},{17,19},{33,35},{49,51},{65,67},{81,83},{97,99},{113,115},{1... | collective-permute-start | bytes 393224 | tf_op jit(solution)/shard_map/ppermute | solution.py:320
  10.5 2.4 %collective-permute-start.2 = (f32[256,256]{1,0:T(8,128)S(1)}, f32[256,256]{1,0:T(8,128)S(1)}, u32[]{:S(2)}, u32[]{:S(2)}) collective-permute-start(f32[256,256]{1,0:T(8,128)S(1)} %get-tuple-element.62.rhs_of_even), channel_id=1, source_target_pairs={{0,1},{2,3},{4,5},{6,7},{8,9},{10,11},{12,13},{14,15},{16,17},{18,... | collective-permute-start | bytes 786440 | tf_op jit(solution)/shard_map/ppermute | solution.py:320
  11.9 1.8 %collective-permute-start.4 = (f32[256,256]{1,0:T(8,128)S(1)}, f32[256,256]{1,0:T(8,128)S(1)}, u32[]{:S(2)}, u32[]{:S(2)}) collective-permute-start(f32[256,256]{1,0:T(8,128)S(1)} %get-tuple-element.66), channel_id=1, source_target_pairs={{4,5},{8,9},{20,21},{24,25},{36,37},{40,41},{52,53},{56,57},{68,69... | collective-permute-start | bytes 786440 | tf_op jit(solution)/shard_map/ppermute | solution.py:320
  13.0 1.4 %collective-permute-start.7 = (bf16[256,256]{1,0:T(8,128)(2,1)S(1)}, bf16[256,256]{1,0:T(8,128)(2,1)S(1)}, u32[]{:S(2)}, u32[]{:S(2)}) collective-permute-start(bf16[256,256]{1,0:T(8,128)(2,1)S(1)} %get-tuple-element.73), channel_id=1, source_target_pairs={{3,5},{19,21},{35,37},{51,53},{67,69},{83,85},{99,101},{115,117},{... | collective-permute-start | bytes 393224 | tf_op jit(solution)/shard_map/ppermute | solution.py:320
  13.7 1.6 %collective-permute-start.6 = (bf16[256,256]{1,0:T(8,128)(2,1)S(1)}, bf16[256,256]{1,0:T(8,128)(2,1)S(1)}, u32[]{:S(2)}, u32[]{:S(2)}) collective-permute-start(bf16[256,256]{1,0:T(8,128)(2,1)S(1)} %get-tuple-element.72), channel_id=1, source_target_pairs={{5,7},{21,23},{37,39},{53,55},{69,71},{85,87},{101,103},{117,119},... | collective-permute-start | bytes 393224 | tf_op jit(solution)/shard_map/ppermute | solution.py:320
  14.6 2.7 %collective-permute-start.9 = (bf16[256,256]{1,0:T(8,128)(2,1)S(1)}, bf16[256,256]{1,0:T(8,128)(2,1)S(1)}, u32[]{:S(2)}, u32[]{:S(2)}) collective-permute-start(bf16[256,256]{1,0:T(8,128)(2,1)S(1)} %get-tuple-element.77), channel_id=1, source_target_pairs={{5,7},{21,23},{37,39},{53,55},{69,71},{85,87},{101,103},{117,119},... | collective-permute-start | bytes 393224 | tf_op jit(solution)/shard_map/ppermute | solution.py:320
  15.3 2.7 %collective-permute-start.11 = (bf16[256,256]{1,0:T(8,128)(2,1)S(1)}, bf16[256,256]{1,0:T(8,128)(2,1)S(1)}, u32[]{:S(2)}, u32[]{:S(2)}) collective-permute-start(bf16[256,256]{1,0:T(8,128)(2,1)S(1)} %get-tuple-element.76), channel_id=1, source_target_pairs={{7,9},{23,25},{39,41},{55,57},{71,73},{87,89},{103,105},{119,121},... | collective-permute-start | bytes 393224 | tf_op jit(solution)/shard_map/ppermute | solution.py:320
  16.0 2.1 %collective-permute-start.10 = (bf16[256,256]{1,0:T(8,128)(2,1)S(1)}, bf16[256,256]{1,0:T(8,128)(2,1)S(1)}, u32[]{:S(2)}, u32[]{:S(2)}) collective-permute-start(bf16[256,256]{1,0:T(8,128)(2,1)S(1)} %get-tuple-element.72), channel_id=1, source_target_pairs={{9,11},{25,27},{41,43},{57,59},{73,75},{89,91},{105,107},{121,123}... | collective-permute-start | bytes 393224 | tf_op jit(solution)/shard_map/ppermute | solution.py:320
  16.6 2.8 %collective-permute-start.8 = (bf16[256,256]{1,0:T(8,128)(2,1)S(1)}, bf16[256,256]{1,0:T(8,128)(2,1)S(1)}, u32[]{:S(2)}, u32[]{:S(2)}) collective-permute-start(bf16[256,256]{1,0:T(8,128)(2,1)S(1)} %get-tuple-element.76), channel_id=1, source_target_pairs={{7,11},{23,27},{39,43},{55,59},{71,75},{87,91},{103,107},{119,123}... | collective-permute-start | bytes 393224 | tf_op jit(solution)/shard_map/ppermute | solution.py:320
  17.4 2.2 %collective-permute-start.12 = (bf16[256,256]{1,0:T(8,128)(2,1)S(1)}, bf16[256,256]{1,0:T(8,128)(2,1)S(1)}, u32[]{:S(2)}, u32[]{:S(2)}) collective-permute-start(bf16[256,256]{1,0:T(8,128)(2,1)S(1)} %get-tuple-element.79.other.mine), channel_id=1, source_target_pairs={{7,11},{23,27},{39,43},{55,59},{71,75},{87,91},{103,107},{119,123}... | collective-permute-start | bytes 393224 | tf_op jit(solution)/shard_map/ppermute | solution.py:320
  18.1 1.4 %collective-permute-start.13 = (bf16[256,256]{1,0:T(8,128)(2,1)S(1)}, bf16[256,256]{1,0:T(8,128)(2,1)S(1)}, u32[]{:S(2)}, u32[]{:S(2)}) collective-permute-start(bf16[256,256]{1,0:T(8,128)(2,1)S(1)} %get-tuple-element.89), channel_id=1, source_target_pairs={{9,11},{11,13},{25,27},{27,29},{41,43},{43,45},{57,59},{59,61},{73... | collective-permute-start | bytes 393224 | tf_op jit(solution)/shard_map/ppermute | solution.py:320
  18.8 2.1 %collective-permute-start.14 = (bf16[256,256]{1,0:T(8,128)(2,1)S(1)}, bf16[256,256]{1,0:T(8,128)(2,1)S(1)}, u32[]{:S(2)}, u32[]{:S(2)}) collective-permute-start(bf16[256,256]{1,0:T(8,128)(2,1)S(1)} %get-tuple-element.82.other), channel_id=1, source_target_pairs={{7,9},{11,15},{23,25},{27,31},{39,41},{43,47},{55,57},{59,63},{71,... | collective-permute-start | bytes 393224 | tf_op jit(solution)/shard_map/ppermute | solution.py:320
  19.6 1.4 %collective-permute-start.15 = (bf16[256,256]{1,0:T(8,128)(2,1)S(1)}, bf16[256,256]{1,0:T(8,128)(2,1)S(1)}, u32[]{:S(2)}, u32[]{:S(2)}) collective-permute-start(bf16[256,256]{1,0:T(8,128)(2,1)S(1)} %get-tuple-element.91.mine), channel_id=1, source_target_pairs={{11,13},{13,15},{27,29},{29,31},{43,45},{45,47},{59,61},{61,63},{7... | collective-permute-start | bytes 393224 | tf_op jit(solution)/shard_map/ppermute | solution.py:320
  20.3 2.7 %collective-permute-start.18 = (bf16[256,256]{1,0:T(8,128)(2,1)S(1)}, bf16[256,256]{1,0:T(8,128)(2,1)S(1)}, u32[]{:S(2)}, u32[]{:S(2)}) collective-permute-start(bf16[256,256]{1,0:T(8,128)(2,1)S(1)} %get-tuple-element.91.mine), channel_id=1, source_target_pairs={{11,15},{3,2},{5,4},{7,8},{27,31},{19,18},{21,20},{23,24},{43,47},... | collective-permute-start | bytes 393224 | tf_op jit(solution)/shard_map/ppermute | solution.py:320
  21.0 2.0 %collective-permute-start.17 = (bf16[256,256]{1,0:T(8,128)(2,1)S(1)}, bf16[256,256]{1,0:T(8,128)(2,1)S(1)}, u32[]{:S(2)}, u32[]{:S(2)}) collective-permute-start(bf16[256,256]{1,0:T(8,128)(2,1)S(1)} %get-tuple-element.93), channel_id=1, source_target_pairs={{13,15},{9,11},{29,31},{25,27},{45,47},{41,43},{61,63},{57,59},{77... | collective-permute-start | bytes 393224 | tf_op jit(solution)/shard_map/ppermute | solution.py:320
  21.7 21.7 %collective-permute-start.16 = (bf16[256,256]{1,0:T(8,128)(2,1)S(1)}, bf16[256,256]{1,0:T(8,128)(2,1)S(1)}, u32[]{:S(2)}, u32[]{:S(2)}) collective-permute-start(bf16[256,256]{1,0:T(8,128)(2,1)S(1)} %get-tuple-element.93), channel_id=1, source_target_pairs={{13,14},{9,10},{11,12},{7,6},{29,30},{25,26},{27,28},{23,22},{45,4... | collective-permute-start | bytes 393224 | tf_op jit(solution)/shard_map/ppermute | solution.py:320

commit v7 on v6

--- a/solution.py
+++ b/solution.py
@@ -201,6 +201,10 @@
         solved[...] = value
         out[...] = value.astype(BF16)
 
+    @pl.when(place() == 7)
+    def _():
+        out[...] = rhs[...].astype(BF16)
+
 
 def one_step(owners, first, rhs, own_w, _, out, solved):
     @pl.when(either(place(), owners))
@@ -212,6 +216,15 @@
 def coarse_step(got, own_w):
     value = got[...].astype(F32)
     return value + 4.0 * conv_tanh(value, own_w)
+
+
+def relax_rest(rhs, own_w, odd_w, odd_rhs, got, _, out, solved):
+    @pl.when(place() == 6)
+    def _():
+        value = got[...].astype(F32)
+        value = value + conv_tanh(value, own_w) + rhs[...]
+        value = value + conv_tanh(value, odd_w) + odd_rhs[...].astype(F32)
+        out[...] = value.astype(BF16)
 
 
 def steps_or_copy(owner, copier, other, even_rhs, rhs, even_w, own_w, got, _, out, solved):
@@ -347,7 +360,7 @@
         aliases={3: 1, 4: 2, 5: 3},
     )
     left_odd = send(from_even, up_inside)
-    even_w = send(own_w, up_inside)
+    even_w = send(own_w, [*up_inside, (7, 6)])
 
     left_even, start = kernel_call(
         in_order, [narrow, wide], [left_even, start], "even_first", 1, aliases={0: 0, 1: 1}
@@ -394,15 +407,17 @@
 
     part = chained(lead_half, [got3, even_w], "lead_first", 7, wide)
     upper1 = chained(lead_rest, [rhs, own_w, even_rhs, part], "relax_lead", 20)
-    got4 = send(upper1, [(3, 5)])
+    got4 = send(upper1, [(3, 5), (7, 6)])
     c5 = chained(functools.partial(one_step, (5, 9)), [first, rhs, own_w], "relax_first", 1)
-    got3_rest = send(c5, [(5, 7)])
+    got3_rest = send(c5, [(5, 6)])
     got3_last = send(c5, [(9, 11)])
     c5_lead = pair((5,), False, got4, "again_lead")
     got5 = send(c5_lead, [(5, 7)])
-    upper7 = pair((7,), False, got3_rest, "relax_rest")
-    got4_rest = send(upper7, [(7, 9)])
-    upper_prev = send(upper7, [(7, 11)])
+    upper6 = chained(
+        relax_rest, [rhs_of_even, own_w, even_w, got4, got3_rest], "relax_rest", 2
+    )
+    got4_rest = send(upper6, [(6, 9)])
+    upper_prev = send(upper6, [(6, 11)])
     z2 = pair((7,), True, got5, "again_end_lead")
     got6 = send(z2, [(7, 11)])
     got4_rest, solved = kernel_call(

time: 46.2 us -> 47.5 us (1.028)
  waiting for transfers between devices: 21 us -> 22.3 us
    ppermute x19, waiting for transfers between devices: 21 us -> 22.3 us  [send(): return lax.ppermute(value, 'layer', pairs)]
where the time goes in v7:
time: 47.5 us; the launch traced here: 47.1 us
  waiting for transfers between devices  22.3 us (47%)
  starting transfers between devices  15.9 us (33%)
  Pallas kernels  8.32 us (18%)
  between operations  0.57 us (1%)
    ppermute x19, waiting for transfers between devices, send(): return lax.ppermute(value, 'layer', pairs)  22.3 us
    ppermute x19, starting transfers between devices, send(): return lax.ppermute(value, 'layer', pairs)  15.9 us
    pallas_call x21, Pallas kernels, kernel_call(): pl.pallas_call(body, out_shape=outs, in_specs=[pl.BlockSpec(memory_space=...  8.32 us
  transfers between devices with their start and end apart: 19, of which 3 were waited for; matrix products, arithmetic and copies ran while one was open for 0% of the time, Pallas kernels for 13%

profile of v7, /device:TPU:248, one launch (start us, length us, event | category | flops | bytes accessed | tf_op | source)
XLA Modules:
  0.0 47.1 jit_solution(17637034732693755925)
XLA Ops:
  0.1 1.3 %collective-permute-start = (bf16[256,256]{1,0:T(8,128)(2,1)S(1)}, bf16[256,256]{1,0:T(8,128)(2,1)S(1)}, u32[]{:S(2)}, u32[]{:S(2)}) collective-permute-start(bf16[256,256]{1,0:T(8,128)(2,1)S(1)} %get-tuple-element.50.refs_6_), channel_id=1, source_target_pairs={{1,2},{3,4},{5,6},{7,8},{9,10},{11,12},{13,14},{17,18},{19,20},{21... | collective-permute-start | bytes 393224 | tf_op jit(solution)/shard_map/ppermute | solution.py:333
  1.4 3.7 %first_sweep_even.1 = (bf16[256,256]{1,0:T(8,128)(2,1)S(1)}, bf16[256,2304]{1,0:T(8,128)(2,1)S(1)}, bf16[3,256,2304]{2,1,0:T(8,128)(2,1)S(1)}, f32[256,256]{1,0:T(8,128)S(1)}) custom-call(f32[256,256]{1,0:T(8,128)} %inputs.1, f32[1,256,256]{2,1,0:T(8,128)} %refs_1_.3, ...), custom_call_target="tpu_custom_call", output_to_operand_aliasing={{1}: (3, {}), {2}: (4, {}), {3}: (5, {})} | custom-call | flops 1207959552 | bytes 1048576 | tf_op jit(solution)/shard_map/first_sweep_even/pallas_call | solution.py:58
  5.0 1.3 %collective-permute-start.1 = (bf16[256,256]{1,0:T(8,128)(2,1)S(1)}, bf16[256,256]{1,0:T(8,128)(2,1)S(1)}, u32[]{:S(2)}, u32[]{:S(2)}) collective-permute-start(bf16[256,256]{1,0:T(8,128)(2,1)S(1)} %get-tuple-element.59), channel_id=1, source_target_pairs={{0,1},{2,3},{4,5},{6,7},{8,9},{10,11},{12,13},{14,15},{16,17},{18,... | collective-permute-start | bytes 393224 | tf_op jit(solution)/shard_map/ppermute | solution.py:333
  6.3 1.4 %collective-permute-start.3 = (bf16[256,2304]{1,0:T(8,128)(2,1)S(1)}, bf16[256,2304]{1,0:T(8,128)(2,1)S(1)}, u32[]{:S(2)}, u32[]{:S(2)}) collective-permute-start(bf16[256,2304]{1,0:T(8,128)(2,1)S(1)} %get-tuple-element.56.own_w), channel_id=1, source_target_pairs={{0,1},{2,3},{4,5},{6,7},{8,9},{10,11},{12,13},{14,15},{7,6},{16,17... | collective-permute-start | bytes 3538952 | tf_op jit(solution)/shard_map/ppermute | solution.py:333
  7.7 0.3 collective-permute-done.refs_0_
  8.0 0.0 collective-permute-done.1.left_odd
  8.0 0.7 %collective-permute-start.4 = (bf16[256,256]{1,0:T(8,128)(2,1)S(1)}, bf16[256,256]{1,0:T(8,128)(2,1)S(1)}, u32[]{:S(2)}, u32[]{:S(2)}) collective-permute-start(bf16[256,256]{1,0:T(8,128)(2,1)S(1)} %get-tuple-element.66), channel_id=1, source_target_pairs={{1,3},{17,19},{33,35},{49,51},{65,67},{81,83},{97,99},{113,115},{1... | collective-permute-start | bytes 393224 | tf_op jit(solution)/shard_map/ppermute | solution.py:333
  8.6 1.9 %second_sweep_even.1 = (f32[256,256]{1,0:T(8,128)S(1)}, f32[256,256]{1,0:T(8,128)S(1)}, f32[256,256]{1,0:T(8,128)S(1)}, f32[256,256]{1,0:T(8,128)S(1)}) custom-call(bf16[256,256]{1,0:T(8,128)(2,1)S(1)} %get-tuple-element.55.left_even, bf16[256,2304]{1,0:T(8,128)(2,1)S(1)} %get-tuple-element.56.own_w, ...), custom_call_target="tpu_custom_call", output_to_operand_aliasing={{2}: (4, {}), {3}: (5, {})} | custom-call | flops 1207959552 | bytes 1048576 | tf_op jit(solution)/shard_map/second_sweep_even/pallas_call | solution.py:58
  10.5 1.3 %collective-permute-start.2 = (f32[256,256]{1,0:T(8,128)S(1)}, f32[256,256]{1,0:T(8,128)S(1)}, u32[]{:S(2)}, u32[]{:S(2)}) collective-permute-start(f32[256,256]{1,0:T(8,128)S(1)} %get-tuple-element.62.rhs.rhs_of_even), channel_id=1, source_target_pairs={{0,1},{2,3},{4,5},{6,7},{8,9},{10,11},{12,13},{14,15},{16,17},{18,... | collective-permute-start | bytes 786440 | tf_op jit(solution)/shard_map/ppermute | solution.py:333
  11.9 0.7 %collective-permute-start.6 = (f32[256,256]{1,0:T(8,128)S(1)}, f32[256,256]{1,0:T(8,128)S(1)}, u32[]{:S(2)}, u32[]{:S(2)}) collective-permute-start(f32[256,256]{1,0:T(8,128)S(1)} %get-tuple-element.71), channel_id=1, source_target_pairs={{4,5},{8,9},{20,21},{24,25},{36,37},{40,41},{52,53},{56,57},{68,69... | collective-permute-start | bytes 786440 | tf_op jit(solution)/shard_map/ppermute | solution.py:333
  12.6 0.0 collective-permute-done.4.got.early3.got3
  12.6 0.4 collective-permute-done.2.even_rhs
  13.0 0.7 %collective-permute-start.5 = (bf16[256,256]{1,0:T(8,128)(2,1)S(1)}, bf16[256,256]{1,0:T(8,128)(2,1)S(1)}, u32[]{:S(2)}, u32[]{:S(2)}) collective-permute-start(bf16[256,256]{1,0:T(8,128)(2,1)S(1)} %get-tuple-element.70), channel_id=1, source_target_pairs={{3,5},{7,6},{19,21},{23,22},{35,37},{39,38},{51,53},{55,54},{67,69... | collective-permute-start | bytes 393224 | tf_op jit(solution)/shard_map/ppermute | solution.py:333
  13.7 0.7 %collective-permute-start.7 = (bf16[256,256]{1,0:T(8,128)(2,1)S(1)}, bf16[256,256]{1,0:T(8,128)(2,1)S(1)}, u32[]{:S(2)}, u32[]{:S(2)}) collective-permute-start(bf16[256,256]{1,0:T(8,128)(2,1)S(1)} %get-tuple-element.73), channel_id=1, source_target_pairs={{5,6},{21,22},{37,38},{53,54},{69,70},{85,86},{101,102},{117,118},... | collective-permute-start | bytes 393224 | tf_op jit(solution)/shard_map/ppermute | solution.py:333
  14.4 0.2 again_lead.1
  14.6 0.7 %collective-permute-start.9 = (bf16[256,256]{1,0:T(8,128)(2,1)S(1)}, bf16[256,256]{1,0:T(8,128)(2,1)S(1)}, u32[]{:S(2)}, u32[]{:S(2)}) collective-permute-start(bf16[256,256]{1,0:T(8,128)(2,1)S(1)} %get-tuple-element.77), channel_id=1, source_target_pairs={{5,7},{21,23},{37,39},{53,55},{69,71},{85,87},{101,103},{117,119},... | collective-permute-start | bytes 393224 | tf_op jit(solution)/shard_map/ppermute | solution.py:333
  15.3 0.7 %collective-permute-start.11 = (bf16[256,256]{1,0:T(8,128)(2,1)S(1)}, bf16[256,256]{1,0:T(8,128)(2,1)S(1)}, u32[]{:S(2)}, u32[]{:S(2)}) collective-permute-start(bf16[256,256]{1,0:T(8,128)(2,1)S(1)} %get-tuple-element.76), channel_id=1, source_target_pairs={{6,9},{22,25},{38,41},{54,57},{70,73},{86,89},{102,105},{118,121},... | collective-permute-start | bytes 393224 | tf_op jit(solution)/shard_map/ppermute | solution.py:333
  16.0 0.7 %collective-permute-start.10 = (bf16[256,256]{1,0:T(8,128)(2,1)S(1)}, bf16[256,256]{1,0:T(8,128)(2,1)S(1)}, u32[]{:S(2)}, u32[]{:S(2)}) collective-permute-start(bf16[256,256]{1,0:T(8,128)(2,1)S(1)} %get-tuple-element.73), channel_id=1, source_target_pairs={{9,11},{25,27},{41,43},{57,59},{73,75},{89,91},{105,107},{121,123}... | collective-permute-start | bytes 393224 | tf_op jit(solution)/shard_map/ppermute | solution.py:333
  16.6 0.7 %collective-permute-start.8 = (bf16[256,256]{1,0:T(8,128)(2,1)S(1)}, bf16[256,256]{1,0:T(8,128)(2,1)S(1)}, u32[]{:S(2)}, u32[]{:S(2)}) collective-permute-start(bf16[256,256]{1,0:T(8,128)(2,1)S(1)} %get-tuple-element.76), channel_id=1, source_target_pairs={{6,11},{22,27},{38,43},{54,59},{70,75},{86,91},{102,107},{118,123}... | collective-permute-start | bytes 393224 | tf_op jit(solution)/shard_map/ppermute | solution.py:333
  17.4 0.7 %collective-permute-start.12 = (bf16[256,256]{1,0:T(8,128)(2,1)S(1)}, bf16[256,256]{1,0:T(8,128)(2,1)S(1)}, u32[]{:S(2)}, u32[]{:S(2)}) collective-permute-start(bf16[256,256]{1,0:T(8,128)(2,1)S(1)} %get-tuple-element.79.other.mine), channel_id=1, source_target_pairs={{7,11},{23,27},{39,43},{55,59},{71,75},{87,91},{103,107},{119,123}... | collective-permute-start | bytes 393224 | tf_op jit(solution)/shard_map/ppermute | solution.py:333
  18.0 0.0 collective-permute-done.10.got
  18.1 0.7 %collective-permute-start.13 = (bf16[256,256]{1,0:T(8,128)(2,1)S(1)}, bf16[256,256]{1,0:T(8,128)(2,1)S(1)}, u32[]{:S(2)}, u32[]{:S(2)}) collective-permute-start(bf16[256,256]{1,0:T(8,128)(2,1)S(1)} %get-tuple-element.89), channel_id=1, source_target_pairs={{9,11},{11,13},{25,27},{27,29},{41,43},{43,45},{57,59},{59,61},{73... | collective-permute-start | bytes 393224 | tf_op jit(solution)/shard_map/ppermute | solution.py:333
  18.8 0.7 %collective-permute-start.14 = (bf16[256,256]{1,0:T(8,128)(2,1)S(1)}, bf16[256,256]{1,0:T(8,128)(2,1)S(1)}, u32[]{:S(2)}, u32[]{:S(2)}) collective-permute-start(bf16[256,256]{1,0:T(8,128)(2,1)S(1)} %get-tuple-element.82.other), channel_id=1, source_target_pairs={{7,9},{11,15},{23,25},{27,31},{39,41},{43,47},{55,57},{59,63},{71,... | collective-permute-start | bytes 393224 | tf_op jit(solution)/shard_map/ppermute | solution.py:333
  19.5 0.0 collective-permute-done.8.upper
  19.5 0.0 collective-permute-done.13.got
  19.6 0.7 %collective-permute-start.15 = (bf16[256,256]{1,0:T(8,128)(2,1)S(1)}, bf16[256,256]{1,0:T(8,128)(2,1)S(1)}, u32[]{:S(2)}, u32[]{:S(2)}) collective-permute-start(bf16[256,256]{1,0:T(8,128)(2,1)S(1)} %get-tuple-element.91.mine), channel_id=1, source_target_pairs={{11,13},{13,15},{27,29},{29,31},{43,45},{45,47},{59,61},{61,63},{7... | collective-permute-start | bytes 393224 | tf_op jit(solution)/shard_map/ppermute | solution.py:333
  20.3 0.7 %collective-permute-start.18 = (bf16[256,256]{1,0:T(8,128)(2,1)S(1)}, bf16[256,256]{1,0:T(8,128)(2,1)S(1)}, u32[]{:S(2)}, u32[]{:S(2)}) collective-permute-start(bf16[256,256]{1,0:T(8,128)(2,1)S(1)} %get-tuple-element.91.mine), channel_id=1, source_target_pairs={{11,15},{3,2},{5,4},{7,8},{27,31},{19,18},{21,20},{23,24},{43,47},... | collective-permute-start | bytes 393224 | tf_op jit(solution)/shard_map/ppermute | solution.py:333
  20.9 0.0 collective-permute-done.14.rest.upper.got6
  21.0 0.7 %collective-permute-start.17 = (bf16[256,256]{1,0:T(8,128)(2,1)S(1)}, bf16[256,256]{1,0:T(8,128)(2,1)S(1)}, u32[]{:S(2)}, u32[]{:S(2)}) collective-permute-start(bf16[256,256]{1,0:T(8,128)(2,1)S(1)} %get-tuple-element.93), channel_id=1, source_target_pairs={{13,15},{9,11},{29,31},{25,27},{45,47},{41,43},{61,63},{57,59},{77... | collective-permute-start | bytes 393224 | tf_op jit(solution)/shard_map/ppermute | solution.py:333
  21.7 1.3 %collective-permute-start.16 = (bf16[256,256]{1,0:T(8,128)(2,1)S(1)}, bf16[256,256]{1,0:T(8,128)(2,1)S(1)}, u32[]{:S(2)}, u32[]{:S(2)}) collective-permute-start(bf16[256,256]{1,0:T(8,128)(2,1)S(1)} %get-tuple-element.93), channel_id=1, source_target_pairs={{13,14},{9,10},{11,12},{7,6},{29,30},{25,26},{27,28},{23,22},{45,4... | collective-permute-start | bytes 393224 | tf_op jit(solution)/shard_map/ppermute | solution.py:333
  23.0 21.6 %collective-permute-done.16.got8b = bf16[256,256]{1,0:T(8,128)(2,1)S(1)} collective-permute-done((bf16[256,256]{1,0:T(8,128)(2,1)S(1)}, bf16[256,256]{1,0:T(8,128)(2,1)S(1)}, u32[]{:S(2)}, u32[]{:S(2)}) %collective-permute-start.16) | collective-permute-done | bytes 131104 | tf_op jit(solution)/shard_map/ppermute | solution.py:333
  44.6 2.3 %last_sweep.1 = f32[4,256,256]{2,1,0:T(8,128)} custom-call(f32[256,256]{1,0:T(8,128)S(1)} %get-tuple-element.61.start, bf16[256,256]{1,0:T(8,128)(2,1)S(1)} %collective-permute-done.16.got8b, bf16[256,256]{1,0:T(8,128)(2,1)S(1)} %collective-permute-done.17.got8, bf16[256,256]{1,0:T(8,128)(2,1)S(1)} %collective-permute-done.4.got.early3.got3, ...), custom_call_target="tpu_custom_call" | custom-call | flops 1207959552 | bytes 1048576 | tf_op jit(solution)/shard_map/last_sweep/pallas_call | solution.py:58
  (27 shorter events, 0.3 us)
Async XLA Ops:
  0.1 7.9 %collective-permute-start = (bf16[256,256]{1,0:T(8,128)(2,1)S(1)}, bf16[256,256]{1,0:T(8,128)(2,1)S(1)}, u32[]{:S(2)}, u32[]{:S(2)}) collective-permute-start(bf16[256,256]{1,0:T(8,128)(2,1)S(1)} %get-tuple-element.50.refs_6_), channel_id=1, source_target_pairs={{1,2},{3,4},{5,6},{7,8},{9,10},{11,12},{13,14},{17,18},{19,20},{21... | collective-permute-start | bytes 393224 | tf_op jit(solution)/shard_map/ppermute | solution.py:333
  5.0 3.0 %collective-permute-start.1 = (bf16[256,256]{1,0:T(8,128)(2,1)S(1)}, bf16[256,256]{1,0:T(8,128)(2,1)S(1)}, u32[]{:S(2)}, u32[]{:S(2)}) collective-permute-start(bf16[256,256]{1,0:T(8,128)(2,1)S(1)} %get-tuple-element.59), channel_id=1, source_target_pairs={{0,1},{2,3},{4,5},{6,7},{8,9},{10,11},{12,13},{14,15},{16,17},{18,... | collective-permute-start | bytes 393224 | tf_op jit(solution)/shard_map/ppermute | solution.py:333
  6.3 6.3 %collective-permute-start.3 = (bf16[256,2304]{1,0:T(8,128)(2,1)S(1)}, bf16[256,2304]{1,0:T(8,128)(2,1)S(1)}, u32[]{:S(2)}, u32[]{:S(2)}) collective-permute-start(bf16[256,2304]{1,0:T(8,128)(2,1)S(1)} %get-tuple-element.56.own_w), channel_id=1, source_target_pairs={{0,1},{2,3},{4,5},{6,7},{8,9},{10,11},{12,13},{14,15},{7,6},{16,17... | collective-permute-start | bytes 3538952 | tf_op jit(solution)/shard_map/ppermute | solution.py:333
  8.0 4.6 %collective-permute-start.4 = (bf16[256,256]{1,0:T(8,128)(2,1)S(1)}, bf16[256,256]{1,0:T(8,128)(2,1)S(1)}, u32[]{:S(2)}, u32[]{:S(2)}) collective-permute-start(bf16[256,256]{1,0:T(8,128)(2,1)S(1)} %get-tuple-element.66), channel_id=1, source_target_pairs={{1,3},{17,19},{33,35},{49,51},{65,67},{81,83},{97,99},{113,115},{1... | collective-permute-start | bytes 393224 | tf_op jit(solution)/shard_map/ppermute | solution.py:333
  10.5 2.4 %collective-permute-start.2 = (f32[256,256]{1,0:T(8,128)S(1)}, f32[256,256]{1,0:T(8,128)S(1)}, u32[]{:S(2)}, u32[]{:S(2)}) collective-permute-start(f32[256,256]{1,0:T(8,128)S(1)} %get-tuple-element.62.rhs.rhs_of_even), channel_id=1, source_target_pairs={{0,1},{2,3},{4,5},{6,7},{8,9},{10,11},{12,13},{14,15},{16,17},{18,... | collective-permute-start | bytes 786440 | tf_op jit(solution)/shard_map/ppermute | solution.py:333
  11.9 1.8 %collective-permute-start.6 = (f32[256,256]{1,0:T(8,128)S(1)}, f32[256,256]{1,0:T(8,128)S(1)}, u32[]{:S(2)}, u32[]{:S(2)}) collective-permute-start(f32[256,256]{1,0:T(8,128)S(1)} %get-tuple-element.71), channel_id=1, source_target_pairs={{4,5},{8,9},{20,21},{24,25},{36,37},{40,41},{52,53},{56,57},{68,69... | collective-permute-start | bytes 786440 | tf_op jit(solution)/shard_map/ppermute | solution.py:333
  13.0 1.4 %collective-permute-start.5 = (bf16[256,256]{1,0:T(8,128)(2,1)S(1)}, bf16[256,256]{1,0:T(8,128)(2,1)S(1)}, u32[]{:S(2)}, u32[]{:S(2)}) collective-permute-start(bf16[256,256]{1,0:T(8,128)(2,1)S(1)} %get-tuple-element.70), channel_id=1, source_target_pairs={{3,5},{7,6},{19,21},{23,22},{35,37},{39,38},{51,53},{55,54},{67,69... | collective-permute-start | bytes 393224 | tf_op jit(solution)/shard_map/ppermute | solution.py:333
  13.7 1.6 %collective-permute-start.7 = (bf16[256,256]{1,0:T(8,128)(2,1)S(1)}, bf16[256,256]{1,0:T(8,128)(2,1)S(1)}, u32[]{:S(2)}, u32[]{:S(2)}) collective-permute-start(bf16[256,256]{1,0:T(8,128)(2,1)S(1)} %get-tuple-element.73), channel_id=1, source_target_pairs={{5,6},{21,22},{37,38},{53,54},{69,70},{85,86},{101,102},{117,118},... | collective-permute-start | bytes 393224 | tf_op jit(solution)/shard_map/ppermute | solution.py:333
  14.6 2.7 %collective-permute-start.9 = (bf16[256,256]{1,0:T(8,128)(2,1)S(1)}, bf16[256,256]{1,0:T(8,128)(2,1)S(1)}, u32[]{:S(2)}, u32[]{:S(2)}) collective-permute-start(bf16[256,256]{1,0:T(8,128)(2,1)S(1)} %get-tuple-element.77), channel_id=1, source_target_pairs={{5,7},{21,23},{37,39},{53,55},{69,71},{85,87},{101,103},{117,119},... | collective-permute-start | bytes 393224 | tf_op jit(solution)/shard_map/ppermute | solution.py:333
  15.3 2.7 %collective-permute-start.11 = (bf16[256,256]{1,0:T(8,128)(2,1)S(1)}, bf16[256,256]{1,0:T(8,128)(2,1)S(1)}, u32[]{:S(2)}, u32[]{:S(2)}) collective-permute-start(bf16[256,256]{1,0:T(8,128)(2,1)S(1)} %get-tuple-element.76), channel_id=1, source_target_pairs={{6,9},{22,25},{38,41},{54,57},{70,73},{86,89},{102,105},{118,121},... | collective-permute-start | bytes 393224 | tf_op jit(solution)/shard_map/ppermute | solution.py:333
  16.0 2.1 %collective-permute-start.10 = (bf16[256,256]{1,0:T(8,128)(2,1)S(1)}, bf16[256,256]{1,0:T(8,128)(2,1)S(1)}, u32[]{:S(2)}, u32[]{:S(2)}) collective-permute-start(bf16[256,256]{1,0:T(8,128)(2,1)S(1)} %get-tuple-element.73), channel_id=1, source_target_pairs={{9,11},{25,27},{41,43},{57,59},{73,75},{89,91},{105,107},{121,123}... | collective-permute-start | bytes 393224 | tf_op jit(solution)/shard_map/ppermute | solution.py:333
  16.6 2.8 %collective-permute-start.8 = (bf16[256,256]{1,0:T(8,128)(2,1)S(1)}, bf16[256,256]{1,0:T(8,128)(2,1)S(1)}, u32[]{:S(2)}, u32[]{:S(2)}) collective-permute-start(bf16[256,256]{1,0:T(8,128)(2,1)S(1)} %get-tuple-element.76), channel_id=1, source_target_pairs={{6,11},{22,27},{38,43},{54,59},{70,75},{86,91},{102,107},{118,123}... | collective-permute-start | bytes 393224 | tf_op jit(solution)/shard_map/ppermute | solution.py:333
  17.4 2.2 %collective-permute-start.12 = (bf16[256,256]{1,0:T(8,128)(2,1)S(1)}, bf16[256,256]{1,0:T(8,128)(2,1)S(1)}, u32[]{:S(2)}, u32[]{:S(2)}) collective-permute-start(bf16[256,256]{1,0:T(8,128)(2,1)S(1)} %get-tuple-element.79.other.mine), channel_id=1, source_target_pairs={{7,11},{23,27},{39,43},{55,59},{71,75},{87,91},{103,107},{119,123}... | collective-permute-start | bytes 393224 | tf_op jit(solution)/shard_map/ppermute | solution.py:333
  18.1 1.4 %collective-permute-start.13 = (bf16[256,256]{1,0:T(8,128)(2,1)S(1)}, bf16[256,256]{1,0:T(8,128)(2,1)S(1)}, u32[]{:S(2)}, u32[]{:S(2)}) collective-permute-start(bf16[256,256]{1,0:T(8,128)(2,1)S(1)} %get-tuple-element.89), channel_id=1, source_target_pairs={{9,11},{11,13},{25,27},{27,29},{41,43},{43,45},{57,59},{59,61},{73... | collective-permute-start | bytes 393224 | tf_op jit(solution)/shard_map/ppermute | solution.py:333
  18.8 2.1 %collective-permute-start.14 = (bf16[256,256]{1,0:T(8,128)(2,1)S(1)}, bf16[256,256]{1,0:T(8,128)(2,1)S(1)}, u32[]{:S(2)}, u32[]{:S(2)}) collective-permute-start(bf16[256,256]{1,0:T(8,128)(2,1)S(1)} %get-tuple-element.82.other), channel_id=1, source_target_pairs={{7,9},{11,15},{23,25},{27,31},{39,41},{43,47},{55,57},{59,63},{71,... | collective-permute-start | bytes 393224 | tf_op jit(solution)/shard_map/ppermute | solution.py:333
  19.6 1.4 %collective-permute-start.15 = (bf16[256,256]{1,0:T(8,128)(2,1)S(1)}, bf16[256,256]{1,0:T(8,128)(2,1)S(1)}, u32[]{:S(2)}, u32[]{:S(2)}) collective-permute-start(bf16[256,256]{1,0:T(8,128)(2,1)S(1)} %get-tuple-element.91.mine), channel_id=1, source_target_pairs={{11,13},{13,15},{27,29},{29,31},{43,45},{45,47},{59,61},{61,63},{7... | collective-permute-start | bytes 393224 | tf_op jit(solution)/shard_map/ppermute | solution.py:333
  20.3 2.7 %collective-permute-start.18 = (bf16[256,256]{1,0:T(8,128)(2,1)S(1)}, bf16[256,256]{1,0:T(8,128)(2,1)S(1)}, u32[]{:S(2)}, u32[]{:S(2)}) collective-permute-start(bf16[256,256]{1,0:T(8,128)(2,1)S(1)} %get-tuple-element.91.mine), channel_id=1, source_target_pairs={{11,15},{3,2},{5,4},{7,8},{27,31},{19,18},{21,20},{23,24},{43,47},... | collective-permute-start | bytes 393224 | tf_op jit(solution)/shard_map/ppermute | solution.py:333
  21.0 2.0 %collective-permute-start.17 = (bf16[256,256]{1,0:T(8,128)(2,1)S(1)}, bf16[256,256]{1,0:T(8,128)(2,1)S(1)}, u32[]{:S(2)}, u32[]{:S(2)}) collective-permute-start(bf16[256,256]{1,0:T(8,128)(2,1)S(1)} %get-tuple-element.93), channel_id=1, source_target_pairs={{13,15},{9,11},{29,31},{25,27},{45,47},{41,43},{61,63},{57,59},{77... | collective-permute-start | bytes 393224 | tf_op jit(solution)/shard_map/ppermute | solution.py:333
  21.7 23.0 %collective-permute-start.16 = (bf16[256,256]{1,0:T(8,128)(2,1)S(1)}, bf16[256,256]{1,0:T(8,128)(2,1)S(1)}, u32[]{:S(2)}, u32[]{:S(2)}) collective-permute-start(bf16[256,256]{1,0:T(8,128)(2,1)S(1)} %get-tuple-element.93), channel_id=1, source_target_pairs={{13,14},{9,10},{11,12},{7,6},{29,30},{25,26},{27,28},{23,22},{45,4... | collective-permute-start | bytes 393224 | tf_op jit(solution)/shard_map/ppermute | solution.py:333

commit v8 on v6

--- a/solution.py
+++ b/solution.py
@@ -136,13 +136,14 @@
         out[...] = sweep(left_odd[...].astype(F32), own_w, later_w, rhs).astype(BF16)
 
 
-def second_sweep_even(left_even, own_w, later_w, inputs, _, __, rhs, first, start, solved, raw, sem):
+def second_sweep_even(left_even, own_w, later_w, inputs, _, __, rhs, first, start, solved, sent, raw, sem):
     me = place()
 
     @pl.when(me % 2 == 0)
     def _():
         left = jnp.where(me == 0, start[...], left_even[...].astype(F32))
         first[...] = sweep(left, own_w, later_w, rhs)
+        sent[...] = rhs[...].astype(BF16)
 
     @pl.when(me == 1)
     def _():
@@ -173,7 +174,7 @@
 
 def both_steps(even_rhs, rhs, even_w, own_w, got):
     value = got[...].astype(F32)
-    value = value + conv_tanh(value, even_w) + even_rhs[...]
+    value = value + conv_tanh(value, even_w) + even_rhs[...].astype(F32)
     return value + conv_tanh(value, own_w) + rhs[...]
 
 
@@ -196,7 +197,7 @@
 def lead_rest(rhs, own_w, even_rhs, part, _, out, solved):
     @pl.when(place() == 3)
     def _():
-        value = part[...] + even_rhs[...]
+        value = part[...] + even_rhs[...].astype(F32)
         value = value + conv_tanh(value, own_w) + rhs[...]
         solved[...] = value
         out[...] = value.astype(BF16)
@@ -293,7 +294,7 @@
     @pl.when(me % 2 == 1)
     def _():
         value = left[...]
-        left[...] = value + conv_tanh(value, even_w) + even_rhs[...]
+        left[...] = value + conv_tanh(value, even_w) + even_rhs[...].astype(F32)
 
     def store(i, value):
         ready[i] = value.T
@@ -360,9 +361,9 @@
         40,
     )
     got3 = send(c1, [(1, 3)])
-    rhs_of_even, first, start, solved = kernel_call(
+    rhs_of_even, first, start, solved, sent = kernel_call(
         second_sweep_even,
-        [wide, wide, wide, wide],
+        [wide, wide, wide, wide, narrow],
         [left_even, own_w, later_w, inputs, start, solved],
         "second_sweep_even",
         4,
@@ -370,7 +371,7 @@
         scratch=[pltpu.VMEM((CHANS, CELLS), F32), pltpu.SemaphoreType.DMA(())],
         aliases={4: 2, 5: 3},
     )
-    even_rhs = send(rhs_of_even, up_inside)
+    even_rhs = send(sent, up_inside)
     first = send(first, [(4, 5), (8, 9)])
     rhs, solved = kernel_call(
         second_sweep_odd,

time: 46.2 us -> 46 us (level)
  no operation moved by 1% of the time
where the time goes in v8:
time: 46 us; the launch traced here: 45.6 us
  waiting for transfers between devices  20.8 us (45%)
  starting transfers between devices  15.9 us (35%)
  Pallas kernels  8.32 us (18%)
  between operations  0.57 us (1%)
    ppermute x19, waiting for transfers between devices, send(): return lax.ppermute(value, 'layer', pairs)  20.8 us
    ppermute x19, starting transfers between devices, send(): return lax.ppermute(value, 'layer', pairs)  15.9 us
    pallas_call x21, Pallas kernels, kernel_call(): pl.pallas_call(body, out_shape=outs, in_specs=[pl.BlockSpec(memory_space=...  8.32 us
  transfers between devices with their start and end apart: 19, of which 3 were waited for; matrix products, arithmetic and copies ran while one was open for 0% of the time, Pallas kernels for 13%

profile of v8, /device:TPU:248, one launch (start us, length us, event | category | flops | bytes accessed | tf_op | source)
XLA Modules:
  0.0 45.6 jit_solution(9797345356486197553)
XLA Ops:
  0.1 1.3 %collective-permute-start = (bf16[256,256]{1,0:T(8,128)(2,1)S(1)}, bf16[256,256]{1,0:T(8,128)(2,1)S(1)}, u32[]{:S(2)}, u32[]{:S(2)}) collective-permute-start(bf16[256,256]{1,0:T(8,128)(2,1)S(1)} %get-tuple-element.51.refs_6_), channel_id=1, source_target_pairs={{1,2},{3,4},{5,6},{7,8},{9,10},{11,12},{13,14},{17,18},{19,20},{21... | collective-permute-start | bytes 393224 | tf_op jit(solution)/shard_map/ppermute | solution.py:321
  1.4 3.7 %first_sweep_even.1 = (bf16[256,256]{1,0:T(8,128)(2,1)S(1)}, bf16[256,2304]{1,0:T(8,128)(2,1)S(1)}, bf16[3,256,2304]{2,1,0:T(8,128)(2,1)S(1)}, f32[256,256]{1,0:T(8,128)S(1)}) custom-call(f32[256,256]{1,0:T(8,128)} %inputs.1, f32[1,256,256]{2,1,0:T(8,128)} %refs_1_.3, ...), custom_call_target="tpu_custom_call", output_to_operand_aliasing={{1}: (3, {}), {2}: (4, {}), {3}: (5, {})} | custom-call | flops 1207959552 | bytes 1048576 | tf_op jit(solution)/shard_map/first_sweep_even/pallas_call | solution.py:58
  5.0 1.3 %collective-permute-start.1 = (bf16[256,256]{1,0:T(8,128)(2,1)S(1)}, bf16[256,256]{1,0:T(8,128)(2,1)S(1)}, u32[]{:S(2)}, u32[]{:S(2)}) collective-permute-start(bf16[256,256]{1,0:T(8,128)(2,1)S(1)} %get-tuple-element.60), channel_id=1, source_target_pairs={{0,1},{2,3},{4,5},{6,7},{8,9},{10,11},{12,13},{14,15},{16,17},{18,... | collective-permute-start | bytes 393224 | tf_op jit(solution)/shard_map/ppermute | solution.py:321
  6.3 1.4 %collective-permute-start.3 = (bf16[256,2304]{1,0:T(8,128)(2,1)S(1)}, bf16[256,2304]{1,0:T(8,128)(2,1)S(1)}, u32[]{:S(2)}, u32[]{:S(2)}) collective-permute-start(bf16[256,2304]{1,0:T(8,128)(2,1)S(1)} %get-tuple-element.57.own_w), channel_id=1, source_target_pairs={{0,1},{2,3},{4,5},{6,7},{8,9},{10,11},{12,13},{14,15},{16,17},{18,... | collective-permute-start | bytes 3538952 | tf_op jit(solution)/shard_map/ppermute | solution.py:321
  7.7 0.3 collective-permute-done.refs_0_
  8.0 0.0 collective-permute-done.1.left_odd
  8.0 0.7 %collective-permute-start.5 = (bf16[256,256]{1,0:T(8,128)(2,1)S(1)}, bf16[256,256]{1,0:T(8,128)(2,1)S(1)}, u32[]{:S(2)}, u32[]{:S(2)}) collective-permute-start(bf16[256,256]{1,0:T(8,128)(2,1)S(1)} %get-tuple-element.68), channel_id=1, source_target_pairs={{1,3},{17,19},{33,35},{49,51},{65,67},{81,83},{97,99},{113,115},{1... | collective-permute-start | bytes 393224 | tf_op jit(solution)/shard_map/ppermute | solution.py:321
  8.6 1.9 %second_sweep_even.1 = (f32[256,256]{1,0:T(8,128)S(1)}, f32[256,256]{1,0:T(8,128)S(1)}, f32[256,256]{1,0:T(8,128)S(1)}, f32[256,256]{1,0:T(8,128)S(1)}, bf16[256,256]{1,0:T(8,128)(2,1)S(1)}) custom-call(bf16[256,256]{1,0:T(8,128)(2,1)S(1)} %get-tuple-element.56.left_even, ...), custom_call_target="tpu_custom_call", output_to_operand_aliasing={{2}: (4, {}), {3}: (5, {})} | custom-call | flops 1207959552 | bytes 1048576 | tf_op jit(solution)/shard_map/second_sweep_even/pallas_call | solution.py:58
  10.6 1.3 %collective-permute-start.2 = (bf16[256,256]{1,0:T(8,128)(2,1)S(1)}, bf16[256,256]{1,0:T(8,128)(2,1)S(1)}, u32[]{:S(2)}, u32[]{:S(2)}) collective-permute-start(bf16[256,256]{1,0:T(8,128)(2,1)S(1)} %get-tuple-element.63), channel_id=1, source_target_pairs={{0,1},{2,3},{4,5},{6,7},{8,9},{10,11},{12,13},{14,15},{16,17},{18,... | collective-permute-start | bytes 393224 | tf_op jit(solution)/shard_map/ppermute | solution.py:321
  11.9 0.7 %collective-permute-start.4 = (f32[256,256]{1,0:T(8,128)S(1)}, f32[256,256]{1,0:T(8,128)S(1)}, u32[]{:S(2)}, u32[]{:S(2)}) collective-permute-start(f32[256,256]{1,0:T(8,128)S(1)} %get-tuple-element.67), channel_id=1, source_target_pairs={{4,5},{8,9},{20,21},{24,25},{36,37},{40,41},{52,53},{56,57},{68,69... | collective-permute-start | bytes 786440 | tf_op jit(solution)/shard_map/ppermute | solution.py:321
  12.6 0.0 collective-permute-done.5.got.early3.got3
  12.6 0.0 collective-permute-done.3.even_w
  12.6 0.2 collective-permute-done.2.even_rhs
  12.8 0.7 %collective-permute-start.7 = (bf16[256,256]{1,0:T(8,128)(2,1)S(1)}, bf16[256,256]{1,0:T(8,128)(2,1)S(1)}, u32[]{:S(2)}, u32[]{:S(2)}) collective-permute-start(bf16[256,256]{1,0:T(8,128)(2,1)S(1)} %get-tuple-element.74), channel_id=1, source_target_pairs={{3,5},{19,21},{35,37},{51,53},{67,69},{83,85},{99,101},{115,117},{... | collective-permute-start | bytes 393224 | tf_op jit(solution)/shard_map/ppermute | solution.py:321
  13.5 0.7 %collective-permute-start.6 = (bf16[256,256]{1,0:T(8,128)(2,1)S(1)}, bf16[256,256]{1,0:T(8,128)(2,1)S(1)}, u32[]{:S(2)}, u32[]{:S(2)}) collective-permute-start(bf16[256,256]{1,0:T(8,128)(2,1)S(1)} %get-tuple-element.73), channel_id=1, source_target_pairs={{5,7},{21,23},{37,39},{53,55},{69,71},{85,87},{101,103},{117,119},... | collective-permute-start | bytes 393224 | tf_op jit(solution)/shard_map/ppermute | solution.py:321
  14.2 0.2 again_lead.1
  14.4 0.7 %collective-permute-start.9 = (bf16[256,256]{1,0:T(8,128)(2,1)S(1)}, bf16[256,256]{1,0:T(8,128)(2,1)S(1)}, u32[]{:S(2)}, u32[]{:S(2)}) collective-permute-start(bf16[256,256]{1,0:T(8,128)(2,1)S(1)} %get-tuple-element.78), channel_id=1, source_target_pairs={{5,7},{21,23},{37,39},{53,55},{69,71},{85,87},{101,103},{117,119},... | collective-permute-start | bytes 393224 | tf_op jit(solution)/shard_map/ppermute | solution.py:321
  15.1 0.7 %collective-permute-start.11 = (bf16[256,256]{1,0:T(8,128)(2,1)S(1)}, bf16[256,256]{1,0:T(8,128)(2,1)S(1)}, u32[]{:S(2)}, u32[]{:S(2)}) collective-permute-start(bf16[256,256]{1,0:T(8,128)(2,1)S(1)} %get-tuple-element.77), channel_id=1, source_target_pairs={{7,9},{23,25},{39,41},{55,57},{71,73},{87,89},{103,105},{119,121},... | collective-permute-start | bytes 393224 | tf_op jit(solution)/shard_map/ppermute | solution.py:321
  15.8 0.7 %collective-permute-start.10 = (bf16[256,256]{1,0:T(8,128)(2,1)S(1)}, bf16[256,256]{1,0:T(8,128)(2,1)S(1)}, u32[]{:S(2)}, u32[]{:S(2)}) collective-permute-start(bf16[256,256]{1,0:T(8,128)(2,1)S(1)} %get-tuple-element.73), channel_id=1, source_target_pairs={{9,11},{25,27},{41,43},{57,59},{73,75},{89,91},{105,107},{121,123}... | collective-permute-start | bytes 393224 | tf_op jit(solution)/shard_map/ppermute | solution.py:321
  16.5 0.7 %collective-permute-start.8 = (bf16[256,256]{1,0:T(8,128)(2,1)S(1)}, bf16[256,256]{1,0:T(8,128)(2,1)S(1)}, u32[]{:S(2)}, u32[]{:S(2)}) collective-permute-start(bf16[256,256]{1,0:T(8,128)(2,1)S(1)} %get-tuple-element.77), channel_id=1, source_target_pairs={{7,11},{23,27},{39,43},{55,59},{71,75},{87,91},{103,107},{119,123}... | collective-permute-start | bytes 393224 | tf_op jit(solution)/shard_map/ppermute | solution.py:321
  17.1 0.0 collective-permute-done.9.got.early5.got5
  17.2 0.7 %collective-permute-start.12 = (bf16[256,256]{1,0:T(8,128)(2,1)S(1)}, bf16[256,256]{1,0:T(8,128)(2,1)S(1)}, u32[]{:S(2)}, u32[]{:S(2)}) collective-permute-start(bf16[256,256]{1,0:T(8,128)(2,1)S(1)} %get-tuple-element.80.other.mine), channel_id=1, source_target_pairs={{7,11},{23,27},{39,43},{55,59},{71,75},{87,91},{103,107},{119,123}... | collective-permute-start | bytes 393224 | tf_op jit(solution)/shard_map/ppermute | solution.py:321
  17.9 0.0 collective-permute-done.11.refs_0_
  17.9 0.0 collective-permute-done.10.got
  17.9 0.7 %collective-permute-start.13 = (bf16[256,256]{1,0:T(8,128)(2,1)S(1)}, bf16[256,256]{1,0:T(8,128)(2,1)S(1)}, u32[]{:S(2)}, u32[]{:S(2)}) collective-permute-start(bf16[256,256]{1,0:T(8,128)(2,1)S(1)} %get-tuple-element.90), channel_id=1, source_target_pairs={{9,11},{11,13},{25,27},{27,29},{41,43},{43,45},{57,59},{59,61},{73... | collective-permute-start | bytes 393224 | tf_op jit(solution)/shard_map/ppermute | solution.py:321
  18.6 0.7 %collective-permute-start.14 = (bf16[256,256]{1,0:T(8,128)(2,1)S(1)}, bf16[256,256]{1,0:T(8,128)(2,1)S(1)}, u32[]{:S(2)}, u32[]{:S(2)}) collective-permute-start(bf16[256,256]{1,0:T(8,128)(2,1)S(1)} %get-tuple-element.83.other), channel_id=1, source_target_pairs={{7,9},{11,15},{23,25},{27,31},{39,41},{43,47},{55,57},{59,63},{71,... | collective-permute-start | bytes 393224 | tf_op jit(solution)/shard_map/ppermute | solution.py:321
  19.4 0.7 %collective-permute-start.15 = (bf16[256,256]{1,0:T(8,128)(2,1)S(1)}, bf16[256,256]{1,0:T(8,128)(2,1)S(1)}, u32[]{:S(2)}, u32[]{:S(2)}) collective-permute-start(bf16[256,256]{1,0:T(8,128)(2,1)S(1)} %get-tuple-element.92.mine), channel_id=1, source_target_pairs={{11,13},{13,15},{27,29},{29,31},{43,45},{45,47},{59,61},{61,63},{7... | collective-permute-start | bytes 393224 | tf_op jit(solution)/shard_map/ppermute | solution.py:321
  20.1 0.7 %collective-permute-start.18 = (bf16[256,256]{1,0:T(8,128)(2,1)S(1)}, bf16[256,256]{1,0:T(8,128)(2,1)S(1)}, u32[]{:S(2)}, u32[]{:S(2)}) collective-permute-start(bf16[256,256]{1,0:T(8,128)(2,1)S(1)} %get-tuple-element.92.mine), channel_id=1, source_target_pairs={{11,15},{3,2},{5,4},{7,8},{27,31},{19,18},{21,20},{23,24},{43,47},... | collective-permute-start | bytes 393224 | tf_op jit(solution)/shard_map/ppermute | solution.py:321
  20.8 0.7 %collective-permute-start.17 = (bf16[256,256]{1,0:T(8,128)(2,1)S(1)}, bf16[256,256]{1,0:T(8,128)(2,1)S(1)}, u32[]{:S(2)}, u32[]{:S(2)}) collective-permute-start(bf16[256,256]{1,0:T(8,128)(2,1)S(1)} %get-tuple-element.94), channel_id=1, source_target_pairs={{13,15},{9,11},{29,31},{25,27},{45,47},{41,43},{61,63},{57,59},{77... | collective-permute-start | bytes 393224 | tf_op jit(solution)/shard_map/ppermute | solution.py:321
  21.5 1.3 %collective-permute-start.16 = (bf16[256,256]{1,0:T(8,128)(2,1)S(1)}, bf16[256,256]{1,0:T(8,128)(2,1)S(1)}, u32[]{:S(2)}, u32[]{:S(2)}) collective-permute-start(bf16[256,256]{1,0:T(8,128)(2,1)S(1)} %get-tuple-element.94), channel_id=1, source_target_pairs={{13,14},{9,10},{11,12},{7,6},{29,30},{25,26},{27,28},{23,22},{45,4... | collective-permute-start | bytes 393224 | tf_op jit(solution)/shard_map/ppermute | solution.py:321
  22.8 20.3 %collective-permute-done.16.got8b = bf16[256,256]{1,0:T(8,128)(2,1)S(1)} collective-permute-done((bf16[256,256]{1,0:T(8,128)(2,1)S(1)}, bf16[256,256]{1,0:T(8,128)(2,1)S(1)}, u32[]{:S(2)}, u32[]{:S(2)}) %collective-permute-start.16) | collective-permute-done | bytes 131104 | tf_op jit(solution)/shard_map/ppermute | solution.py:321
  43.2 2.3 %last_sweep.1 = f32[4,256,256]{2,1,0:T(8,128)} custom-call(f32[256,256]{1,0:T(8,128)S(1)} %get-tuple-element.62.start, bf16[256,256]{1,0:T(8,128)(2,1)S(1)} %collective-permute-done.16.got8b, bf16[256,256]{1,0:T(8,128)(2,1)S(1)} %collective-permute-done.17.got8, bf16[256,256]{1,0:T(8,128)(2,1)S(1)} %collective-permute-done.5.got.early3.got3, ...), custom_call_target="tpu_custom_call" | custom-call | flops 1207959552 | bytes 1048576 | tf_op jit(solution)/shard_map/last_sweep/pallas_call | solution.py:58
  (27 shorter events, 0.3 us)
Async XLA Ops:
  0.1 7.9 %collective-permute-start = (bf16[256,256]{1,0:T(8,128)(2,1)S(1)}, bf16[256,256]{1,0:T(8,128)(2,1)S(1)}, u32[]{:S(2)}, u32[]{:S(2)}) collective-permute-start(bf16[256,256]{1,0:T(8,128)(2,1)S(1)} %get-tuple-element.51.refs_6_), channel_id=1, source_target_pairs={{1,2},{3,4},{5,6},{7,8},{9,10},{11,12},{13,14},{17,18},{19,20},{21... | collective-permute-start | bytes 393224 | tf_op jit(solution)/shard_map/ppermute | solution.py:321
  5.0 3.0 %collective-permute-start.1 = (bf16[256,256]{1,0:T(8,128)(2,1)S(1)}, bf16[256,256]{1,0:T(8,128)(2,1)S(1)}, u32[]{:S(2)}, u32[]{:S(2)}) collective-permute-start(bf16[256,256]{1,0:T(8,128)(2,1)S(1)} %get-tuple-element.60), channel_id=1, source_target_pairs={{0,1},{2,3},{4,5},{6,7},{8,9},{10,11},{12,13},{14,15},{16,17},{18,... | collective-permute-start | bytes 393224 | tf_op jit(solution)/shard_map/ppermute | solution.py:321
  6.3 6.3 %collective-permute-start.3 = (bf16[256,2304]{1,0:T(8,128)(2,1)S(1)}, bf16[256,2304]{1,0:T(8,128)(2,1)S(1)}, u32[]{:S(2)}, u32[]{:S(2)}) collective-permute-start(bf16[256,2304]{1,0:T(8,128)(2,1)S(1)} %get-tuple-element.57.own_w), channel_id=1, source_target_pairs={{0,1},{2,3},{4,5},{6,7},{8,9},{10,11},{12,13},{14,15},{16,17},{18,... | collective-permute-start | bytes 3538952 | tf_op jit(solution)/shard_map/ppermute | solution.py:321
  8.0 4.6 %collective-permute-start.5 = (bf16[256,256]{1,0:T(8,128)(2,1)S(1)}, bf16[256,256]{1,0:T(8,128)(2,1)S(1)}, u32[]{:S(2)}, u32[]{:S(2)}) collective-permute-start(bf16[256,256]{1,0:T(8,128)(2,1)S(1)} %get-tuple-element.68), channel_id=1, source_target_pairs={{1,3},{17,19},{33,35},{49,51},{65,67},{81,83},{97,99},{113,115},{1... | collective-permute-start | bytes 393224 | tf_op jit(solution)/shard_map/ppermute | solution.py:321
  10.6 2.3 %collective-permute-start.2 = (bf16[256,256]{1,0:T(8,128)(2,1)S(1)}, bf16[256,256]{1,0:T(8,128)(2,1)S(1)}, u32[]{:S(2)}, u32[]{:S(2)}) collective-permute-start(bf16[256,256]{1,0:T(8,128)(2,1)S(1)} %get-tuple-element.63), channel_id=1, source_target_pairs={{0,1},{2,3},{4,5},{6,7},{8,9},{10,11},{12,13},{14,15},{16,17},{18,... | collective-permute-start | bytes 393224 | tf_op jit(solution)/shard_map/ppermute | solution.py:321
  11.9 1.6 %collective-permute-start.4 = (f32[256,256]{1,0:T(8,128)S(1)}, f32[256,256]{1,0:T(8,128)S(1)}, u32[]{:S(2)}, u32[]{:S(2)}) collective-permute-start(f32[256,256]{1,0:T(8,128)S(1)} %get-tuple-element.67), channel_id=1, source_target_pairs={{4,5},{8,9},{20,21},{24,25},{36,37},{40,41},{52,53},{56,57},{68,69... | collective-permute-start | bytes 786440 | tf_op jit(solution)/shard_map/ppermute | solution.py:321
  12.8 1.4 %collective-permute-start.7 = (bf16[256,256]{1,0:T(8,128)(2,1)S(1)}, bf16[256,256]{1,0:T(8,128)(2,1)S(1)}, u32[]{:S(2)}, u32[]{:S(2)}) collective-permute-start(bf16[256,256]{1,0:T(8,128)(2,1)S(1)} %get-tuple-element.74), channel_id=1, source_target_pairs={{3,5},{19,21},{35,37},{51,53},{67,69},{83,85},{99,101},{115,117},{... | collective-permute-start | bytes 393224 | tf_op jit(solution)/shard_map/ppermute | solution.py:321
  13.5 1.6 %collective-permute-start.6 = (bf16[256,256]{1,0:T(8,128)(2,1)S(1)}, bf16[256,256]{1,0:T(8,128)(2,1)S(1)}, u32[]{:S(2)}, u32[]{:S(2)}) collective-permute-start(bf16[256,256]{1,0:T(8,128)(2,1)S(1)} %get-tuple-element.73), channel_id=1, source_target_pairs={{5,7},{21,23},{37,39},{53,55},{69,71},{85,87},{101,103},{117,119},... | collective-permute-start | bytes 393224 | tf_op jit(solution)/shard_map/ppermute | solution.py:321
  14.4 2.7 %collective-permute-start.9 = (bf16[256,256]{1,0:T(8,128)(2,1)S(1)}, bf16[256,256]{1,0:T(8,128)(2,1)S(1)}, u32[]{:S(2)}, u32[]{:S(2)}) collective-permute-start(bf16[256,256]{1,0:T(8,128)(2,1)S(1)} %get-tuple-element.78), channel_id=1, source_target_pairs={{5,7},{21,23},{37,39},{53,55},{69,71},{85,87},{101,103},{117,119},... | collective-permute-start | bytes 393224 | tf_op jit(solution)/shard_map/ppermute | solution.py:321
  15.1 2.7 %collective-permute-start.11 = (bf16[256,256]{1,0:T(8,128)(2,1)S(1)}, bf16[256,256]{1,0:T(8,128)(2,1)S(1)}, u32[]{:S(2)}, u32[]{:S(2)}) collective-permute-start(bf16[256,256]{1,0:T(8,128)(2,1)S(1)} %get-tuple-element.77), channel_id=1, source_target_pairs={{7,9},{23,25},{39,41},{55,57},{71,73},{87,89},{103,105},{119,121},... | collective-permute-start | bytes 393224 | tf_op jit(solution)/shard_map/ppermute | solution.py:321
  15.8 2.1 %collective-permute-start.10 = (bf16[256,256]{1,0:T(8,128)(2,1)S(1)}, bf16[256,256]{1,0:T(8,128)(2,1)S(1)}, u32[]{:S(2)}, u32[]{:S(2)}) collective-permute-start(bf16[256,256]{1,0:T(8,128)(2,1)S(1)} %get-tuple-element.73), channel_id=1, source_target_pairs={{9,11},{25,27},{41,43},{57,59},{73,75},{89,91},{105,107},{121,123}... | collective-permute-start | bytes 393224 | tf_op jit(solution)/shard_map/ppermute | solution.py:321
  16.5 2.8 %collective-permute-start.8 = (bf16[256,256]{1,0:T(8,128)(2,1)S(1)}, bf16[256,256]{1,0:T(8,128)(2,1)S(1)}, u32[]{:S(2)}, u32[]{:S(2)}) collective-permute-start(bf16[256,256]{1,0:T(8,128)(2,1)S(1)} %get-tuple-element.77), channel_id=1, source_target_pairs={{7,11},{23,27},{39,43},{55,59},{71,75},{87,91},{103,107},{119,123}... | collective-permute-start | bytes 393224 | tf_op jit(solution)/shard_map/ppermute | solution.py:321
  17.2 2.2 %collective-permute-start.12 = (bf16[256,256]{1,0:T(8,128)(2,1)S(1)}, bf16[256,256]{1,0:T(8,128)(2,1)S(1)}, u32[]{:S(2)}, u32[]{:S(2)}) collective-permute-start(bf16[256,256]{1,0:T(8,128)(2,1)S(1)} %get-tuple-element.80.other.mine), channel_id=1, source_target_pairs={{7,11},{23,27},{39,43},{55,59},{71,75},{87,91},{103,107},{119,123}... | collective-permute-start | bytes 393224 | tf_op jit(solution)/shard_map/ppermute | solution.py:321
  17.9 1.4 %collective-permute-start.13 = (bf16[256,256]{1,0:T(8,128)(2,1)S(1)}, bf16[256,256]{1,0:T(8,128)(2,1)S(1)}, u32[]{:S(2)}, u32[]{:S(2)}) collective-permute-start(bf16[256,256]{1,0:T(8,128)(2,1)S(1)} %get-tuple-element.90), channel_id=1, source_target_pairs={{9,11},{11,13},{25,27},{27,29},{41,43},{43,45},{57,59},{59,61},{73... | collective-permute-start | bytes 393224 | tf_op jit(solution)/shard_map/ppermute | solution.py:321
  18.6 2.1 %collective-permute-start.14 = (bf16[256,256]{1,0:T(8,128)(2,1)S(1)}, bf16[256,256]{1,0:T(8,128)(2,1)S(1)}, u32[]{:S(2)}, u32[]{:S(2)}) collective-permute-start(bf16[256,256]{1,0:T(8,128)(2,1)S(1)} %get-tuple-element.83.other), channel_id=1, source_target_pairs={{7,9},{11,15},{23,25},{27,31},{39,41},{43,47},{55,57},{59,63},{71,... | collective-permute-start | bytes 393224 | tf_op jit(solution)/shard_map/ppermute | solution.py:321
  19.4 1.4 %collective-permute-start.15 = (bf16[256,256]{1,0:T(8,128)(2,1)S(1)}, bf16[256,256]{1,0:T(8,128)(2,1)S(1)}, u32[]{:S(2)}, u32[]{:S(2)}) collective-permute-start(bf16[256,256]{1,0:T(8,128)(2,1)S(1)} %get-tuple-element.92.mine), channel_id=1, source_target_pairs={{11,13},{13,15},{27,29},{29,31},{43,45},{45,47},{59,61},{61,63},{7... | collective-permute-start | bytes 393224 | tf_op jit(solution)/shard_map/ppermute | solution.py:321
  20.1 2.7 %collective-permute-start.18 = (bf16[256,256]{1,0:T(8,128)(2,1)S(1)}, bf16[256,256]{1,0:T(8,128)(2,1)S(1)}, u32[]{:S(2)}, u32[]{:S(2)}) collective-permute-start(bf16[256,256]{1,0:T(8,128)(2,1)S(1)} %get-tuple-element.92.mine), channel_id=1, source_target_pairs={{11,15},{3,2},{5,4},{7,8},{27,31},{19,18},{21,20},{23,24},{43,47},... | collective-permute-start | bytes 393224 | tf_op jit(solution)/shard_map/ppermute | solution.py:321
  20.8 2.0 %collective-permute-start.17 = (bf16[256,256]{1,0:T(8,128)(2,1)S(1)}, bf16[256,256]{1,0:T(8,128)(2,1)S(1)}, u32[]{:S(2)}, u32[]{:S(2)}) collective-permute-start(bf16[256,256]{1,0:T(8,128)(2,1)S(1)} %get-tuple-element.94), channel_id=1, source_target_pairs={{13,15},{9,11},{29,31},{25,27},{45,47},{41,43},{61,63},{57,59},{77... | collective-permute-start | bytes 393224 | tf_op jit(solution)/shard_map/ppermute | solution.py:321
  21.5 21.7 %collective-permute-start.16 = (bf16[256,256]{1,0:T(8,128)(2,1)S(1)}, bf16[256,256]{1,0:T(8,128)(2,1)S(1)}, u32[]{:S(2)}, u32[]{:S(2)}) collective-permute-start(bf16[256,256]{1,0:T(8,128)(2,1)S(1)} %get-tuple-element.94), channel_id=1, source_target_pairs={{13,14},{9,10},{11,12},{7,6},{29,30},{25,26},{27,28},{23,22},{45,4... | collective-permute-start | bytes 393224 | tf_op jit(solution)/shard_map/ppermute | solution.py:321

commit v9 on v8

--- a/solution.py
+++ b/solution.py
@@ -404,6 +404,9 @@
     upper7 = pair((7,), False, got3_rest, "relax_rest")
     got4_rest = send(upper7, [(7, 9)])
     upper_prev = send(upper7, [(7, 11)])
+    got3_last, solved = kernel_call(
+        in_order, [narrow, wide], [got3_last, solved], "last_first", 1, aliases={0: 0, 1: 1}
+    )
     z2 = pair((7,), True, got5, "again_end_lead")
     got6 = send(z2, [(7, 11)])
     got4_rest, solved = kernel_call(

time: 46 us -> 45.9 us (level)
    pallas_call x21 -> x22, Pallas kernels: 8.32 us -> 8.32 us  [kernel_call(): pl.pallas_call(body, out_shape=outs, in_specs=[pl.BlockSpec(memory_space=...]
where the time goes in v9:
time: 45.9 us; the launch traced here: 45.5 us
  waiting for transfers between devices  20.7 us (45%)
  starting transfers between devices  15.9 us (35%)
  Pallas kernels  8.32 us (18%)
  between operations  0.58 us (1%)
    ppermute x19, waiting for transfers between devices, send(): return lax.ppermute(value, 'layer', pairs)  20.7 us
    ppermute x19, starting transfers between devices, send(): return lax.ppermute(value, 'layer', pairs)  15.9 us
    pallas_call x22, Pallas kernels, kernel_call(): pl.pallas_call(body, out_shape=outs, in_specs=[pl.BlockSpec(memory_space=...  8.32 us
  transfers between devices with their start and end apart: 19, of which 3 were waited for; matrix products, arithmetic and copies ran while one was open for 0% of the time, Pallas kernels for 13%

profile of v9, /device:TPU:248, one launch (start us, length us, event | category | flops | bytes accessed | tf_op | source)
XLA Modules:
  0.0 45.5 jit_solution(5381312586341996769)
XLA Ops:
  0.1 1.3 %collective-permute-start = (bf16[256,256]{1,0:T(8,128)(2,1)S(1)}, bf16[256,256]{1,0:T(8,128)(2,1)S(1)}, u32[]{:S(2)}, u32[]{:S(2)}) collective-permute-start(bf16[256,256]{1,0:T(8,128)(2,1)S(1)} %get-tuple-element.53.refs_6_), channel_id=1, source_target_pairs={{1,2},{3,4},{5,6},{7,8},{9,10},{11,12},{13,14},{17,18},{19,20},{21... | collective-permute-start | bytes 393224 | tf_op jit(solution)/shard_map/ppermute | solution.py:321
  1.4 3.7 %first_sweep_even.1 = (bf16[256,256]{1,0:T(8,128)(2,1)S(1)}, bf16[256,2304]{1,0:T(8,128)(2,1)S(1)}, bf16[3,256,2304]{2,1,0:T(8,128)(2,1)S(1)}, f32[256,256]{1,0:T(8,128)S(1)}) custom-call(f32[256,256]{1,0:T(8,128)} %inputs.1, f32[1,256,256]{2,1,0:T(8,128)} %refs_1_.3, ...), custom_call_target="tpu_custom_call", output_to_operand_aliasing={{1}: (3, {}), {2}: (4, {}), {3}: (5, {})} | custom-call | flops 1207959552 | bytes 1048576 | tf_op jit(solution)/shard_map/first_sweep_even/pallas_call | solution.py:58
  5.0 1.3 %collective-permute-start.1 = (bf16[256,256]{1,0:T(8,128)(2,1)S(1)}, bf16[256,256]{1,0:T(8,128)(2,1)S(1)}, u32[]{:S(2)}, u32[]{:S(2)}) collective-permute-start(bf16[256,256]{1,0:T(8,128)(2,1)S(1)} %get-tuple-element.62), channel_id=1, source_target_pairs={{0,1},{2,3},{4,5},{6,7},{8,9},{10,11},{12,13},{14,15},{16,17},{18,... | collective-permute-start | bytes 393224 | tf_op jit(solution)/shard_map/ppermute | solution.py:321
  6.3 1.4 %collective-permute-start.3 = (bf16[256,2304]{1,0:T(8,128)(2,1)S(1)}, bf16[256,2304]{1,0:T(8,128)(2,1)S(1)}, u32[]{:S(2)}, u32[]{:S(2)}) collective-permute-start(bf16[256,2304]{1,0:T(8,128)(2,1)S(1)} %get-tuple-element.59.own_w), channel_id=1, source_target_pairs={{0,1},{2,3},{4,5},{6,7},{8,9},{10,11},{12,13},{14,15},{16,17},{18,... | collective-permute-start | bytes 3538952 | tf_op jit(solution)/shard_map/ppermute | solution.py:321
  7.7 0.3 collective-permute-done.refs_0_
  8.0 0.7 %collective-permute-start.5 = (bf16[256,256]{1,0:T(8,128)(2,1)S(1)}, bf16[256,256]{1,0:T(8,128)(2,1)S(1)}, u32[]{:S(2)}, u32[]{:S(2)}) collective-permute-start(bf16[256,256]{1,0:T(8,128)(2,1)S(1)} %get-tuple-element.70), channel_id=1, source_target_pairs={{1,3},{17,19},{33,35},{49,51},{65,67},{81,83},{97,99},{113,115},{1... | collective-permute-start | bytes 393224 | tf_op jit(solution)/shard_map/ppermute | solution.py:321
  8.6 1.9 %second_sweep_even.1 = (f32[256,256]{1,0:T(8,128)S(1)}, f32[256,256]{1,0:T(8,128)S(1)}, f32[256,256]{1,0:T(8,128)S(1)}, f32[256,256]{1,0:T(8,128)S(1)}, bf16[256,256]{1,0:T(8,128)(2,1)S(1)}) custom-call(bf16[256,256]{1,0:T(8,128)(2,1)S(1)} %get-tuple-element.58.left_even, ...), custom_call_target="tpu_custom_call", output_to_operand_aliasing={{2}: (4, {}), {3}: (5, {})} | custom-call | flops 1207959552 | bytes 1048576 | tf_op jit(solution)/shard_map/second_sweep_even/pallas_call | solution.py:58
  10.6 1.3 %collective-permute-start.2 = (bf16[256,256]{1,0:T(8,128)(2,1)S(1)}, bf16[256,256]{1,0:T(8,128)(2,1)S(1)}, u32[]{:S(2)}, u32[]{:S(2)}) collective-permute-start(bf16[256,256]{1,0:T(8,128)(2,1)S(1)} %get-tuple-element.65), channel_id=1, source_target_pairs={{0,1},{2,3},{4,5},{6,7},{8,9},{10,11},{12,13},{14,15},{16,17},{18,... | collective-permute-start | bytes 393224 | tf_op jit(solution)/shard_map/ppermute | solution.py:321
  11.9 0.7 %collective-permute-start.4 = (f32[256,256]{1,0:T(8,128)S(1)}, f32[256,256]{1,0:T(8,128)S(1)}, u32[]{:S(2)}, u32[]{:S(2)}) collective-permute-start(f32[256,256]{1,0:T(8,128)S(1)} %get-tuple-element.69), channel_id=1, source_target_pairs={{4,5},{8,9},{20,21},{24,25},{36,37},{40,41},{52,53},{56,57},{68,69... | collective-permute-start | bytes 786440 | tf_op jit(solution)/shard_map/ppermute | solution.py:321
  12.6 0.2 collective-permute-done.2.even_rhs
  12.8 0.7 %collective-permute-start.7 = (bf16[256,256]{1,0:T(8,128)(2,1)S(1)}, bf16[256,256]{1,0:T(8,128)(2,1)S(1)}, u32[]{:S(2)}, u32[]{:S(2)}) collective-permute-start(bf16[256,256]{1,0:T(8,128)(2,1)S(1)} %get-tuple-element.76), channel_id=1, source_target_pairs={{3,5},{19,21},{35,37},{51,53},{67,69},{83,85},{99,101},{115,117},{... | collective-permute-start | bytes 393224 | tf_op jit(solution)/shard_map/ppermute | solution.py:321
  13.5 0.0 collective-permute-done.4.first
  13.5 0.7 %collective-permute-start.6 = (bf16[256,256]{1,0:T(8,128)(2,1)S(1)}, bf16[256,256]{1,0:T(8,128)(2,1)S(1)}, u32[]{:S(2)}, u32[]{:S(2)}) collective-permute-start(bf16[256,256]{1,0:T(8,128)(2,1)S(1)} %get-tuple-element.75), channel_id=1, source_target_pairs={{5,7},{21,23},{37,39},{53,55},{69,71},{85,87},{101,103},{117,119},... | collective-permute-start | bytes 393224 | tf_op jit(solution)/shard_map/ppermute | solution.py:321
  14.2 0.7 %collective-permute-start.10 = (bf16[256,256]{1,0:T(8,128)(2,1)S(1)}, bf16[256,256]{1,0:T(8,128)(2,1)S(1)}, u32[]{:S(2)}, u32[]{:S(2)}) collective-permute-start(bf16[256,256]{1,0:T(8,128)(2,1)S(1)} %get-tuple-element.75), channel_id=1, source_target_pairs={{9,11},{25,27},{41,43},{57,59},{73,75},{89,91},{105,107},{121,123}... | collective-permute-start | bytes 393224 | tf_op jit(solution)/shard_map/ppermute | solution.py:321
  14.9 0.0 collective-permute-done.7.got.early4.got4
  14.9 0.2 again_lead.1
  15.1 0.7 %collective-permute-start.9 = (bf16[256,256]{1,0:T(8,128)(2,1)S(1)}, bf16[256,256]{1,0:T(8,128)(2,1)S(1)}, u32[]{:S(2)}, u32[]{:S(2)}) collective-permute-start(bf16[256,256]{1,0:T(8,128)(2,1)S(1)} %get-tuple-element.80), channel_id=1, source_target_pairs={{5,7},{21,23},{37,39},{53,55},{69,71},{85,87},{101,103},{117,119},... | collective-permute-start | bytes 393224 | tf_op jit(solution)/shard_map/ppermute | solution.py:321
  15.8 0.0 collective-permute-done.6.got
  15.8 0.7 %collective-permute-start.11 = (bf16[256,256]{1,0:T(8,128)(2,1)S(1)}, bf16[256,256]{1,0:T(8,128)(2,1)S(1)}, u32[]{:S(2)}, u32[]{:S(2)}) collective-permute-start(bf16[256,256]{1,0:T(8,128)(2,1)S(1)} %get-tuple-element.79), channel_id=1, source_target_pairs={{7,9},{23,25},{39,41},{55,57},{71,73},{87,89},{103,105},{119,121},... | collective-permute-start | bytes 393224 | tf_op jit(solution)/shard_map/ppermute | solution.py:321
  16.5 0.7 %collective-permute-start.8 = (bf16[256,256]{1,0:T(8,128)(2,1)S(1)}, bf16[256,256]{1,0:T(8,128)(2,1)S(1)}, u32[]{:S(2)}, u32[]{:S(2)}) collective-permute-start(bf16[256,256]{1,0:T(8,128)(2,1)S(1)} %get-tuple-element.79), channel_id=1, source_target_pairs={{7,11},{23,27},{39,43},{55,59},{71,75},{87,91},{103,107},{119,123}... | collective-permute-start | bytes 393224 | tf_op jit(solution)/shard_map/ppermute | solution.py:321
  17.2 0.7 %collective-permute-start.12 = (bf16[256,256]{1,0:T(8,128)(2,1)S(1)}, bf16[256,256]{1,0:T(8,128)(2,1)S(1)}, u32[]{:S(2)}, u32[]{:S(2)}) collective-permute-start(bf16[256,256]{1,0:T(8,128)(2,1)S(1)} %get-tuple-element.83.other.mine), channel_id=1, source_target_pairs={{7,11},{23,27},{39,43},{55,59},{71,75},{87,91},{103,107},{119,123}... | collective-permute-start | bytes 393224 | tf_op jit(solution)/shard_map/ppermute | solution.py:321
  18.0 0.7 %collective-permute-start.13 = (bf16[256,256]{1,0:T(8,128)(2,1)S(1)}, bf16[256,256]{1,0:T(8,128)(2,1)S(1)}, u32[]{:S(2)}, u32[]{:S(2)}) collective-permute-start(bf16[256,256]{1,0:T(8,128)(2,1)S(1)} %get-tuple-element.94), channel_id=1, source_target_pairs={{9,11},{11,13},{25,27},{27,29},{41,43},{43,45},{57,59},{59,61},{73... | collective-permute-start | bytes 393224 | tf_op jit(solution)/shard_map/ppermute | solution.py:321
  18.6 0.7 %collective-permute-start.14 = (bf16[256,256]{1,0:T(8,128)(2,1)S(1)}, bf16[256,256]{1,0:T(8,128)(2,1)S(1)}, u32[]{:S(2)}, u32[]{:S(2)}) collective-permute-start(bf16[256,256]{1,0:T(8,128)(2,1)S(1)} %get-tuple-element.87.other), channel_id=1, source_target_pairs={{7,9},{11,15},{23,25},{27,31},{39,41},{43,47},{55,57},{59,63},{71,... | collective-permute-start | bytes 393224 | tf_op jit(solution)/shard_map/ppermute | solution.py:321
  19.3 0.0 collective-permute-done.12.lead
  19.4 0.0 collective-permute-done.13.got
  19.4 0.7 %collective-permute-start.15 = (bf16[256,256]{1,0:T(8,128)(2,1)S(1)}, bf16[256,256]{1,0:T(8,128)(2,1)S(1)}, u32[]{:S(2)}, u32[]{:S(2)}) collective-permute-start(bf16[256,256]{1,0:T(8,128)(2,1)S(1)} %get-tuple-element.96.mine), channel_id=1, source_target_pairs={{11,13},{13,15},{27,29},{29,31},{43,45},{45,47},{59,61},{61,63},{7... | collective-permute-start | bytes 393224 | tf_op jit(solution)/shard_map/ppermute | solution.py:321
  20.1 0.7 %collective-permute-start.18 = (bf16[256,256]{1,0:T(8,128)(2,1)S(1)}, bf16[256,256]{1,0:T(8,128)(2,1)S(1)}, u32[]{:S(2)}, u32[]{:S(2)}) collective-permute-start(bf16[256,256]{1,0:T(8,128)(2,1)S(1)} %get-tuple-element.96.mine), channel_id=1, source_target_pairs={{11,15},{3,2},{5,4},{7,8},{27,31},{19,18},{21,20},{23,24},{43,47},... | collective-permute-start | bytes 393224 | tf_op jit(solution)/shard_map/ppermute | solution.py:321
  20.8 0.0 collective-permute-done.15.got.got7
  20.8 0.7 %collective-permute-start.17 = (bf16[256,256]{1,0:T(8,128)(2,1)S(1)}, bf16[256,256]{1,0:T(8,128)(2,1)S(1)}, u32[]{:S(2)}, u32[]{:S(2)}) collective-permute-start(bf16[256,256]{1,0:T(8,128)(2,1)S(1)} %get-tuple-element.98), channel_id=1, source_target_pairs={{13,15},{9,11},{29,31},{25,27},{45,47},{41,43},{61,63},{57,59},{77... | collective-permute-start | bytes 393224 | tf_op jit(solution)/shard_map/ppermute | solution.py:321
  21.5 1.3 %collective-permute-start.16 = (bf16[256,256]{1,0:T(8,128)(2,1)S(1)}, bf16[256,256]{1,0:T(8,128)(2,1)S(1)}, u32[]{:S(2)}, u32[]{:S(2)}) collective-permute-start(bf16[256,256]{1,0:T(8,128)(2,1)S(1)} %get-tuple-element.98), channel_id=1, source_target_pairs={{13,14},{9,10},{11,12},{7,6},{29,30},{25,26},{27,28},{23,22},{45,4... | collective-permute-start | bytes 393224 | tf_op jit(solution)/shard_map/ppermute | solution.py:321
  22.9 20.2 %collective-permute-done.16.got8b = bf16[256,256]{1,0:T(8,128)(2,1)S(1)} collective-permute-done((bf16[256,256]{1,0:T(8,128)(2,1)S(1)}, bf16[256,256]{1,0:T(8,128)(2,1)S(1)}, u32[]{:S(2)}, u32[]{:S(2)}) %collective-permute-start.16) | collective-permute-done | bytes 131104 | tf_op jit(solution)/shard_map/ppermute | solution.py:321
  43.1 2.3 %last_sweep.1 = f32[4,256,256]{2,1,0:T(8,128)} custom-call(f32[256,256]{1,0:T(8,128)S(1)} %get-tuple-element.64.start, bf16[256,256]{1,0:T(8,128)(2,1)S(1)} %collective-permute-done.16.got8b, bf16[256,256]{1,0:T(8,128)(2,1)S(1)} %collective-permute-done.17.got8, bf16[256,256]{1,0:T(8,128)(2,1)S(1)} %collective-permute-done.5.got.early3.got3, ...), custom_call_target="tpu_custom_call" | custom-call | flops 1207959552 | bytes 1048576 | tf_op jit(solution)/shard_map/last_sweep/pallas_call | solution.py:58
  (28 shorter events, 0.3 us)
Async XLA Ops:
  0.1 7.9 %collective-permute-start = (bf16[256,256]{1,0:T(8,128)(2,1)S(1)}, bf16[256,256]{1,0:T(8,128)(2,1)S(1)}, u32[]{:S(2)}, u32[]{:S(2)}) collective-permute-start(bf16[256,256]{1,0:T(8,128)(2,1)S(1)} %get-tuple-element.53.refs_6_), channel_id=1, source_target_pairs={{1,2},{3,4},{5,6},{7,8},{9,10},{11,12},{13,14},{17,18},{19,20},{21... | collective-permute-start | bytes 393224 | tf_op jit(solution)/shard_map/ppermute | solution.py:321
  5.0 3.0 %collective-permute-start.1 = (bf16[256,256]{1,0:T(8,128)(2,1)S(1)}, bf16[256,256]{1,0:T(8,128)(2,1)S(1)}, u32[]{:S(2)}, u32[]{:S(2)}) collective-permute-start(bf16[256,256]{1,0:T(8,128)(2,1)S(1)} %get-tuple-element.62), channel_id=1, source_target_pairs={{0,1},{2,3},{4,5},{6,7},{8,9},{10,11},{12,13},{14,15},{16,17},{18,... | collective-permute-start | bytes 393224 | tf_op jit(solution)/shard_map/ppermute | solution.py:321
  6.3 6.3 %collective-permute-start.3 = (bf16[256,2304]{1,0:T(8,128)(2,1)S(1)}, bf16[256,2304]{1,0:T(8,128)(2,1)S(1)}, u32[]{:S(2)}, u32[]{:S(2)}) collective-permute-start(bf16[256,2304]{1,0:T(8,128)(2,1)S(1)} %get-tuple-element.59.own_w), channel_id=1, source_target_pairs={{0,1},{2,3},{4,5},{6,7},{8,9},{10,11},{12,13},{14,15},{16,17},{18,... | collective-permute-start | bytes 3538952 | tf_op jit(solution)/shard_map/ppermute | solution.py:321
  8.0 4.6 %collective-permute-start.5 = (bf16[256,256]{1,0:T(8,128)(2,1)S(1)}, bf16[256,256]{1,0:T(8,128)(2,1)S(1)}, u32[]{:S(2)}, u32[]{:S(2)}) collective-permute-start(bf16[256,256]{1,0:T(8,128)(2,1)S(1)} %get-tuple-element.70), channel_id=1, source_target_pairs={{1,3},{17,19},{33,35},{49,51},{65,67},{81,83},{97,99},{113,115},{1... | collective-permute-start | bytes 393224 | tf_op jit(solution)/shard_map/ppermute | solution.py:321
  10.6 2.3 %collective-permute-start.2 = (bf16[256,256]{1,0:T(8,128)(2,1)S(1)}, bf16[256,256]{1,0:T(8,128)(2,1)S(1)}, u32[]{:S(2)}, u32[]{:S(2)}) collective-permute-start(bf16[256,256]{1,0:T(8,128)(2,1)S(1)} %get-tuple-element.65), channel_id=1, source_target_pairs={{0,1},{2,3},{4,5},{6,7},{8,9},{10,11},{12,13},{14,15},{16,17},{18,... | collective-permute-start | bytes 393224 | tf_op jit(solution)/shard_map/ppermute | solution.py:321
  11.9 1.6 %collective-permute-start.4 = (f32[256,256]{1,0:T(8,128)S(1)}, f32[256,256]{1,0:T(8,128)S(1)}, u32[]{:S(2)}, u32[]{:S(2)}) collective-permute-start(f32[256,256]{1,0:T(8,128)S(1)} %get-tuple-element.69), channel_id=1, source_target_pairs={{4,5},{8,9},{20,21},{24,25},{36,37},{40,41},{52,53},{56,57},{68,69... | collective-permute-start | bytes 786440 | tf_op jit(solution)/shard_map/ppermute | solution.py:321
  12.8 2.1 %collective-permute-start.7 = (bf16[256,256]{1,0:T(8,128)(2,1)S(1)}, bf16[256,256]{1,0:T(8,128)(2,1)S(1)}, u32[]{:S(2)}, u32[]{:S(2)}) collective-permute-start(bf16[256,256]{1,0:T(8,128)(2,1)S(1)} %get-tuple-element.76), channel_id=1, source_target_pairs={{3,5},{19,21},{35,37},{51,53},{67,69},{83,85},{99,101},{115,117},{... | collective-permute-start | bytes 393224 | tf_op jit(solution)/shard_map/ppermute | solution.py:321
  13.5 2.2 %collective-permute-start.6 = (bf16[256,256]{1,0:T(8,128)(2,1)S(1)}, bf16[256,256]{1,0:T(8,128)(2,1)S(1)}, u32[]{:S(2)}, u32[]{:S(2)}) collective-permute-start(bf16[256,256]{1,0:T(8,128)(2,1)S(1)} %get-tuple-element.75), channel_id=1, source_target_pairs={{5,7},{21,23},{37,39},{53,55},{69,71},{85,87},{101,103},{117,119},... | collective-permute-start | bytes 393224 | tf_op jit(solution)/shard_map/ppermute | solution.py:321
  14.2 3.0 %collective-permute-start.10 = (bf16[256,256]{1,0:T(8,128)(2,1)S(1)}, bf16[256,256]{1,0:T(8,128)(2,1)S(1)}, u32[]{:S(2)}, u32[]{:S(2)}) collective-permute-start(bf16[256,256]{1,0:T(8,128)(2,1)S(1)} %get-tuple-element.75), channel_id=1, source_target_pairs={{9,11},{25,27},{41,43},{57,59},{73,75},{89,91},{105,107},{121,123}... | collective-permute-start | bytes 393224 | tf_op jit(solution)/shard_map/ppermute | solution.py:321
  15.1 2.1 %collective-permute-start.9 = (bf16[256,256]{1,0:T(8,128)(2,1)S(1)}, bf16[256,256]{1,0:T(8,128)(2,1)S(1)}, u32[]{:S(2)}, u32[]{:S(2)}) collective-permute-start(bf16[256,256]{1,0:T(8,128)(2,1)S(1)} %get-tuple-element.80), channel_id=1, source_target_pairs={{5,7},{21,23},{37,39},{53,55},{69,71},{85,87},{101,103},{117,119},... | collective-permute-start | bytes 393224 | tf_op jit(solution)/shard_map/ppermute | solution.py:321
  15.8 2.1 %collective-permute-start.11 = (bf16[256,256]{1,0:T(8,128)(2,1)S(1)}, bf16[256,256]{1,0:T(8,128)(2,1)S(1)}, u32[]{:S(2)}, u32[]{:S(2)}) collective-permute-start(bf16[256,256]{1,0:T(8,128)(2,1)S(1)} %get-tuple-element.79), channel_id=1, source_target_pairs={{7,9},{23,25},{39,41},{55,57},{71,73},{87,89},{103,105},{119,121},... | collective-permute-start | bytes 393224 | tf_op jit(solution)/shard_map/ppermute | solution.py:321
  16.5 2.8 %collective-permute-start.8 = (bf16[256,256]{1,0:T(8,128)(2,1)S(1)}, bf16[256,256]{1,0:T(8,128)(2,1)S(1)}, u32[]{:S(2)}, u32[]{:S(2)}) collective-permute-start(bf16[256,256]{1,0:T(8,128)(2,1)S(1)} %get-tuple-element.79), channel_id=1, source_target_pairs={{7,11},{23,27},{39,43},{55,59},{71,75},{87,91},{103,107},{119,123}... | collective-permute-start | bytes 393224 | tf_op jit(solution)/shard_map/ppermute | solution.py:321
  17.2 2.1 %collective-permute-start.12 = (bf16[256,256]{1,0:T(8,128)(2,1)S(1)}, bf16[256,256]{1,0:T(8,128)(2,1)S(1)}, u32[]{:S(2)}, u32[]{:S(2)}) collective-permute-start(bf16[256,256]{1,0:T(8,128)(2,1)S(1)} %get-tuple-element.83.other.mine), channel_id=1, source_target_pairs={{7,11},{23,27},{39,43},{55,59},{71,75},{87,91},{103,107},{119,123}... | collective-permute-start | bytes 393224 | tf_op jit(solution)/shard_map/ppermute | solution.py:321
  18.0 1.4 %collective-permute-start.13 = (bf16[256,256]{1,0:T(8,128)(2,1)S(1)}, bf16[256,256]{1,0:T(8,128)(2,1)S(1)}, u32[]{:S(2)}, u32[]{:S(2)}) collective-permute-start(bf16[256,256]{1,0:T(8,128)(2,1)S(1)} %get-tuple-element.94), channel_id=1, source_target_pairs={{9,11},{11,13},{25,27},{27,29},{41,43},{43,45},{57,59},{59,61},{73... | collective-permute-start | bytes 393224 | tf_op jit(solution)/shard_map/ppermute | solution.py:321
  18.6 2.1 %collective-permute-start.14 = (bf16[256,256]{1,0:T(8,128)(2,1)S(1)}, bf16[256,256]{1,0:T(8,128)(2,1)S(1)}, u32[]{:S(2)}, u32[]{:S(2)}) collective-permute-start(bf16[256,256]{1,0:T(8,128)(2,1)S(1)} %get-tuple-element.87.other), channel_id=1, source_target_pairs={{7,9},{11,15},{23,25},{27,31},{39,41},{43,47},{55,57},{59,63},{71,... | collective-permute-start | bytes 393224 | tf_op jit(solution)/shard_map/ppermute | solution.py:321
  19.4 1.4 %collective-permute-start.15 = (bf16[256,256]{1,0:T(8,128)(2,1)S(1)}, bf16[256,256]{1,0:T(8,128)(2,1)S(1)}, u32[]{:S(2)}, u32[]{:S(2)}) collective-permute-start(bf16[256,256]{1,0:T(8,128)(2,1)S(1)} %get-tuple-element.96.mine), channel_id=1, source_target_pairs={{11,13},{13,15},{27,29},{29,31},{43,45},{45,47},{59,61},{61,63},{7... | collective-permute-start | bytes 393224 | tf_op jit(solution)/shard_map/ppermute | solution.py:321
  20.1 2.7 %collective-permute-start.18 = (bf16[256,256]{1,0:T(8,128)(2,1)S(1)}, bf16[256,256]{1,0:T(8,128)(2,1)S(1)}, u32[]{:S(2)}, u32[]{:S(2)}) collective-permute-start(bf16[256,256]{1,0:T(8,128)(2,1)S(1)} %get-tuple-element.96.mine), channel_id=1, source_target_pairs={{11,15},{3,2},{5,4},{7,8},{27,31},{19,18},{21,20},{23,24},{43,47},... | collective-permute-start | bytes 393224 | tf_op jit(solution)/shard_map/ppermute | solution.py:321
  20.8 2.0 %collective-permute-start.17 = (bf16[256,256]{1,0:T(8,128)(2,1)S(1)}, bf16[256,256]{1,0:T(8,128)(2,1)S(1)}, u32[]{:S(2)}, u32[]{:S(2)}) collective-permute-start(bf16[256,256]{1,0:T(8,128)(2,1)S(1)} %get-tuple-element.98), channel_id=1, source_target_pairs={{13,15},{9,11},{29,31},{25,27},{45,47},{41,43},{61,63},{57,59},{77... | collective-permute-start | bytes 393224 | tf_op jit(solution)/shard_map/ppermute | solution.py:321
  21.5 21.6 %collective-permute-start.16 = (bf16[256,256]{1,0:T(8,128)(2,1)S(1)}, bf16[256,256]{1,0:T(8,128)(2,1)S(1)}, u32[]{:S(2)}, u32[]{:S(2)}) collective-permute-start(bf16[256,256]{1,0:T(8,128)(2,1)S(1)} %get-tuple-element.98), channel_id=1, source_target_pairs={{13,14},{9,10},{11,12},{7,6},{29,30},{25,26},{27,28},{23,22},{45,4... | collective-permute-start | bytes 393224 | tf_op jit(solution)/shard_map/ppermute | solution.py:321

commit v10 on v8

--- a/solution.py
+++ b/solution.py
@@ -306,12 +306,10 @@
     term = conv_tanh(state, own_w)
     own = jnp.where(me % 2 == 0, rhs_of_even[...], rhs[...])
     end = jnp.where(me % 4 == 3, solved[...], state + term + own)
-    copies = [store(COARSEN - 1, end)]
-    state = state + 0.25 * term
-    copies.append(store(0, state))
-    for i in range(1, COARSEN - 1):
-        state = state + 0.25 * conv_tanh(state, later_w[i - 1])
-        copies.append(store(i, state))
+    first = state + 0.25 * term
+    middle = first + 0.25 * conv_tanh(first, later_w[0])
+    copies = [store(COARSEN - 1, end), store(0, first), store(1, middle)]
+    copies.append(store(2, middle + 0.25 * conv_tanh(middle, later_w[1])))
     for copy in copies:
         copy.wait()
 

time: 46 us -> 46 us (level)
  no operation moved by 1% of the time
where the time goes in v10:
time: 46 us; the launch traced here: 45.6 us
  waiting for transfers between devices  20.8 us (45%)
  starting transfers between devices  15.9 us (35%)
  Pallas kernels  8.32 us (18%)
  between operations  0.57 us (1%)
    ppermute x19, waiting for transfers between devices, send(): return lax.ppermute(value, 'layer', pairs)  20.8 us
    ppermute x19, starting transfers between devices, send(): return lax.ppermute(value, 'layer', pairs)  15.9 us
    pallas_call x21, Pallas kernels, kernel_call(): pl.pallas_call(body, out_shape=outs, in_specs=[pl.BlockSpec(memory_space=...  8.32 us
  transfers between devices with their start and end apart: 19, of which 3 were waited for; matrix products, arithmetic and copies ran while one was open for 0% of the time, Pallas kernels for 13%

profile of v10, /device:TPU:248, one launch (start us, length us, event | category | flops | bytes accessed | tf_op | source)
XLA Modules:
  0.0 45.6 jit_solution(9797345356486197553)
XLA Ops:
  0.1 1.3 %collective-permute-start = (bf16[256,256]{1,0:T(8,128)(2,1)S(1)}, bf16[256,256]{1,0:T(8,128)(2,1)S(1)}, u32[]{:S(2)}, u32[]{:S(2)}) collective-permute-start(bf16[256,256]{1,0:T(8,128)(2,1)S(1)} %get-tuple-element.51.refs_6_), channel_id=1, source_target_pairs={{1,2},{3,4},{5,6},{7,8},{9,10},{11,12},{13,14},{17,18},{19,20},{21... | collective-permute-start | bytes 393224 | tf_op jit(solution)/shard_map/ppermute | solution.py:319
  1.4 3.7 %first_sweep_even.1 = (bf16[256,256]{1,0:T(8,128)(2,1)S(1)}, bf16[256,2304]{1,0:T(8,128)(2,1)S(1)}, bf16[3,256,2304]{2,1,0:T(8,128)(2,1)S(1)}, f32[256,256]{1,0:T(8,128)S(1)}) custom-call(f32[256,256]{1,0:T(8,128)} %inputs.1, f32[1,256,256]{2,1,0:T(8,128)} %refs_1_.3, ...), custom_call_target="tpu_custom_call", output_to_operand_aliasing={{1}: (3, {}), {2}: (4, {}), {3}: (5, {})} | custom-call | flops 1207959552 | bytes 1048576 | tf_op jit(solution)/shard_map/first_sweep_even/pallas_call | solution.py:58
  5.0 1.3 %collective-permute-start.1 = (bf16[256,256]{1,0:T(8,128)(2,1)S(1)}, bf16[256,256]{1,0:T(8,128)(2,1)S(1)}, u32[]{:S(2)}, u32[]{:S(2)}) collective-permute-start(bf16[256,256]{1,0:T(8,128)(2,1)S(1)} %get-tuple-element.60), channel_id=1, source_target_pairs={{0,1},{2,3},{4,5},{6,7},{8,9},{10,11},{12,13},{14,15},{16,17},{18,... | collective-permute-start | bytes 393224 | tf_op jit(solution)/shard_map/ppermute | solution.py:319
  6.3 1.4 %collective-permute-start.3 = (bf16[256,2304]{1,0:T(8,128)(2,1)S(1)}, bf16[256,2304]{1,0:T(8,128)(2,1)S(1)}, u32[]{:S(2)}, u32[]{:S(2)}) collective-permute-start(bf16[256,2304]{1,0:T(8,128)(2,1)S(1)} %get-tuple-element.57.own_w), channel_id=1, source_target_pairs={{0,1},{2,3},{4,5},{6,7},{8,9},{10,11},{12,13},{14,15},{16,17},{18,... | collective-permute-start | bytes 3538952 | tf_op jit(solution)/shard_map/ppermute | solution.py:319
  7.7 0.3 collective-permute-done.refs_0_
  8.0 0.0 collective-permute-done.1.left_odd
  8.0 0.7 %collective-permute-start.5 = (bf16[256,256]{1,0:T(8,128)(2,1)S(1)}, bf16[256,256]{1,0:T(8,128)(2,1)S(1)}, u32[]{:S(2)}, u32[]{:S(2)}) collective-permute-start(bf16[256,256]{1,0:T(8,128)(2,1)S(1)} %get-tuple-element.68), channel_id=1, source_target_pairs={{1,3},{17,19},{33,35},{49,51},{65,67},{81,83},{97,99},{113,115},{1... | collective-permute-start | bytes 393224 | tf_op jit(solution)/shard_map/ppermute | solution.py:319
  8.6 1.9 %second_sweep_even.1 = (f32[256,256]{1,0:T(8,128)S(1)}, f32[256,256]{1,0:T(8,128)S(1)}, f32[256,256]{1,0:T(8,128)S(1)}, f32[256,256]{1,0:T(8,128)S(1)}, bf16[256,256]{1,0:T(8,128)(2,1)S(1)}) custom-call(bf16[256,256]{1,0:T(8,128)(2,1)S(1)} %get-tuple-element.56.left_even, ...), custom_call_target="tpu_custom_call", output_to_operand_aliasing={{2}: (4, {}), {3}: (5, {})} | custom-call | flops 1207959552 | bytes 1048576 | tf_op jit(solution)/shard_map/second_sweep_even/pallas_call | solution.py:58
  10.6 1.3 %collective-permute-start.2 = (bf16[256,256]{1,0:T(8,128)(2,1)S(1)}, bf16[256,256]{1,0:T(8,128)(2,1)S(1)}, u32[]{:S(2)}, u32[]{:S(2)}) collective-permute-start(bf16[256,256]{1,0:T(8,128)(2,1)S(1)} %get-tuple-element.63), channel_id=1, source_target_pairs={{0,1},{2,3},{4,5},{6,7},{8,9},{10,11},{12,13},{14,15},{16,17},{18,... | collective-permute-start | bytes 393224 | tf_op jit(solution)/shard_map/ppermute | solution.py:319
  11.9 0.7 %collective-permute-start.4 = (f32[256,256]{1,0:T(8,128)S(1)}, f32[256,256]{1,0:T(8,128)S(1)}, u32[]{:S(2)}, u32[]{:S(2)}) collective-permute-start(f32[256,256]{1,0:T(8,128)S(1)} %get-tuple-element.67), channel_id=1, source_target_pairs={{4,5},{8,9},{20,21},{24,25},{36,37},{40,41},{52,53},{56,57},{68,69... | collective-permute-start | bytes 786440 | tf_op jit(solution)/shard_map/ppermute | solution.py:319
  12.6 0.0 collective-permute-done.5.got.early3.got3
  12.6 0.0 collective-permute-done.3.even_w
  12.6 0.2 collective-permute-done.2.even_rhs
  12.8 0.7 %collective-permute-start.7 = (bf16[256,256]{1,0:T(8,128)(2,1)S(1)}, bf16[256,256]{1,0:T(8,128)(2,1)S(1)}, u32[]{:S(2)}, u32[]{:S(2)}) collective-permute-start(bf16[256,256]{1,0:T(8,128)(2,1)S(1)} %get-tuple-element.74), channel_id=1, source_target_pairs={{3,5},{19,21},{35,37},{51,53},{67,69},{83,85},{99,101},{115,117},{... | collective-permute-start | bytes 393224 | tf_op jit(solution)/shard_map/ppermute | solution.py:319
  13.5 0.7 %collective-permute-start.6 = (bf16[256,256]{1,0:T(8,128)(2,1)S(1)}, bf16[256,256]{1,0:T(8,128)(2,1)S(1)}, u32[]{:S(2)}, u32[]{:S(2)}) collective-permute-start(bf16[256,256]{1,0:T(8,128)(2,1)S(1)} %get-tuple-element.73), channel_id=1, source_target_pairs={{5,7},{21,23},{37,39},{53,55},{69,71},{85,87},{101,103},{117,119},... | collective-permute-start | bytes 393224 | tf_op jit(solution)/shard_map/ppermute | solution.py:319
  14.2 0.2 again_lead.1
  14.4 0.7 %collective-permute-start.9 = (bf16[256,256]{1,0:T(8,128)(2,1)S(1)}, bf16[256,256]{1,0:T(8,128)(2,1)S(1)}, u32[]{:S(2)}, u32[]{:S(2)}) collective-permute-start(bf16[256,256]{1,0:T(8,128)(2,1)S(1)} %get-tuple-element.78), channel_id=1, source_target_pairs={{5,7},{21,23},{37,39},{53,55},{69,71},{85,87},{101,103},{117,119},... | collective-permute-start | bytes 393224 | tf_op jit(solution)/shard_map/ppermute | solution.py:319
  15.1 0.7 %collective-permute-start.11 = (bf16[256,256]{1,0:T(8,128)(2,1)S(1)}, bf16[256,256]{1,0:T(8,128)(2,1)S(1)}, u32[]{:S(2)}, u32[]{:S(2)}) collective-permute-start(bf16[256,256]{1,0:T(8,128)(2,1)S(1)} %get-tuple-element.77), channel_id=1, source_target_pairs={{7,9},{23,25},{39,41},{55,57},{71,73},{87,89},{103,105},{119,121},... | collective-permute-start | bytes 393224 | tf_op jit(solution)/shard_map/ppermute | solution.py:319
  15.8 0.7 %collective-permute-start.10 = (bf16[256,256]{1,0:T(8,128)(2,1)S(1)}, bf16[256,256]{1,0:T(8,128)(2,1)S(1)}, u32[]{:S(2)}, u32[]{:S(2)}) collective-permute-start(bf16[256,256]{1,0:T(8,128)(2,1)S(1)} %get-tuple-element.73), channel_id=1, source_target_pairs={{9,11},{25,27},{41,43},{57,59},{73,75},{89,91},{105,107},{121,123}... | collective-permute-start | bytes 393224 | tf_op jit(solution)/shard_map/ppermute | solution.py:319
  16.5 0.7 %collective-permute-start.8 = (bf16[256,256]{1,0:T(8,128)(2,1)S(1)}, bf16[256,256]{1,0:T(8,128)(2,1)S(1)}, u32[]{:S(2)}, u32[]{:S(2)}) collective-permute-start(bf16[256,256]{1,0:T(8,128)(2,1)S(1)} %get-tuple-element.77), channel_id=1, source_target_pairs={{7,11},{23,27},{39,43},{55,59},{71,75},{87,91},{103,107},{119,123}... | collective-permute-start | bytes 393224 | tf_op jit(solution)/shard_map/ppermute | solution.py:319
  17.1 0.0 collective-permute-done.9.got.early5.got5
  17.2 0.7 %collective-permute-start.12 = (bf16[256,256]{1,0:T(8,128)(2,1)S(1)}, bf16[256,256]{1,0:T(8,128)(2,1)S(1)}, u32[]{:S(2)}, u32[]{:S(2)}) collective-permute-start(bf16[256,256]{1,0:T(8,128)(2,1)S(1)} %get-tuple-element.80.other.mine), channel_id=1, source_target_pairs={{7,11},{23,27},{39,43},{55,59},{71,75},{87,91},{103,107},{119,123}... | collective-permute-start | bytes 393224 | tf_op jit(solution)/shard_map/ppermute | solution.py:319
  17.9 0.0 collective-permute-done.11.refs_0_
  17.9 0.0 collective-permute-done.10.got
  17.9 0.7 %collective-permute-start.13 = (bf16[256,256]{1,0:T(8,128)(2,1)S(1)}, bf16[256,256]{1,0:T(8,128)(2,1)S(1)}, u32[]{:S(2)}, u32[]{:S(2)}) collective-permute-start(bf16[256,256]{1,0:T(8,128)(2,1)S(1)} %get-tuple-element.90), channel_id=1, source_target_pairs={{9,11},{11,13},{25,27},{27,29},{41,43},{43,45},{57,59},{59,61},{73... | collective-permute-start | bytes 393224 | tf_op jit(solution)/shard_map/ppermute | solution.py:319
  18.6 0.7 %collective-permute-start.14 = (bf16[256,256]{1,0:T(8,128)(2,1)S(1)}, bf16[256,256]{1,0:T(8,128)(2,1)S(1)}, u32[]{:S(2)}, u32[]{:S(2)}) collective-permute-start(bf16[256,256]{1,0:T(8,128)(2,1)S(1)} %get-tuple-element.83.other), channel_id=1, source_target_pairs={{7,9},{11,15},{23,25},{27,31},{39,41},{43,47},{55,57},{59,63},{71,... | collective-permute-start | bytes 393224 | tf_op jit(solution)/shard_map/ppermute | solution.py:319
  19.4 0.7 %collective-permute-start.15 = (bf16[256,256]{1,0:T(8,128)(2,1)S(1)}, bf16[256,256]{1,0:T(8,128)(2,1)S(1)}, u32[]{:S(2)}, u32[]{:S(2)}) collective-permute-start(bf16[256,256]{1,0:T(8,128)(2,1)S(1)} %get-tuple-element.92.mine), channel_id=1, source_target_pairs={{11,13},{13,15},{27,29},{29,31},{43,45},{45,47},{59,61},{61,63},{7... | collective-permute-start | bytes 393224 | tf_op jit(solution)/shard_map/ppermute | solution.py:319
  20.1 0.7 %collective-permute-start.18 = (bf16[256,256]{1,0:T(8,128)(2,1)S(1)}, bf16[256,256]{1,0:T(8,128)(2,1)S(1)}, u32[]{:S(2)}, u32[]{:S(2)}) collective-permute-start(bf16[256,256]{1,0:T(8,128)(2,1)S(1)} %get-tuple-element.92.mine), channel_id=1, source_target_pairs={{11,15},{3,2},{5,4},{7,8},{27,31},{19,18},{21,20},{23,24},{43,47},... | collective-permute-start | bytes 393224 | tf_op jit(solution)/shard_map/ppermute | solution.py:319
  20.8 0.7 %collective-permute-start.17 = (bf16[256,256]{1,0:T(8,128)(2,1)S(1)}, bf16[256,256]{1,0:T(8,128)(2,1)S(1)}, u32[]{:S(2)}, u32[]{:S(2)}) collective-permute-start(bf16[256,256]{1,0:T(8,128)(2,1)S(1)} %get-tuple-element.94), channel_id=1, source_target_pairs={{13,15},{9,11},{29,31},{25,27},{45,47},{41,43},{61,63},{57,59},{77... | collective-permute-start | bytes 393224 | tf_op jit(solution)/shard_map/ppermute | solution.py:319
  21.5 1.3 %collective-permute-start.16 = (bf16[256,256]{1,0:T(8,128)(2,1)S(1)}, bf16[256,256]{1,0:T(8,128)(2,1)S(1)}, u32[]{:S(2)}, u32[]{:S(2)}) collective-permute-start(bf16[256,256]{1,0:T(8,128)(2,1)S(1)} %get-tuple-element.94), channel_id=1, source_target_pairs={{13,14},{9,10},{11,12},{7,6},{29,30},{25,26},{27,28},{23,22},{45,4... | collective-permute-start | bytes 393224 | tf_op jit(solution)/shard_map/ppermute | solution.py:319
  22.8 20.3 %collective-permute-done.16.got8b = bf16[256,256]{1,0:T(8,128)(2,1)S(1)} collective-permute-done((bf16[256,256]{1,0:T(8,128)(2,1)S(1)}, bf16[256,256]{1,0:T(8,128)(2,1)S(1)}, u32[]{:S(2)}, u32[]{:S(2)}) %collective-permute-start.16) | collective-permute-done | bytes 131104 | tf_op jit(solution)/shard_map/ppermute | solution.py:319
  43.2 2.3 %last_sweep.1 = f32[4,256,256]{2,1,0:T(8,128)} custom-call(f32[256,256]{1,0:T(8,128)S(1)} %get-tuple-element.62.start, bf16[256,256]{1,0:T(8,128)(2,1)S(1)} %collective-permute-done.16.got8b, bf16[256,256]{1,0:T(8,128)(2,1)S(1)} %collective-permute-done.17.got8, bf16[256,256]{1,0:T(8,128)(2,1)S(1)} %collective-permute-done.5.got.early3.got3, ...), custom_call_target="tpu_custom_call" | custom-call | flops 1207959552 | bytes 1048576 | tf_op jit(solution)/shard_map/last_sweep/pallas_call | solution.py:58
  (27 shorter events, 0.3 us)
Async XLA Ops:
  0.1 7.9 %collective-permute-start = (bf16[256,256]{1,0:T(8,128)(2,1)S(1)}, bf16[256,256]{1,0:T(8,128)(2,1)S(1)}, u32[]{:S(2)}, u32[]{:S(2)}) collective-permute-start(bf16[256,256]{1,0:T(8,128)(2,1)S(1)} %get-tuple-element.51.refs_6_), channel_id=1, source_target_pairs={{1,2},{3,4},{5,6},{7,8},{9,10},{11,12},{13,14},{17,18},{19,20},{21... | collective-permute-start | bytes 393224 | tf_op jit(solution)/shard_map/ppermute | solution.py:319
  5.0 3.0 %collective-permute-start.1 = (bf16[256,256]{1,0:T(8,128)(2,1)S(1)}, bf16[256,256]{1,0:T(8,128)(2,1)S(1)}, u32[]{:S(2)}, u32[]{:S(2)}) collective-permute-start(bf16[256,256]{1,0:T(8,128)(2,1)S(1)} %get-tuple-element.60), channel_id=1, source_target_pairs={{0,1},{2,3},{4,5},{6,7},{8,9},{10,11},{12,13},{14,15},{16,17},{18,... | collective-permute-start | bytes 393224 | tf_op jit(solution)/shard_map/ppermute | solution.py:319
  6.3 6.3 %collective-permute-start.3 = (bf16[256,2304]{1,0:T(8,128)(2,1)S(1)}, bf16[256,2304]{1,0:T(8,128)(2,1)S(1)}, u32[]{:S(2)}, u32[]{:S(2)}) collective-permute-start(bf16[256,2304]{1,0:T(8,128)(2,1)S(1)} %get-tuple-element.57.own_w), channel_id=1, source_target_pairs={{0,1},{2,3},{4,5},{6,7},{8,9},{10,11},{12,13},{14,15},{16,17},{18,... | collective-permute-start | bytes 3538952 | tf_op jit(solution)/shard_map/ppermute | solution.py:319
  8.0 4.6 %collective-permute-start.5 = (bf16[256,256]{1,0:T(8,128)(2,1)S(1)}, bf16[256,256]{1,0:T(8,128)(2,1)S(1)}, u32[]{:S(2)}, u32[]{:S(2)}) collective-permute-start(bf16[256,256]{1,0:T(8,128)(2,1)S(1)} %get-tuple-element.68), channel_id=1, source_target_pairs={{1,3},{17,19},{33,35},{49,51},{65,67},{81,83},{97,99},{113,115},{1... | collective-permute-start | bytes 393224 | tf_op jit(solution)/shard_map/ppermute | solution.py:319
  10.6 2.3 %collective-permute-start.2 = (bf16[256,256]{1,0:T(8,128)(2,1)S(1)}, bf16[256,256]{1,0:T(8,128)(2,1)S(1)}, u32[]{:S(2)}, u32[]{:S(2)}) collective-permute-start(bf16[256,256]{1,0:T(8,128)(2,1)S(1)} %get-tuple-element.63), channel_id=1, source_target_pairs={{0,1},{2,3},{4,5},{6,7},{8,9},{10,11},{12,13},{14,15},{16,17},{18,... | collective-permute-start | bytes 393224 | tf_op jit(solution)/shard_map/ppermute | solution.py:319
  11.9 1.6 %collective-permute-start.4 = (f32[256,256]{1,0:T(8,128)S(1)}, f32[256,256]{1,0:T(8,128)S(1)}, u32[]{:S(2)}, u32[]{:S(2)}) collective-permute-start(f32[256,256]{1,0:T(8,128)S(1)} %get-tuple-element.67), channel_id=1, source_target_pairs={{4,5},{8,9},{20,21},{24,25},{36,37},{40,41},{52,53},{56,57},{68,69... | collective-permute-start | bytes 786440 | tf_op jit(solution)/shard_map/ppermute | solution.py:319
  12.8 1.4 %collective-permute-start.7 = (bf16[256,256]{1,0:T(8,128)(2,1)S(1)}, bf16[256,256]{1,0:T(8,128)(2,1)S(1)}, u32[]{:S(2)}, u32[]{:S(2)}) collective-permute-start(bf16[256,256]{1,0:T(8,128)(2,1)S(1)} %get-tuple-element.74), channel_id=1, source_target_pairs={{3,5},{19,21},{35,37},{51,53},{67,69},{83,85},{99,101},{115,117},{... | collective-permute-start | bytes 393224 | tf_op jit(solution)/shard_map/ppermute | solution.py:319
  13.5 1.6 %collective-permute-start.6 = (bf16[256,256]{1,0:T(8,128)(2,1)S(1)}, bf16[256,256]{1,0:T(8,128)(2,1)S(1)}, u32[]{:S(2)}, u32[]{:S(2)}) collective-permute-start(bf16[256,256]{1,0:T(8,128)(2,1)S(1)} %get-tuple-element.73), channel_id=1, source_target_pairs={{5,7},{21,23},{37,39},{53,55},{69,71},{85,87},{101,103},{117,119},... | collective-permute-start | bytes 393224 | tf_op jit(solution)/shard_map/ppermute | solution.py:319
  14.4 2.7 %collective-permute-start.9 = (bf16[256,256]{1,0:T(8,128)(2,1)S(1)}, bf16[256,256]{1,0:T(8,128)(2,1)S(1)}, u32[]{:S(2)}, u32[]{:S(2)}) collective-permute-start(bf16[256,256]{1,0:T(8,128)(2,1)S(1)} %get-tuple-element.78), channel_id=1, source_target_pairs={{5,7},{21,23},{37,39},{53,55},{69,71},{85,87},{101,103},{117,119},... | collective-permute-start | bytes 393224 | tf_op jit(solution)/shard_map/ppermute | solution.py:319
  15.1 2.7 %collective-permute-start.11 = (bf16[256,256]{1,0:T(8,128)(2,1)S(1)}, bf16[256,256]{1,0:T(8,128)(2,1)S(1)}, u32[]{:S(2)}, u32[]{:S(2)}) collective-permute-start(bf16[256,256]{1,0:T(8,128)(2,1)S(1)} %get-tuple-element.77), channel_id=1, source_target_pairs={{7,9},{23,25},{39,41},{55,57},{71,73},{87,89},{103,105},{119,121},... | collective-permute-start | bytes 393224 | tf_op jit(solution)/shard_map/ppermute | solution.py:319
  15.8 2.1 %collective-permute-start.10 = (bf16[256,256]{1,0:T(8,128)(2,1)S(1)}, bf16[256,256]{1,0:T(8,128)(2,1)S(1)}, u32[]{:S(2)}, u32[]{:S(2)}) collective-permute-start(bf16[256,256]{1,0:T(8,128)(2,1)S(1)} %get-tuple-element.73), channel_id=1, source_target_pairs={{9,11},{25,27},{41,43},{57,59},{73,75},{89,91},{105,107},{121,123}... | collective-permute-start | bytes 393224 | tf_op jit(solution)/shard_map/ppermute | solution.py:319
  16.5 2.8 %collective-permute-start.8 = (bf16[256,256]{1,0:T(8,128)(2,1)S(1)}, bf16[256,256]{1,0:T(8,128)(2,1)S(1)}, u32[]{:S(2)}, u32[]{:S(2)}) collective-permute-start(bf16[256,256]{1,0:T(8,128)(2,1)S(1)} %get-tuple-element.77), channel_id=1, source_target_pairs={{7,11},{23,27},{39,43},{55,59},{71,75},{87,91},{103,107},{119,123}... | collective-permute-start | bytes 393224 | tf_op jit(solution)/shard_map/ppermute | solution.py:319
  17.2 2.2 %collective-permute-start.12 = (bf16[256,256]{1,0:T(8,128)(2,1)S(1)}, bf16[256,256]{1,0:T(8,128)(2,1)S(1)}, u32[]{:S(2)}, u32[]{:S(2)}) collective-permute-start(bf16[256,256]{1,0:T(8,128)(2,1)S(1)} %get-tuple-element.80.other.mine), channel_id=1, source_target_pairs={{7,11},{23,27},{39,43},{55,59},{71,75},{87,91},{103,107},{119,123}... | collective-permute-start | bytes 393224 | tf_op jit(solution)/shard_map/ppermute | solution.py:319
  17.9 1.4 %collective-permute-start.13 = (bf16[256,256]{1,0:T(8,128)(2,1)S(1)}, bf16[256,256]{1,0:T(8,128)(2,1)S(1)}, u32[]{:S(2)}, u32[]{:S(2)}) collective-permute-start(bf16[256,256]{1,0:T(8,128)(2,1)S(1)} %get-tuple-element.90), channel_id=1, source_target_pairs={{9,11},{11,13},{25,27},{27,29},{41,43},{43,45},{57,59},{59,61},{73... | collective-permute-start | bytes 393224 | tf_op jit(solution)/shard_map/ppermute | solution.py:319
  18.6 2.1 %collective-permute-start.14 = (bf16[256,256]{1,0:T(8,128)(2,1)S(1)}, bf16[256,256]{1,0:T(8,128)(2,1)S(1)}, u32[]{:S(2)}, u32[]{:S(2)}) collective-permute-start(bf16[256,256]{1,0:T(8,128)(2,1)S(1)} %get-tuple-element.83.other), channel_id=1, source_target_pairs={{7,9},{11,15},{23,25},{27,31},{39,41},{43,47},{55,57},{59,63},{71,... | collective-permute-start | bytes 393224 | tf_op jit(solution)/shard_map/ppermute | solution.py:319
  19.4 1.4 %collective-permute-start.15 = (bf16[256,256]{1,0:T(8,128)(2,1)S(1)}, bf16[256,256]{1,0:T(8,128)(2,1)S(1)}, u32[]{:S(2)}, u32[]{:S(2)}) collective-permute-start(bf16[256,256]{1,0:T(8,128)(2,1)S(1)} %get-tuple-element.92.mine), channel_id=1, source_target_pairs={{11,13},{13,15},{27,29},{29,31},{43,45},{45,47},{59,61},{61,63},{7... | collective-permute-start | bytes 393224 | tf_op jit(solution)/shard_map/ppermute | solution.py:319
  20.1 2.7 %collective-permute-start.18 = (bf16[256,256]{1,0:T(8,128)(2,1)S(1)}, bf16[256,256]{1,0:T(8,128)(2,1)S(1)}, u32[]{:S(2)}, u32[]{:S(2)}) collective-permute-start(bf16[256,256]{1,0:T(8,128)(2,1)S(1)} %get-tuple-element.92.mine), channel_id=1, source_target_pairs={{11,15},{3,2},{5,4},{7,8},{27,31},{19,18},{21,20},{23,24},{43,47},... | collective-permute-start | bytes 393224 | tf_op jit(solution)/shard_map/ppermute | solution.py:319
  20.8 2.0 %collective-permute-start.17 = (bf16[256,256]{1,0:T(8,128)(2,1)S(1)}, bf16[256,256]{1,0:T(8,128)(2,1)S(1)}, u32[]{:S(2)}, u32[]{:S(2)}) collective-permute-start(bf16[256,256]{1,0:T(8,128)(2,1)S(1)} %get-tuple-element.94), channel_id=1, source_target_pairs={{13,15},{9,11},{29,31},{25,27},{45,47},{41,43},{61,63},{57,59},{77... | collective-permute-start | bytes 393224 | tf_op jit(solution)/shard_map/ppermute | solution.py:319
  21.5 21.7 %collective-permute-start.16 = (bf16[256,256]{1,0:T(8,128)(2,1)S(1)}, bf16[256,256]{1,0:T(8,128)(2,1)S(1)}, u32[]{:S(2)}, u32[]{:S(2)}) collective-permute-start(bf16[256,256]{1,0:T(8,128)(2,1)S(1)} %get-tuple-element.94), channel_id=1, source_target_pairs={{13,14},{9,10},{11,12},{7,6},{29,30},{25,26},{27,28},{23,22},{45,4... | collective-permute-start | bytes 393224 | tf_op jit(solution)/shard_map/ppermute | solution.py:319
